TPU v7x, 32 devices: a whole 2x2x4 slice. The times are simulated.
32 devices in a mesh: fsdp: 32 (over z, y, x, core).
Axes of the slice: x: 2, y: 2, z: 4, core: 2. Of those that a mesh axis runs over, the one named last changes fastest.
Arguments:
- latents: bfloat16 [256, 256, 384], P('fsdp'), may hold values from -6 to 6
- condition: bfloat16 [256, 384], P('fsdp'), may hold values from -6 to 6
- attn_params: bfloat16 [1477632], P('fsdp'), as said below
- mlp_params: bfloat16 [1181952], P('fsdp'), as said below
- counts: int32 [32], P('fsdp'), may hold values from 1 to 8, as said below
- cotangent: bfloat16 [256, 256, 384], P('fsdp'), may hold values from -6 to 6
Outputs:
- output: bfloat16 [256, 256, 384], P('fsdp')
- grad_latents: float32 [256, 256, 384], P('fsdp')
- grad_condition: float32 [256, 384], P('fsdp')
- grad_attn: float32 [1477632], P('fsdp')
- grad_mlp: float32 [1181952], P('fsdp')
Inputs may be any that keep to these rules, and one draw needn't show every extreme that they name: Device i holds live latents in its first counts[i] slots; some device holds 8 and some device 1. `attn_params`: weights and biases in the layout of the steps. `mlp_params`: weights and biases in the layout of the steps.
All inputs are finite; a program needn't handle non-finite values.
Results may differ from a plain program's by a relative error of at most 0.009.
The roundings to bfloat16 on the way count: a program that leaves them out, or rounds other values in their place, can miss the bound.
Values may be sent and summed in bfloat16 or wider, within the bound.
No kernel may reach another device: no remote copies, remote signals or barrier semaphores. Data moves between devices by JAX's collectives and lax.ppermute only.
A program may use at most 128 MiB of HBM per device.

v0:
```python
import math

import jax
import jax.numpy as jnp
from jax import lax
from jax.sharding import PartitionSpec as P

D = 384
HEADS = 6
HEAD_DIM = 64
FF = 1536


EPSILON = 1e-06


def split_flat(flat, shapes):
    pieces = []
    start = 0
    for shape in shapes:
        count = math.prod(shape)
        pieces.append(flat[start : start + count].reshape(shape))
        start = start + count
    return pieces


def attention_shapes():
    return [(D, 6 * D), (D, 3 * D), (D, D), (6 * D,), (2 * D,)]


def feedforward_shapes():
    return [(D, FF), (FF, D), (FF,), (D,), (D,)]


def outer_sum(left, right):
    return lax.dot_general(
        left, right, (((0,), (0,)), ((), ())), preferred_element_type=jnp.float32
    )


def back_product(grad, weight):
    return lax.dot_general(
        grad, weight, (((1,), (1,)), ((), ())), preferred_element_type=jnp.float32
    )


def column_sum(values):
    return jnp.sum(values.astype(jnp.float32), axis=0)


def normalize(values):
    average = jnp.mean(values, -1, keepdims=True)
    centered = values - average
    rstd = lax.rsqrt(jnp.mean(centered * centered, -1, keepdims=True) + EPSILON)
    return (centered * rstd, rstd)


def normalize_back(grad, normed, rstd):
    first = jnp.mean(grad, -1, keepdims=True)
    second = jnp.mean(grad * normed, -1, keepdims=True)
    return rstd * (grad - first - normed * second)


def gelu_tanh(values):
    return jax.nn.gelu(values, approximate=True)


def attend(queries, keys_all, values):
    factor = HEAD_DIM ** (-0.5)
    outputs = []
    lse_list = []
    for head in range(HEADS):
        lower = head * HEAD_DIM
        upper = lower + HEAD_DIM
        scores = (
            jnp.einsum(
                "lqd,lkd->lqk",
                queries[..., lower:upper],
                keys_all[..., lower:upper],
                preferred_element_type=jnp.float32,
            )
            * factor
        )
        highest = jnp.max(scores, -1, keepdims=True)
        expo = jnp.exp(scores - highest)
        total = jnp.sum(expo, -1, keepdims=True)
        probs = (expo / total).astype(jnp.bfloat16)
        outputs.append(
            jnp.einsum(
                "lqk,lkd->lqd", probs, values[..., lower:upper], preferred_element_type=jnp.float32
            )
        )
        lse_list.append(highest + jnp.log(total))
    return (jnp.concatenate(outputs, -1), lse_list)


def attend_back(queries, keys_all, values, grad_mixed, lse_list):
    factor = HEAD_DIM ** (-0.5)
    grad_queries = []
    grad_keys = []
    grad_values = []
    for head in range(HEADS):
        lower = head * HEAD_DIM
        upper = lower + HEAD_DIM
        query_head = queries[..., lower:upper]
        key_head = keys_all[..., lower:upper]
        value_head = values[..., lower:upper]
        grad_head = grad_mixed[..., lower:upper]
        scores = (
            jnp.einsum("lqd,lkd->lqk", query_head, key_head, preferred_element_type=jnp.float32)
            * factor
        )
        probs = jnp.exp(scores - lse_list[head])
        probs_low = probs.astype(jnp.bfloat16)
        grad_values.append(
            jnp.einsum(
                "lqk,lqd->lkd", probs_low, grad_head, preferred_element_type=jnp.float32
            ).astype(jnp.bfloat16)
        )
        grad_probs = jnp.einsum(
            "lqd,lkd->lqk", grad_head, value_head, preferred_element_type=jnp.float32
        )
        grad_scores = probs * (grad_probs - jnp.sum(probs * grad_probs, -1, keepdims=True))
        grad_scores = grad_scores.astype(jnp.bfloat16)
        grad_queries.append(
            (
                jnp.einsum(
                    "lqk,lkd->lqd", grad_scores, key_head, preferred_element_type=jnp.float32
                )
                * factor
            ).astype(jnp.bfloat16)
        )
        grad_keys.append(
            (
                jnp.einsum(
                    "lqk,lqd->lkd", grad_scores, query_head, preferred_element_type=jnp.float32
                )
                * factor
            ).astype(jnp.bfloat16)
        )
    return (
        jnp.concatenate(grad_queries, -1),
        jnp.concatenate(grad_keys, -1),
        jnp.concatenate(grad_values, -1),
    )


def body(latents, condition, attn_params, mlp_params, counts, cotangent):
    latent_count = latents.shape[0]
    seq_len = latents.shape[1]
    row_count = latent_count * seq_len
    attn_full, mlp_full = (
        lax.all_gather(attn_params, "fsdp", axis=0, tiled=True),
        lax.all_gather(mlp_params, "fsdp", axis=0, tiled=True),
    )
    w_ada, w_qkv, w_proj, b_ada, b_qv = split_flat(attn_full, attention_shapes())
    w_fc1, w_fc2, b_fc1, b_fc2, b_proj = split_flat(mlp_full, feedforward_shapes())
    live_mask = (jnp.arange(latent_count) < counts[0]).astype(jnp.float32)[:, None, None]
    cond_float = condition.astype(jnp.float32)
    cond_act = jax.nn.silu(cond_float).astype(jnp.bfloat16)
    modulation = jnp.dot(cond_act, w_ada, preferred_element_type=jnp.float32) + b_ada.astype(
        jnp.float32
    )
    parts = [modulation[:, index * D : (index + 1) * D][:, None, :] for index in range(6)]
    shift_one, scale_one, gate_one, shift_two, scale_two, gate_two = parts
    inputs = latents.astype(jnp.float32)
    normed_one, rstd_one = normalize(inputs)
    mod_one = (
        (normed_one * (1.0 + scale_one) + shift_one).astype(jnp.bfloat16).reshape(row_count, D)
    )
    qkv = jnp.dot(mod_one, w_qkv, preferred_element_type=jnp.float32).reshape(
        latent_count, seq_len, 3 * D
    )
    queries = (qkv[..., :D] + b_qv[:D].astype(jnp.float32)).astype(jnp.bfloat16)
    keys_all = qkv[..., D : 2 * D].astype(jnp.bfloat16)
    values = (qkv[..., 2 * D :] + b_qv[D:].astype(jnp.float32)).astype(jnp.bfloat16)
    mixed, lse_list = attend(queries, keys_all, values)
    mixed_low = mixed.astype(jnp.bfloat16).reshape(row_count, D)
    branch_one = (
        jnp.dot(mixed_low, w_proj, preferred_element_type=jnp.float32) + b_proj.astype(jnp.float32)
    ).reshape(latent_count, seq_len, D)
    middle = inputs + gate_one * branch_one
    normed_two, rstd_two = normalize(middle)
    mod_two = (
        (normed_two * (1.0 + scale_two) + shift_two).astype(jnp.bfloat16).reshape(row_count, D)
    )
    hidden_pre = jnp.dot(mod_two, w_fc1, preferred_element_type=jnp.float32) + b_fc1.astype(
        jnp.float32
    )
    hidden_act = gelu_tanh(hidden_pre).astype(jnp.bfloat16)
    branch_two = (
        jnp.dot(hidden_act, w_fc2, preferred_element_type=jnp.float32) + b_fc2.astype(jnp.float32)
    ).reshape(latent_count, seq_len, D)
    result = middle + gate_two * branch_two
    output = (result * live_mask).astype(jnp.bfloat16)
    attn_back, mlp_back = (
        lax.all_gather(attn_params, "fsdp", axis=0, tiled=True),
        lax.all_gather(mlp_params, "fsdp", axis=0, tiled=True),
    )
    w_ada, w_qkv, w_proj, b_ada, b_qv = split_flat(attn_back, attention_shapes())
    w_fc1, w_fc2, b_fc1, b_fc2, b_proj = split_flat(mlp_back, feedforward_shapes())
    grad_out = cotangent.astype(jnp.float32) * live_mask
    grad_gate_two = jnp.sum(grad_out * branch_two, axis=1)
    grad_branch_two = (gate_two * grad_out).astype(jnp.bfloat16).reshape(row_count, D)
    grad_w_fc2 = outer_sum(hidden_act, grad_branch_two)
    grad_b_fc2 = column_sum(grad_branch_two)
    grad_hidden = back_product(grad_branch_two, w_fc2)
    unused_value, gelu_pull = jax.vjp(gelu_tanh, hidden_pre)
    grad_pre = gelu_pull(grad_hidden)[0].astype(jnp.bfloat16)
    grad_w_fc1 = outer_sum(mod_two, grad_pre)
    grad_b_fc1 = column_sum(grad_pre)
    grad_mod_two = back_product(grad_pre, w_fc1).reshape(latent_count, seq_len, D)
    grad_shift_two = jnp.sum(grad_mod_two, axis=1)
    grad_scale_two = jnp.sum(grad_mod_two * normed_two, axis=1)
    grad_middle = grad_out + normalize_back(grad_mod_two * (1.0 + scale_two), normed_two, rstd_two)
    grad_gate_one = jnp.sum(grad_middle * branch_one, axis=1)
    grad_branch_one = (gate_one * grad_middle).astype(jnp.bfloat16).reshape(row_count, D)
    grad_b_proj = column_sum(grad_branch_one)
    mlp_terms = jnp.concatenate(
        [grad_w_fc1.reshape(-1), grad_w_fc2.reshape(-1), grad_b_fc1, grad_b_fc2, grad_b_proj]
    )
    grad_w_proj = outer_sum(mixed_low, grad_branch_one)
    grad_mixed = (
        back_product(grad_branch_one, w_proj).astype(jnp.bfloat16).reshape(latent_count, seq_len, D)
    )
    grad_queries, grad_keys, grad_values = attend_back(
        queries, keys_all, values, grad_mixed, lse_list
    )
    grad_qkv = jnp.concatenate([grad_queries, grad_keys, grad_values], -1).reshape(row_count, 3 * D)
    grad_w_qkv = outer_sum(mod_one, grad_qkv)
    grad_b_qv = jnp.concatenate(
        [
            column_sum(grad_queries.reshape(row_count, D)),
            column_sum(grad_values.reshape(row_count, D)),
        ]
    )
    grad_mod_one = back_product(grad_qkv, w_qkv).reshape(latent_count, seq_len, D)
    grad_shift_one = jnp.sum(grad_mod_one, axis=1)
    grad_scale_one = jnp.sum(grad_mod_one * normed_one, axis=1)
    grad_latents = grad_middle + normalize_back(
        grad_mod_one * (1.0 + scale_one), normed_one, rstd_one
    )
    grad_modulation = jnp.concatenate(
        [
            grad_shift_one,
            grad_scale_one,
            grad_gate_one,
            grad_shift_two,
            grad_scale_two,
            grad_gate_two,
        ],
        -1,
    ).astype(jnp.bfloat16)
    grad_w_ada = outer_sum(cond_act, grad_modulation)
    grad_b_ada = column_sum(grad_modulation)
    grad_cond_act = back_product(grad_modulation, w_ada)
    unused_cond, silu_pull = jax.vjp(jax.nn.silu, cond_float)
    grad_condition = silu_pull(grad_cond_act)[0]
    attn_terms = jnp.concatenate(
        [
            grad_w_ada.reshape(-1),
            grad_w_qkv.reshape(-1),
            grad_w_proj.reshape(-1),
            grad_b_ada,
            grad_b_qv,
        ]
    )
    grad_attn, grad_mlp = (
        lax.psum_scatter(attn_terms, "fsdp", scatter_dimension=0, tiled=True),
        lax.psum_scatter(mlp_terms, "fsdp", scatter_dimension=0, tiled=True),
    )
    return (output, grad_latents, grad_condition, grad_attn, grad_mlp)


def solution(mesh):
    in_specs = (
        P("fsdp", None, None),
        P("fsdp", None),
        P("fsdp"),
        P("fsdp"),
        P("fsdp"),
        P("fsdp", None, None),
    )
    out_specs = (
        P("fsdp", None, None),
        P("fsdp", None, None),
        P("fsdp", None),
        P("fsdp"),
        P("fsdp"),
    )
    return jax.shard_map(body, mesh=mesh, in_specs=in_specs, out_specs=out_specs, check_vma=False)
```

profile of v0, /device:TPU:0, one launch (start us, length us, event | category | flops | bytes accessed | tf_op | source)
XLA Modules:
  0.0 588.6 jit_solution(9539772257712310425)
XLA Ops:
  7.2 1.5 broadcast.133
  8.8 2.4 dynamic-update-slice.1
  12.3 1.6 copy-done.13
  16.6 149.6 %all-reduce.11.cloned.1.call-done = (bf16[1477632]{0:T(1024)(128)(2,1)}, bf16[1181952]{0:T(1024)(128)(2,1)}) async-done(((bf16[1477632]{0:T(1024)(128)(2,1)}, bf16[1181952]{0:T(1024)(128)(2,1)}), (bf16[1477632]{0:T(1024)(128)(2,1)}, bf16[1181952]{0:T(1024)(128)(2,1)})) %all-reduce.11.cloned.1.call-update) | async-done | bytes 5319184
  166.9 3.0 fusion.156
  172.3 1.3 slice.228
  173.6 2.2 reshape.244
  175.7 2.2 reshape.229
  178.0 3.6 reshape.225
  181.6 3.3 reshape.243
  186.0 3.0 fusion.158
  189.0 2.2 fusion.21
  191.8 1.8 multiply_reduce_fusion.14
  193.6 1.9 multiply_reduce_fusion.15
  195.5 1.7 multiply_reduce_fusion.16
  197.2 1.9 multiply_reduce_fusion.17
  199.1 1.8 multiply_reduce_fusion.18
  200.9 1.6 slice.220
  218.0 1.7 convert_reduce_fusion.3
  221.0 9.9 %multiply_convert_fusion = (bf16[2048,1536]{1,0:T(8,128)(2,1)}, f32[2048,1536]{1,0:T(8,128)}) fusion(f32[1536]{0:T(1024)S(1)} %slice_convert_fusion.1, bf16[2048,384]{1,0:T(8,128)(2,1)S(1)} %bitcast.84, bf16[384,1536]{1,0:T(8,128)(2,1)S(1)} %copy-done.30), kind=kOutput, calls=%fused_computation.10 | convolution fusion | flops 2447376384 | bytes 21633024 | tf_op jit(solution)/shard_map/dot_general | solution.py:187
  230.9 16.3 %convert_reduce_fusion = (f32[1536]{0:T(1024)}, bf16[2048,1536]{1,0:T(8,128)(2,1)}) fusion(f32[2048,1536]{1,0:T(8,128)} %get-tuple-element.82, f32[1536]{0:T(1024)S(1)} %slice_convert_fusion.1, bf16[2048,384]{1,0:T(8,128)(2,1)} %bitcast.87, bf16[1536,384]{1,0:T(8,128)(2,1)} %slice.220), kind=kOutput, calls=%fused_computation.9 | convolution fusion | flops 2488269312 | bytes 21639168 | tf_op jit(solution)/shard_map/dot_general | solution.py:42
  247.2 7.0 %fusion.159 = f32[384,1536]{1,0:T(8,128)} fusion(bf16[2048,384]{1,0:T(8,128)(2,1)S(1)} %bitcast.85, bf16[2048,1536]{1,0:T(8,128)(2,1)} %get-tuple-element.109), kind=kOutput, calls=%fused_computation.323 | convolution fusion | flops 2415919104 | bytes 10223616 | tf_op jit(solution)/shard_map/dot_general | solution.py:36
  254.2 4.9 fusion.160
  259.1 5.1 convolution_add_fusion.2
  264.3 5.3 multiply_reduce_fusion.1
  269.6 6.3 %convert_reduce_fusion.2 = (f32[384]{0:T(512)}, bf16[8,256,384]{2,1,0:T(8,128)(2,1)S(1)}, f32[8,256,384]{2,1,0:T(8,128)S(1)}, bf16[8,256,384]{2,1,0:T(8,128)(2,1)}, bf16[8,384]{1,0:T(8,128)(2,1)S(1)}) fusion(f32[8,384]{1,0:T(8,128)S(1)} %get-tuple-element.65, f32[8,256]{1,0:T(8,128)S(1)} %broadcast_multiply_fusion.2, ...), kind=kLoop, calls=%fused_computation.33 | loop fusion | flops 15725184 | bytes 17378848 | tf_op jit(solution)/shard_map/reduce_sum | solution.py:48
  277.0 1.8 multiply_reduce_fusion.12
  282.3 2.1 multiply_convert_fusion.9
  287.9 1.3 constant_dynamic-update-slice_fusion.34
  290.3 1.3 constant_dynamic-update-slice_fusion.32
  291.6 1.2 copy-done.26
  294.0 1.4 constant_dynamic-update-slice_fusion.30
  296.5 1.4 fusion.51
  299.0 1.3 fusion.49
  301.5 1.7 fusion.47
  303.2 1.3 constant_dynamic-update-slice_fusion.41
  304.5 1.4 constant_dynamic-update-slice_fusion.40
  305.9 1.2 constant_dynamic-update-slice_fusion.39
  307.1 1.4 constant_dynamic-update-slice_fusion.38
  308.5 1.2 constant_dynamic-update-slice_fusion.37
  309.7 1.4 constant_dynamic-update-slice_fusion.36
  311.1 7.1 %convolution_bitcast_fusion = f32[384,1152]{1,0:T(8,128)} fusion(bf16[8,256,1152]{1,2,0:T(8,128)(2,1)} %get-tuple-element.37, bf16[8,256,384]{2,1,0:T(8,128)(2,1)S(1)} %copy-done.6, f32[8,384]{1,0:T(8,128)S(1)} %get-tuple-element.63, f32[8,384]{1,0:T(8,128)S(1)} %get-tuple-element.64, f32[8,256]{1,0:T(8,128)S(1)} %add_rsqrt_fusion.1, ...), kind=kOutput, calls=%fused_computation.49 | convolution fusion | flops 1816657920 | bytes 8101888 | tf_op jit(solution)/shard_map/dot_general | solution.py:36
  318.1 4.7 fusion.19
  322.9 3.1 multiply_reduce_fusion.2
  327.3 3.2 reshape.237
  330.5 3.4 reshape.238
  333.9 3.7 convolution_bitcast_fusion.1
  337.5 1.9 reshape.236
  339.5 3.5 constant_dynamic-update-slice_fusion.43
  344.1 2.5 reshape.235
  346.6 2.0 reshape.234
  348.7 4.1 constant_dynamic-update-slice_fusion.42
  352.8 1.6 constant_dynamic-update-slice_fusion.52
  354.4 1.4 constant_dynamic-update-slice_fusion.51
  355.8 1.3 constant_dynamic-update-slice_fusion.50
  357.1 1.3 constant_dynamic-update-slice_fusion.49
  358.4 1.3 constant_dynamic-update-slice_fusion.48
  360.6 1.3 constant_dynamic-update-slice_fusion.46
  361.9 1.3 constant_dynamic-update-slice_fusion.45
  363.1 1.3 constant_dynamic-update-slice_fusion.44
  364.4 1.4 copy-done.9
  367.1 211.1 %all-reduce.9.cloned.1.call-done = (f32[1477632]{0:T(1024)}, f32[1181952]{0:T(1024)}) async-done(((f32[1477632]{0:T(1024)}, f32[1181952]{0:T(1024)}), (f32[1477632]{0:T(1024)}, f32[1181952]{0:T(1024)})) %all-reduce.9.cloned.1.call-update) | async-done | bytes 10638352
  578.1 1.7 dynamic-slice
  579.9 1.7 dynamic-slice.1
  (186 shorter events, 42.8 us)
Async XLA Ops:
  7.2 1.6 copy-start.35
  7.2 159.0 %all-reduce.11.cloned.1.call-start = ((), (), s32[]{:S(2)}) async-start(), calls=%async_computation.1 | async-start | bytes 10641408
  8.8 2.6 copy-start.34
  12.3 1.6 copy-start.13
  13.9 1.4 copy-start.5
  13.9 564.2 %all-reduce.9.cloned.1.call-start = ((), (), s32[]{:S(2)}) async-start(), calls=%async_computation | async-start | bytes 21282816
  166.8 3.0 copy-start.22
  178.0 6.9 %copy-start.36 = (bf16[8,384]{1,0:T(8,128)(2,1)S(1)}, bf16[8,384]{1,0:T(8,128)(2,1)}, u32[]{:S(2)}) copy-start(bf16[8,384]{1,0:T(8,128)(2,1)} %param.7) | copy-start | bytes 18436
  181.5 7.5 %copy-start.8 = (bf16[384,2304]{1,0:T(8,128)(2,1)}, bf16[384,2304]{1,0:T(8,128)(2,1)S(1)}, u32[]{:S(2)}) copy-start(bf16[384,2304]{1,0:T(8,128)(2,1)S(1)} %reshape.225) | copy-start | bytes 5308420
  184.9 1.2 copy-start.20
  189.0 10.1 %copy-start.7 = (bf16[8,256,1152]{2,1,0:T(8,128)(2,1)}, bf16[8,256,1152]{2,1,0:T(8,128)(2,1)S(1)}, u32[]{:S(2)}) copy-start(bf16[8,256,1152]{2,1,0:T(8,128)(2,1)S(1)} %get-tuple-element.66) | copy-start | bytes 14155780
  191.2 7.9 %copy-start.11 = (bf16[8,256,384]{2,1,0:T(8,128)(2,1)}, bf16[8,256,384]{2,1,0:T(8,128)(2,1)S(1)}, u32[]{:S(2)}) copy-start(bf16[8,256,384]{2,1,0:T(8,128)(2,1)S(1)} %get-tuple-element.25) | copy-start | bytes 4718596
  199.1 1.8 copy-start.19
  203.6 1.6 copy-start
  203.6 2.2 copy-start.1
  205.2 1.7 copy-start.2
  205.8 1.7 copy-start.3
  207.0 1.7 copy-start.4
  207.5 1.6 copy-start.10
  213.3 1.2 copy-start.43
  214.7 1.4 copy-start.6
  216.6 1.4 copy-start.16
  219.7 1.3 copy-start.30
  247.2 7.0 %copy-start.28 = (bf16[8,256,384]{2,1,0:T(8,128)(2,1)S(1)}, bf16[8,256,384]{2,1,0:T(8,128)(2,1)}, u32[]{:S(2)}) copy-start(bf16[8,256,384]{2,1,0:T(8,128)(2,1)} %get-tuple-element.21) | copy-start | bytes 4718596
  247.2 7.0 %copy-start.44 = (bf16[2048,1536]{1,0:T(8,128)(2,1)S(1)}, bf16[2048,1536]{1,0:T(8,128)(2,1)}, u32[]{:S(2)}) copy-start(bf16[2048,1536]{1,0:T(8,128)(2,1)} %get-tuple-element.81) | copy-start | bytes 18874372
  254.2 4.9 copy-start.31
  254.2 10.1 %slice-start.2 = ((s8[6291456]{0:T(1024)(128)(4,1)}), s8[4194304]{0:T(1024)(128)(4,1)S(1)}, s32[]{:S(2)}) async-start(s8[6291456]{0:T(1024)(128)(4,1)} %bitcast.81), calls=%async_computation.4 | async-start | bytes 8388608
  259.1 5.1 slice-start.3
  259.1 5.1 copy-start.29
  264.3 5.3 copy-start.17
  275.9 3.0 copy-start.18
  281.0 3.5 slice-start
  281.6 2.9 slice-start.1
  291.6 1.2 copy-start.26
  292.8 2.6 copy-start.12
  311.1 7.1 %copy-start.24 = (bf16[8,256,384]{1,2,0:T(8,128)(2,1)}, bf16[8,256,384]{1,2,0:T(8,128)(2,1)S(1)}, u32[]{:S(2)}) copy-start(bf16[8,256,384]{1,2,0:T(8,128)(2,1)S(1)} %get-tuple-element.36) | copy-start | bytes 4718596
  311.1 7.1 %copy-start.21 = (bf16[384,1152,1]{1,0,2:T(8,128)(2,1)S(1)}, bf16[384,1152,1]{1,0,2:T(8,128)(2,1)}, u32[]{:S(2)}) copy-start(bf16[384,1152,1]{1,0,2:T(8,128)(2,1)} %reshape.243) | copy-start | bytes 2654212
  311.1 7.1 %copy-start.42 = (bf16[8,256,1152]{1,2,0:T(8,128)(2,1)S(1)}, bf16[8,256,1152]{1,2,0:T(8,128)(2,1)}, u32[]{:S(2)}) copy-start(bf16[8,256,1152]{1,2,0:T(8,128)(2,1)} %get-tuple-element.37) | copy-start | bytes 14155780
  322.9 3.8 copy-start.37
  326.0 0.6 copy-start.32
  339.5 3.5 copy-start.27
  339.5 3.8 copy-start.25
  348.7 4.1 copy-start.14
  352.8 1.6 copy-start.40
  352.8 4.2 copy-start.41
  352.8 5.5 copy-start.15
  354.4 5.3 copy-start.23
  358.3 2.2 copy-start.38
  358.3 4.8 copy-start.39
  364.4 1.5 copy-start.9
  364.4 1.5 copy-start.33
Sparse Core Ops, SparseCore 0:
  14.4 151.7 all-reduce.10
  364.6 213.5 all-reduce.8
where the time goes:
time: 599 us; the launch traced here: 589 us
  waiting for transfers between devices  361 us (60%)
  matrix products  113 us (19%)
  local copies, waits for them, and re-layouts  72.5 us (12%)
  other arithmetic  26.4 us (4%)
  between operations  15.6 us (3%)
    unnamed x4, waiting for transfers between devices  361 us
    unnamed x123, local copies, waits for them, and re-layouts  36.8 us
    dot_general x5, matrix products, back_product(): lax.dot_general(grad, weight, (((1,), (1,)), ((), ())), preferred_element...  28.5 us
    dot_general x5, matrix products, outer_sum(): lax.dot_general(left, right, (((0,), (0,)), ((), ())), preferred_element_...  23.4 us
  transfers between devices with their start and end apart: 2, of which 2 were waited for; matrix products, arithmetic and copies ran while one was open for 0% of the time, Pallas kernels for 0%

commit v1 on v0

v1 whole, which is shorter than its diff:
```python
import jax
import jax.numpy as jnp
from jax import lax
from jax.experimental import pallas as pl
from jax.experimental.pallas import tpu as pltpu
from jax.sharding import PartitionSpec as P

D = 384
HEADS = 6
HEAD_DIM = 64
FF = 1536
EPSILON = 1e-06
AXIS = "fsdp"
LANES = 128
TILES = D // LANES
GROUP = 8 * D
FACTOR = HEAD_DIM ** (-0.5)
GELU_A = 0.7978845608028654
GELU_B = 0.044715

ADA_AT = 0
QKV_AT = 6 * D
PROJ_AT = 9 * D
B_ADA_AT = 10 * D
B_QV_AT = 10 * D + 6
ATTN_ROWS = 10 * D + 8
FC1_AT = 0
FC2_AT = FF
B_FC1_AT = 2 * FF
B_FC2_AT = 2 * FF + 4
B_PROJ_AT = 2 * FF + 5
MLP_ROWS = 2 * FF + 6

F32 = jnp.float32
BF16 = jnp.bfloat16


def round_up(value, unit):
    return -(-value // unit) * unit


def piece_rows(share, count):
    lead = max((share * index) % GROUP for index in range(count))
    return round_up(-(-(share + lead) // D), 16)


def mm(left, right):
    return jnp.dot(left, right, preferred_element_type=F32)


def mm_nt(left, right):
    return lax.dot_general(left, right, (((1,), (1,)), ((), ())), preferred_element_type=F32)


def mm_tn(left, right):
    return lax.dot_general(left, right, (((0,), (0,)), ((), ())), preferred_element_type=F32)


def col_sum(values):
    return jnp.sum(values, axis=0, keepdims=True)


def row_mean(values):
    return jnp.mean(values, axis=-1, keepdims=True)


def normalize(values):
    centered = values - row_mean(values)
    rstd = lax.rsqrt(row_mean(centered * centered) + EPSILON)
    return centered * rstd, rstd


def normalize_back(grad, normed, rstd):
    return rstd * (grad - row_mean(grad) - normed * row_mean(grad * normed))


def head_masks():
    lane = lax.broadcasted_iota(jnp.int32, (1, LANES), 1) // HEAD_DIM
    return [(lane == head).astype(F32).astype(BF16) for head in range(2)]


def assemble(scal_ref, base, piece_refs, rows_ref):
    rows_ref[...] = jnp.zeros_like(rows_ref)
    at = base
    for ref in piece_refs:
        slots, height = ref.shape[0], ref.shape[1]

        def one(slot, carry, ref=ref, at=at, height=height):
            start = pl.multiple_of(scal_ref[at + slot] * 8, 8)
            for tile in range(TILES):
                lanes = slice(tile * LANES, (tile + 1) * LANES)
                rows_ref[tile, pl.ds(start, height), :] += ref[slot, :, lanes].astype(F32)
            return carry

        lax.fori_loop(0, slots, one, 0)
        at += slots


def emit(scal_ref, base, out_refs, rows_ref):
    at = base
    for ref in out_refs:
        slots, height = ref.shape[0], ref.shape[1]

        def one(slot, carry, ref=ref, at=at, height=height):
            start = pl.multiple_of(scal_ref[at + slot] * 8, 8)
            for tile in range(TILES):
                lanes = slice(tile * LANES, (tile + 1) * LANES)
                ref[slot, :, lanes] = rows_ref[tile, pl.ds(start, height), :].astype(ref.dtype)
            return carry

        lax.fori_loop(0, slots, one, 0)
        at += slots


def lanes_of(tile, offset=0):
    return slice(offset + tile * LANES, offset + (tile + 1) * LANES)


def forward_kernel(n_pieces, scal_ref, cond_ref, x_ref, *refs):
    pieces = refs[:n_pieces]
    mod_ref, ada_ref, qkv_w_ref, proj_ref, bias_ref, qkv_ref, probs_ref, mixed_ref, branch_ref = refs[
        n_pieces : n_pieces + 9
    ]
    rows_ref = refs[n_pieces + 9]
    step = pl.program_id(0)

    @pl.when(step == 0)
    def _():
        assemble(scal_ref, 1, pieces, rows_ref)
        for block in range(6):
            for tile in range(TILES):
                ada_ref[block, :, lanes_of(tile)] = rows_ref[
                    tile, pl.ds(ADA_AT + block, D, stride=6), :
                ].astype(BF16)
        for block in range(3):
            for tile in range(TILES):
                qkv_w_ref[:, lanes_of(tile, block * D)] = rows_ref[
                    tile, pl.ds(QKV_AT + block, D, stride=3), :
                ].astype(BF16)
        for tile in range(TILES):
            proj_ref[:, lanes_of(tile)] = rows_ref[tile, pl.ds(PROJ_AT, D), :].astype(BF16)
            bias_ref[:, lanes_of(tile)] = rows_ref[tile, pl.ds(B_ADA_AT, 8), :]
        act = jax.nn.silu(cond_ref[...].astype(F32)).astype(BF16)
        for block in range(6):
            mod_ref[block] = mm(act, ada_ref[block]) + bias_ref[pl.ds(block, 1), :]

    @pl.when(step < scal_ref[0])
    def _():
        masks = head_masks()
        values = x_ref[0].astype(F32)
        normed, _ = normalize(values)
        shift = mod_ref[0, pl.ds(step, 1), :]
        scale = mod_ref[1, pl.ds(step, 1), :]
        modulated = (normed * (1.0 + scale) + shift).astype(BF16)
        qkv = mm(modulated, qkv_w_ref[...])
        queries = (qkv[:, :D] + bias_ref[6:7, :]).astype(BF16)
        keys_all = qkv[:, D : 2 * D].astype(BF16)
        values_all = (qkv[:, 2 * D :] + bias_ref[7:8, :]).astype(BF16)
        qkv_ref[0, :, :D] = queries
        qkv_ref[0, :, D : 2 * D] = keys_all
        qkv_ref[0, :, 2 * D :] = values_all
        values_t = values_all.T
        for pair in range(HEADS // 2):
            lanes = lanes_of(pair)
            query, key = queries[:, lanes], keys_all[:, lanes]
            for half in range(2):
                head = 2 * pair + half
                scores = mm_nt(key, query * masks[half]) * FACTOR
                expo = jnp.exp(scores - jnp.max(scores, axis=0, keepdims=True))
                probs = expo * (1.0 / col_sum(expo))
                probs_ref[0, head] = probs
                rows = slice(head * HEAD_DIM, (head + 1) * HEAD_DIM)
                mixed_ref[0, rows, :] = mm(values_t[rows, :], probs.astype(BF16)).astype(BF16)
        branch_ref[0] = mm_tn(mixed_ref[0], proj_ref[...])


def mlp_kernel(n_pieces, n_out, scal_ref, mod_ref, proj_ref, x_ref, branch_ref, mixed_ref, cot_ref, *refs):
    pieces = refs[:n_pieces]
    outs = refs[n_pieces : n_pieces + 5 + n_out]
    out_ref, dx_ref, dmixed_ref, dmod_ref, dproj_ref = outs[:5]
    send_refs = outs[5:]
    rows_ref, fc1_ref, fc2_ref, bias_ref, act_ref, slope_ref, dfc1_ref, dfc2_ref, dbias_ref = refs[
        n_pieces + 5 + n_out :
    ]
    step = pl.program_id(0)
    last = pl.num_programs(0) - 1

    @pl.when(step == 0)
    def _():
        assemble(scal_ref, 1, pieces, rows_ref)
        for block in range(4):
            for tile in range(TILES):
                fc1_ref[:, lanes_of(tile, block * D)] = rows_ref[
                    tile, pl.ds(FC1_AT + block, D, stride=4), :
                ].astype(BF16)
                bias_ref[0:1, lanes_of(tile, block * D)] = rows_ref[tile, pl.ds(B_FC1_AT + block, 1), :]
        for tile in range(TILES):
            fc2_ref[:, lanes_of(tile)] = rows_ref[tile, pl.ds(FC2_AT, FF), :].astype(BF16)
            bias_ref[1:2, lanes_of(tile)] = rows_ref[tile, pl.ds(B_FC2_AT, 1), :]
            bias_ref[2:3, lanes_of(tile)] = rows_ref[tile, pl.ds(B_PROJ_AT, 1), :]
        dfc1_ref[...] = jnp.zeros_like(dfc1_ref)
        dfc2_ref[...] = jnp.zeros_like(dfc2_ref)
        dbias_ref[...] = jnp.zeros_like(dbias_ref)
        dproj_ref[...] = jnp.zeros_like(dproj_ref)
        dmod_ref[...] = jnp.zeros_like(dmod_ref)

    @pl.when(step < scal_ref[0])
    def _():
        row = pl.ds(step, 1)
        gate_one, shift, scale, gate_two = [mod_ref[2 + part, row, :] for part in range(4)]
        branch_one = branch_ref[0] + bias_ref[2:3, :D]
        middle = x_ref[0].astype(F32) + gate_one * branch_one
        normed, rstd = normalize(middle)
        modulated = (normed * (1.0 + scale) + shift).astype(BF16)
        chunk = 512
        branch_two = jnp.zeros_like(middle)
        for start in range(0, FF, chunk):
            part = slice(start, start + chunk)
            pre = mm(modulated, fc1_ref[:, part]) + bias_ref[0:1, part]
            square = pre * pre
            bend = jnp.tanh(GELU_A * pre * (1.0 + GELU_B * square))
            half = 0.5 * (1.0 + bend)
            act = (pre * half).astype(BF16)
            act_ref[:, part] = act
            slope_ref[:, part] = half + (0.5 * GELU_A) * pre * (1.0 - bend * bend) * (
                1.0 + (3.0 * GELU_B) * square
            )
            branch_two += mm(act, fc2_ref[part, :])
        branch_two += bias_ref[1:2, :D]
        out_ref[0] = (middle + gate_two * branch_two).astype(BF16)
        grad_out = cot_ref[0].astype(F32)
        dmod_ref[3, row, :] = col_sum(grad_out * branch_two)
        grad_two = gate_two * grad_out
        grad_two_low = grad_two.astype(BF16)
        dbias_ref[1:2, :D] += col_sum(grad_two_low.astype(F32))
        grad_two_t = grad_two_low.T
        modulated_t = modulated.T
        grad_mod = jnp.zeros_like(middle)
        for start in range(0, FF, chunk):
            part = slice(start, start + chunk)
            du = (mm_nt(grad_two_low, fc2_ref[part, :]) * slope_ref[:, part]).astype(BF16)
            dbias_ref[0:1, part] += col_sum(du.astype(F32))
            dfc2_ref[:, part] += mm(grad_two_t, act_ref[:, part])
            dfc1_ref[:, part] += mm(modulated_t, du)
            grad_mod += mm_nt(du, fc1_ref[:, part])
        dmod_ref[1, row, :] = col_sum(grad_mod)
        dmod_ref[2, row, :] = col_sum(grad_mod * normed)
        grad_middle = grad_out + normalize_back(grad_mod * (1.0 + scale), normed, rstd)
        dx_ref[0] = grad_middle
        dmod_ref[0, row, :] = col_sum(grad_middle * branch_one)
        grad_one = (gate_one * grad_middle).astype(BF16)
        dbias_ref[2:3, :D] += col_sum(grad_one.astype(F32))
        dproj_ref[...] += mm(mixed_ref[0], grad_one)
        dmixed_ref[0] = mm_nt(grad_one, proj_ref[...]).astype(BF16)

    @pl.when(step >= scal_ref[0])
    def _():
        out_ref[...] = jnp.zeros_like(out_ref)
        dx_ref[...] = jnp.zeros_like(dx_ref)
        dmixed_ref[...] = jnp.zeros_like(dmixed_ref)

    @pl.when(step == last)
    def _():
        for block in range(4):
            for tile in range(TILES):
                rows_ref[tile, pl.ds(FC1_AT + block, D, stride=4), :] = dfc1_ref[
                    :, lanes_of(tile, block * D)
                ]
                rows_ref[tile, pl.ds(B_FC1_AT + block, 1), :] = dbias_ref[0:1, lanes_of(tile, block * D)]
        for tile in range(TILES):
            rows_ref[tile, pl.ds(FC2_AT, FF), :] = dfc2_ref[lanes_of(tile), :].T
            rows_ref[tile, pl.ds(B_FC2_AT, 1), :] = dbias_ref[1:2, lanes_of(tile)]
            rows_ref[tile, pl.ds(B_PROJ_AT, 1), :] = dbias_ref[2:3, lanes_of(tile)]
        emit(scal_ref, 1 + sum(ref.shape[0] for ref in pieces), send_refs, rows_ref)


def backward_kernel(
    n_out, base, scal_ref, cond_ref, mod_ref, ada_ref, qkv_w_ref, dmod_in_ref, dproj_ref,
    x_ref, qkv_ref, probs_ref, dx_ref, dmixed_ref, *refs
):
    grad_x_ref, grad_cond_ref = refs[:2]
    send_refs = refs[2 : 2 + n_out]
    rows_ref, dqkv_w_ref, dmod_ref, dbias_ref, dqkv_ref, dq_t_ref = refs[2 + n_out :]
    step = pl.program_id(0)
    last = pl.num_programs(0) - 1

    @pl.when(step == 0)
    def _():
        dqkv_w_ref[...] = jnp.zeros_like(dqkv_w_ref)
        dmod_ref[...] = jnp.zeros_like(dmod_ref)
        dbias_ref[...] = jnp.zeros_like(dbias_ref)

    @pl.when(step < scal_ref[0])
    def _():
        masks = head_masks()
        row = pl.ds(step, 1)
        shift = mod_ref[0, row, :]
        scale = mod_ref[1, row, :]
        normed, rstd = normalize(x_ref[0].astype(F32))
        modulated = (normed * (1.0 + scale) + shift).astype(BF16)
        keys_t = qkv_ref[0, :, D : 2 * D].T
        for pair in range(HEADS // 2):
            query = qkv_ref[0, :, lanes_of(pair)]
            value = qkv_ref[0, :, lanes_of(pair, 2 * D)]
            grad = dmixed_ref[0, :, lanes_of(pair)]
            grad_key = jnp.zeros((query.shape[0], LANES), F32)
            grad_value = jnp.zeros((query.shape[0], LANES), F32)
            for half in range(2):
                head = 2 * pair + half
                rows = slice(head * HEAD_DIM, (head + 1) * HEAD_DIM)
                query_own = query * masks[half]
                grad_own = grad * masks[half]
                probs = probs_ref[0, head]
                grad_value += mm(probs.astype(BF16), grad_own)
                grad_probs = mm_nt(value, grad_own)
                grad_scores = (probs * (grad_probs - col_sum(probs * grad_probs))).astype(BF16)
                grad_key += mm(grad_scores, query_own)
                dq_t_ref[rows, :] = mm(keys_t[rows, :], grad_scores)
            dqkv_ref[:, lanes_of(pair, D)] = (grad_key * FACTOR).astype(BF16)
            dqkv_ref[:, lanes_of(pair, 2 * D)] = grad_value.astype(BF16)
        dqkv_ref[:, :D] = (dq_t_ref[...] * FACTOR).astype(BF16).T
        grad_qkv = dqkv_ref[...]
        dbias_ref[0:1, :] += col_sum(grad_qkv.astype(F32))
        dqkv_w_ref[...] += mm(modulated.T, grad_qkv)
        grad_mod = mm_nt(grad_qkv, qkv_w_ref[...])
        dmod_ref[0, row, :] = col_sum(grad_mod)
        dmod_ref[1, row, :] = col_sum(grad_mod * normed)
        grad_x_ref[0] = dx_ref[0] + normalize_back(grad_mod * (1.0 + scale), normed, rstd)

    @pl.when(step >= scal_ref[0])
    def _():
        grad_x_ref[...] = jnp.zeros_like(grad_x_ref)

    @pl.when(step == last)
    def _():
        cond = cond_ref[...].astype(F32)
        gate = jax.nn.sigmoid(cond)
        act = (cond * gate).astype(BF16)
        grad_act = jnp.zeros_like(cond)
        for block in range(6):
            grad = (dmod_ref[block] if block < 2 else dmod_in_ref[block - 2]).astype(BF16)
            grad_act += mm_nt(grad, ada_ref[block])
            weight = mm_tn(act, grad)
            bias = col_sum(grad.astype(F32))
            for tile in range(TILES):
                rows_ref[tile, pl.ds(ADA_AT + block, D, stride=6), :] = weight[:, lanes_of(tile)]
                rows_ref[tile, pl.ds(B_ADA_AT + block, 1), :] = bias[:, lanes_of(tile)]
        grad_cond_ref[...] = grad_act * (gate * (1.0 + cond * (1.0 - gate)))
        for tile in range(TILES):
            for block in range(3):
                rows_ref[tile, pl.ds(QKV_AT + block, D, stride=3), :] = dqkv_w_ref[
                    :, lanes_of(tile, block * D)
                ]
            rows_ref[tile, pl.ds(PROJ_AT, D), :] = dproj_ref[:, lanes_of(tile)]
            rows_ref[tile, pl.ds(B_QV_AT, 1), :] = dbias_ref[0:1, lanes_of(tile)]
            rows_ref[tile, pl.ds(B_QV_AT + 1, 1), :] = dbias_ref[0:1, lanes_of(tile, 2 * D)]
        emit(scal_ref, base, send_refs, rows_ref)


class Direct:
    def __init__(self, count, me):
        self.count, self.me = count, me
        self.gathered = self.sent = [jnp.int32(index) for index in range(count)]
        self.slots = [(count, F32)]

    def gather(self, piece):
        return [lax.all_gather(piece, AXIS, axis=0)]

    def scatter(self, parts):
        return lax.psum_scatter(parts[0], AXIS, scatter_dimension=0)


class Stages:
    def __init__(self, count, me):
        self.me = me
        core, x, y, z = me % 2, me // 2 % 2, me // 4 % 2, me // 8

        def device(dz, dy, dx, dc):
            return (((z + dz) % 4 * 2 + (y + dy) % 2) * 2 + (x + dx) % 2) * 2 + (core + dc) % 2

        gathered = []
        for dc in range(2):
            gathered += [device(-k, 0, 0, dc) for k in (0, 1, 2, 3)]
            gathered += [device(-k, 0, 1, dc) for k in (0, 1)]
            gathered += [device(-k, 1, 0, dc) for k in (2, 3)]
            gathered += [device(-k, 1, dx, dc) for dx in (0, 1) for k in (0, 1)]
            gathered += [device(-k, dy, 1, dc) for dy in (0, 1) for k in (2, 3)]
        self.gathered = gathered
        sent = []
        for dc in (1, 0):
            sent += [device(k, dy, dx, dc) for dx in (0, 1) for k in (0, 1) for dy in (0, 1)]
            sent += [device(k, dy, dx, dc) for dy in (0, 1) for k in (2, 3) for dx in (0, 1)]
        self.sent = sent
        self.slots = [(8, BF16), (8, BF16), (8, F32), (8, F32)]

    def shift(self, values, dz=0, dy=0, dx=0, dc=0):
        pairs = []
        for source in range(32):
            core, x, y, z = source % 2, source // 2 % 2, source // 4 % 2, source // 8
            target = (((z + dz) % 4 * 2 + (y + dy) % 2) * 2 + (x + dx) % 2) * 2 + (core + dc) % 2
            pairs.append((source, target))
        return lax.ppermute(values, AXIS, pairs)

    def gather(self, piece):
        own = jnp.stack([piece] + [self.shift(piece, dz=k) for k in (1, 2, 3)])
        first, second = own[:2], own[2:]
        by_x = self.shift(first, dx=1)
        by_y = self.shift(second, dy=1)
        by_xy = self.shift(jnp.concatenate([first, by_x]), dy=1)
        by_yx = self.shift(jnp.concatenate([second, by_y]), dx=1)
        held = [own, by_x, by_y, by_xy, by_yx]
        return held + [self.shift(array, dc=1) for array in held]

    def scatter(self, parts):
        def send(values, **how):
            return self.shift(values.astype(BF16), **how).astype(F32)

        send_a, send_b, keep_a, keep_b = parts
        shape = keep_a.shape[1:]
        sum_a = (keep_a + send(send_a, dc=1)).reshape((2, 4) + shape)
        sum_b = (keep_b + send(send_b, dc=1)).reshape((2, 4) + shape)
        sum_a = (sum_a[0] + send(sum_a[1], dx=1)).reshape((2, 2) + shape)
        sum_b = (sum_b[0] + send(sum_b[1], dy=1)).reshape((2, 2) + shape)
        sum_a = sum_a[:, 0] + send(sum_a[:, 1], dy=1)
        sum_b = sum_b[:, 0] + send(sum_b[:, 1], dx=1)
        return (
            sum_a[0] + send(sum_a[1], dz=1) + send(sum_b[0], dz=2) + send(sum_b[1], dz=3)
        )


def to_piece(share, rows, me):
    size = share.shape[0]
    flat = jnp.zeros((rows * D,), share.dtype)
    return lax.dynamic_update_slice(flat, share, (size * me % GROUP,)).reshape(rows, D)


def from_piece(piece, size, me):
    return lax.dynamic_slice(piece.reshape(-1), (size * me % GROUP,), (size,))


def whole(shape=None):
    return pl.BlockSpec(memory_space=pltpu.VMEM)


def by_latent(*shape):
    zeros = (0,) * len(shape)
    return pl.BlockSpec((1,) + shape, lambda step, scal: (step,) + zeros)


def call(kernel, count, in_specs, out_specs, out_shape, scratch, args, flops):
    return pl.pallas_call(
        kernel,
        grid_spec=pltpu.PrefetchScalarGridSpec(
            num_scalar_prefetch=1,
            grid=(count,),
            in_specs=in_specs,
            out_specs=out_specs,
            scratch_shapes=scratch,
        ),
        out_shape=out_shape,
        compiler_params=pltpu.CompilerParams(
            vmem_limit_bytes=60 * 2**20, dimension_semantics=("arbitrary",)
        ),
        cost_estimate=pl.CostEstimate(flops=flops, bytes_accessed=20 * 2**20, transcendentals=0),
    )(*args)


def solution(mesh):
    devices = mesh.shape[AXIS]

    def body(latents, condition, attn_params, mlp_params, counts, cotangent):
        count, seq = latents.shape[0], latents.shape[1]
        me = lax.axis_index(AXIS)
        plan = (Stages if devices == 32 else Direct)(devices, me)
        attn_size, mlp_size = attn_params.shape[0], mlp_params.shape[0]
        attn_height = piece_rows(attn_size, devices)
        mlp_height = piece_rows(mlp_size, devices)

        def scalars(size):
            ids = jnp.stack(plan.gathered + plan.sent)
            return jnp.concatenate([counts.astype(jnp.int32), size * ids // GROUP]).astype(jnp.int32)

        attn_scal, mlp_scal = scalars(attn_size), scalars(mlp_size)
        attn_pieces = plan.gather(to_piece(attn_params, attn_height, me))
        mlp_pieces = plan.gather(to_piece(mlp_params, mlp_height, me))

        def struct(shape, kind):
            return jax.ShapeDtypeStruct(shape, kind)

        n_pieces = len(attn_pieces)
        n_out = len(plan.slots)
        mod, ada, qkv_w, proj, _, qkv, probs, mixed, branch = call(
            lambda *refs: forward_kernel(n_pieces, *refs),
            count,
            [whole(), by_latent(seq, D)] + [whole()] * n_pieces,
            [whole()] * 5
            + [
                by_latent(seq, 3 * D),
                by_latent(HEADS, seq, seq),
                by_latent(D, seq),
                by_latent(seq, D),
            ],
            [
                struct((6, count, D), F32),
                struct((6, D, D), BF16),
                struct((D, 3 * D), BF16),
                struct((D, D), BF16),
                struct((8, D), F32),
                struct((count, seq, 3 * D), BF16),
                struct((count, HEADS, seq, seq), F32),
                struct((count, D, seq), BF16),
                struct((count, seq, D), F32),
            ],
            [pltpu.VMEM((TILES, ATTN_ROWS + attn_height, LANES), F32)],
            [attn_scal, condition, latents] + attn_pieces,
            15 * 10**9,
        )
        results = call(
            lambda *refs: mlp_kernel(n_pieces, n_out, *refs),
            count,
            [whole(), whole(), by_latent(seq, D), by_latent(seq, D), by_latent(D, seq), by_latent(seq, D)]
            + [whole()] * n_pieces,
            [by_latent(seq, D), by_latent(seq, D), by_latent(seq, D), whole(), whole()]
            + [whole()] * n_out,
            [
                struct((count, seq, D), BF16),
                struct((count, seq, D), F32),
                struct((count, seq, D), BF16),
                struct((4, count, D), F32),
                struct((D, D), F32),
            ]
            + [struct((slots, mlp_height, D), kind) for slots, kind in plan.slots],
            [
                pltpu.VMEM((TILES, MLP_ROWS + 2 + mlp_height, LANES), F32),
                pltpu.VMEM((D, FF), BF16),
                pltpu.VMEM((FF, D), BF16),
                pltpu.VMEM((8, FF), F32),
                pltpu.VMEM((seq, FF), BF16),
                pltpu.VMEM((seq, FF), F32),
                pltpu.VMEM((D, FF), F32),
                pltpu.VMEM((D, FF), F32),
                pltpu.VMEM((8, FF), F32),
            ],
            [mlp_scal, mod, proj, latents, branch, mixed, cotangent] + mlp_pieces,
            30 * 10**9,
        )
        output, grad_middle, grad_mixed, dmod, dproj = results[:5]
        grad_mlp = plan.scatter(results[5:])
        results = call(
            lambda *refs: backward_kernel(n_out, 1 + devices, *refs),
            count,
            [whole()] * 6
            + [
                by_latent(seq, D),
                by_latent(seq, 3 * D),
                by_latent(HEADS, seq, seq),
                by_latent(seq, D),
                by_latent(seq, D),
            ],
            [by_latent(seq, D), whole()] + [whole()] * n_out,
            [struct((count, seq, D), F32), struct((count, D), F32)]
            + [struct((slots, attn_height, D), kind) for slots, kind in plan.slots],
            [
                pltpu.VMEM((TILES, ATTN_ROWS + attn_height, LANES), F32),
                pltpu.VMEM((D, 3 * D), F32),
                pltpu.VMEM((2, count, D), F32),
                pltpu.VMEM((8, 3 * D), F32),
                pltpu.VMEM((seq, 3 * D), BF16),
                pltpu.VMEM((D, seq), F32),
            ],
            [attn_scal, condition, mod, ada, qkv_w, dmod, dproj, latents, qkv, probs, grad_middle, grad_mixed],
            30 * 10**9,
        )
        grad_latents, grad_condition = results[:2]
        grad_attn = plan.scatter(results[2:])
        return (
            output,
            grad_latents,
            grad_condition,
            from_piece(grad_attn, attn_size, me),
            from_piece(grad_mlp, mlp_size, me),
        )

    in_specs = (
        P(AXIS, None, None),
        P(AXIS, None),
        P(AXIS),
        P(AXIS),
        P(AXIS),
        P(AXIS, None, None),
    )
    out_specs = (
        P(AXIS, None, None),
        P(AXIS, None, None),
        P(AXIS, None),
        P(AXIS),
        P(AXIS),
    )
    return jax.shard_map(body, mesh=mesh, in_specs=in_specs, out_specs=out_specs, check_vma=False)
```

time: 599 us -> 196 us (0.33); the launches traced: 589 us -> 196 us
  waiting for transfers between devices: 361 us -> 45 us
  matrix products: 113 us -> 0 us
  Pallas kernels: 0 us -> 73.6 us
  starting transfers between devices: 0.08 us -> 67.3 us
  local copies, waits for them, and re-layouts: 72.5 us -> 6.48 us
  other arithmetic: 26.4 us -> 2.07 us
  between operations: 15.6 us -> 1.86 us
    unnamed x4 -> x0, waiting for transfers between devices: 361 us -> none
    dot_general x51 -> x0, matrix products: 113 us -> none  [the longest x5 28.5 us: back_product(): lax.dot_general(grad, weight, (((1,), (1,)), ((), ())), preferred_element...]
    pallas_call x0 -> x3, Pallas kernels: none -> 73.6 us  [call(): pl.pallas_call(kernel, grid_spec=pltpu.PrefetchScalarGridSpec(num_scalar_...]
    ppermute x0 -> x42, starting transfers between devices: none -> 67.3 us  [shift(): return lax.ppermute(values, AXIS, pairs)]
    ppermute x0 -> x42, waiting for transfers between devices: none -> 45 us  [shift(): return lax.ppermute(values, AXIS, pairs)]
    unnamed x123 -> x40, local copies, waits for them, and re-layouts: 36.8 us -> 1.33 us
    reshape x9 -> x4, local copies, waits for them, and re-layouts: 24.3 us -> 0.13 us  [the longest x2 0.1 us: to_piece(): lax.dynamic_update_slice(flat, share, (size * me % GROUP,)).reshape(rows, D)]
    reduce_sum x16 -> x0, other arithmetic: 17.4 us -> none  [the longest x5 9.78 us: column_sum(): return jnp.sum(values.astype(jnp.float32), axis=0)]
  transfers between devices with their start and end apart: 2 -> 42, of which waited for: 2 -> 17; matrix products, arithmetic and copies ran while one was open for 0% -> 2% of each run, Pallas kernels for 0% -> 23%
where the time goes in v1:
time: 196 us
  Pallas kernels  73.6 us (38%)
  starting transfers between devices  67.3 us (34%)
  waiting for transfers between devices  45 us (23%)
  local copies, waits for them, and re-layouts  6.48 us (3%)
  other arithmetic  2.07 us (1%)
    pallas_call x3, Pallas kernels, call(): pl.pallas_call(kernel, grid_spec=pltpu.PrefetchScalarGridSpec(num_scalar_...  73.6 us
    ppermute x42, starting transfers between devices, shift(): return lax.ppermute(values, AXIS, pairs)  67.3 us
    ppermute x42, waiting for transfers between devices, shift(): return lax.ppermute(values, AXIS, pairs)  45 us
  transfers between devices with their start and end apart: 42, of which 17 were waited for; matrix products, arithmetic and copies ran while one was open for 2% of the time, Pallas kernels for 23%

profile of v1, /device:TPU:0, one launch (start us, length us, event | category | flops | bytes accessed | tf_op | source)
XLA Modules:
  0.0 196.4 jit_solution(6104904079233886390)
XLA Ops:
  0.7 2.0 %dynamic_update_slice.6 = bf16[49152]{0:T(1024)(128)(2,1)S(1)} dynamic-update-slice(bf16[49152]{0:T(1024)(128)(2,1)S(1)} %broadcast_in_dim.6, bf16[46176]{0:T(1024)(128)(2,1)} %param.8, s32[]{:T(128)S(6)} %select_n.613) | dynamic-update-slice | bytes 184708 | tf_op jit(solution)/shard_map/dynamic_update_slice | solution.py:434
  2.7 4.1 %collective-permute-start.1 = (bf16[128,384]{1,0:T(8,128)(2,1)S(1)}, bf16[128,384]{1,0:T(8,128)(2,1)S(1)}, u32[]{:S(2)}, u32[]{:S(2)}) collective-permute-start(bf16[128,384]{1,0:T(8,128)(2,1)S(1)} %reshape.64), channel_id=1, source_target_pairs={{0,16},{1,17},{2,18},{3,19},{4,20},{5,21},{6,22},{7,23},{8,24},{9,... | collective-permute-start | bytes 294920 | tf_op jit(solution)/shard_map/ppermute | solution.py:402
  6.8 1.4 collective-permute-start.2
  8.2 0.7 collective-permute-start
  8.9 4.3 %collective-permute-done.1 = bf16[128,384]{1,0:T(8,128)(2,1)S(1)} collective-permute-done((bf16[128,384]{1,0:T(8,128)(2,1)S(1)}, bf16[128,384]{1,0:T(8,128)(2,1)S(1)}, u32[]{:S(2)}, u32[]{:S(2)}) %collective-permute-start.1) | collective-permute-done | bytes 98336 | tf_op jit(solution)/shard_map/ppermute | solution.py:402
  13.2 1.8 collective-permute-start.4
  15.1 1.6 collective-permute-start.3
  16.6 0.9 dynamic_update_slice.7
  17.6 3.6 %collective-permute-start.13 = (bf16[112,384]{1,0:T(8,128)(2,1)S(1)}, bf16[112,384]{1,0:T(8,128)(2,1)S(1)}, u32[]{:S(2)}, u32[]{:S(2)}) collective-permute-start(bf16[112,384]{1,0:T(8,128)(2,1)S(1)} %reshape.65), channel_id=1, source_target_pairs={{0,16},{1,17},{2,18},{3,19},{4,20},{5,21},{6,22},{7,23},{8,24},{9,... | collective-permute-start | bytes 258056 | tf_op jit(solution)/shard_map/ppermute | solution.py:402
  21.2 2.0 %collective-permute-start.14 = (bf16[112,384]{1,0:T(8,128)(2,1)S(1)}, bf16[112,384]{1,0:T(8,128)(2,1)S(1)}, u32[]{:S(2)}, u32[]{:S(2)}) collective-permute-start(bf16[112,384]{1,0:T(8,128)(2,1)S(1)} %reshape.65), channel_id=1, source_target_pairs={{0,24},{1,25},{2,26},{3,27},{4,28},{5,29},{6,30},{7,31},{8,0},{9,1... | collective-permute-start | bytes 258056 | tf_op jit(solution)/shard_map/ppermute | solution.py:402
  23.3 0.1 pad_maximum_fusion.3
  23.5 1.6 collective-permute-start.5
  25.0 0.5 collective-permute-start.6
  25.6 1.1 collective-permute-done.13
  26.8 2.1 %collective-permute-start.16 = (bf16[2,112,384]{2,1,0:T(8,128)(2,1)S(1)}, bf16[2,112,384]{2,1,0:T(8,128)(2,1)S(1)}, u32[]{:S(2)}, u32[]{:S(2)}) collective-permute-start(bf16[2,112,384]{2,1,0:T(8,128)(2,1)S(1)} %pad_maximum_fusion.11), channel_id=1, source_target_pairs={{0,4},{1,5},{2,6},{3,7},{4,0},{5,1},{6,2},{7,3},{8,12},{9,13},{10,... | collective-permute-start | bytes 516104 | tf_op jit(solution)/shard_map/ppermute | solution.py:402
  28.9 0.5 collective-permute-done.12
  29.4 0.6 collective-permute-start.15
  30.1 7.1 %collective-permute-done.16.refs_9_ = bf16[2,112,384]{2,1,0:T(8,128)(2,1)S(1)} collective-permute-done((bf16[2,112,384]{2,1,0:T(8,128)(2,1)S(1)}, bf16[2,112,384]{2,1,0:T(8,128)(2,1)S(1)}, u32[]{:S(2)}, u32[]{:S(2)}) %collective-permute-start.16) | collective-permute-done | bytes 172064 | tf_op jit(solution)/shard_map/ppermute | solution.py:402
  37.2 1.2 collective-permute-done.15.refs_8_
  38.4 0.5 collective-permute-start.10
  39.0 0.1 pad_maximum_fusion.7
  39.1 0.9 collective-permute-start.17
  40.0 0.5 collective-permute-start.18
  41.2 0.1 stack.332
  41.4 0.6 pad_add_fusion
  42.0 7.6 %collective-permute-done.17.refs_10_ = bf16[4,112,384]{2,1,0:T(8,128)(2,1)S(1)} collective-permute-done((bf16[4,112,384]{2,1,0:T(8,128)(2,1)S(1)}, bf16[4,112,384]{2,1,0:T(8,128)(2,1)S(1)}, u32[]{:S(2)}, u32[]{:S(2)}) %collective-permute-start.17) | collective-permute-done | bytes 344096 | tf_op jit(solution)/shard_map/ppermute | solution.py:402
  49.6 0.2 collective-permute-done.18.refs_11_
  49.8 0.3 collective-permute-start.21
  50.1 0.2 collective-permute-start.20
  50.3 0.3 collective-permute-start.22
  50.6 0.2 collective-permute-start.23
  50.9 22.3 %shard_map.101 = (f32[6,8,384]{2,1,0:T(8,128)}, bf16[6,384,384]{2,1,0:T(8,128)(2,1)}, bf16[384,1152]{1,0:T(8,128)(2,1)}, bf16[384,384]{1,0:T(8,128)(2,1)}, f32[8...) custom-call(s32[65]{0:T(128)} %get-tuple-element.64.refs_0_, ...), custom_call_target="tpu_custom_call" | custom-call | flops 15000000512 | bytes 20971520 | tf_op jit(solution)/shard_map/pallas_call | solution.py:451
  73.4 0.6 copy-done.18
  74.0 0.1 copy-done.15
  74.3 27.6 %shard_map.102 = (bf16[8,256,384]{2,1,0:T(8,128)(2,1)}, f32[8,256,384]{2,1,0:T(8,128)}, bf16[8,256,384]{2,1,0:T(8,128)(2,1)}, f32[4,8,384]{2,1,0:T(8,128)}, f32[...) custom-call(s32[65]{0:T(128)} %get-tuple-element.63.refs_0_, ...), custom_call_target="tpu_custom_call" | custom-call | flops 30000001024 | bytes 20971520 | tf_op jit(solution)/shard_map/pallas_call | solution.py:451
  101.9 14.6 %collective-permute-start.37 = (bf16[8,112,384]{2,1,0:T(8,128)(2,1)}, bf16[8,112,384]{2,1,0:T(8,128)(2,1)S(1)}, u32[]{:S(2)}, u32[]{:S(2)}) collective-permute-start(bf16[8,112,384]{2,1,0:T(8,128)(2,1)} %get-tuple-element.50), channel_id=1, source_target_pairs={{0,1},{1,0},{2,3},{3,2},{4,5},{5,4},{6,7},{7,6},{8,9},{9,8},{10,11... | collective-permute-start | bytes 2064392 | tf_op jit(solution)/shard_map/ppermute | solution.py:402
  116.7 23.7 %shard_map.103 = (f32[8,256,384]{2,1,0:T(8,128)}, f32[8,384]{1,0:T(8,128)}, bf16[8,128,384]{2,1,0:T(8,128)(2,1)}, bf16[8,128,384]{2,1,0:T(8,128)(2,1)}, f32[8,128,384]{2,1,0:T(8,128)}, /*index=5*/f32[8,128,384]{2,1,0:T(8,128)}) custom-call(s32[65]{0:T(128)} %get-tuple-element.64.refs_0_, bf16[8,384]{1,0:T(8,128)(2,1)} %refs_1_.3, ...), custom_call_target="tpu_custom_call" | custom-call | flops 30000001024 | bytes 20971520 | tf_op jit(solution)/shard_map/pallas_call | solution.py:451
  140.3 4.8 %collective-permute-start.28 = (bf16[8,128,384]{2,1,0:T(8,128)(2,1)}, bf16[8,128,384]{2,1,0:T(8,128)(2,1)S(1)}, u32[]{:S(2)}, u32[]{:S(2)}) collective-permute-start(bf16[8,128,384]{2,1,0:T(8,128)(2,1)} %get-tuple-element.46), channel_id=1, source_target_pairs={{0,1},{1,0},{2,3},{3,2},{4,5},{5,4},{6,7},{7,6},{8,9},{9,8},{10,11... | collective-permute-start | bytes 2359304 | tf_op jit(solution)/shard_map/ppermute | solution.py:402
  145.4 9.9 %collective-permute-start.38 = (bf16[4,112,384]{2,1,0:T(8,128)(2,1)S(1)}, bf16[4,112,384]{2,1,0:T(8,128)(2,1)S(1)}, u32[]{:S(2)}, u32[]{:S(2)}) collective-permute-start(bf16[4,112,384]{2,1,0:T(8,128)(2,1)S(1)} %slice.200), channel_id=1, source_target_pairs={{0,4},{1,5},{2,6},{3,7},{4,0},{5,1},{6,2},{7,3},{8,12},{9,13},{10,... | collective-permute-start | bytes 1032200 | tf_op jit(solution)/shard_map/ppermute | solution.py:402
  155.2 0.1 convert_add_fusion.3
  155.4 1.0 collective-permute-start.34
  156.4 0.2 copy-done.1
  156.8 1.2 collective-permute-start.29
  158.2 1.0 collective-permute-start.25
  159.2 4.9 %collective-permute-done.38 = bf16[4,112,384]{2,1,0:T(8,128)(2,1)S(1)} collective-permute-done((bf16[4,112,384]{2,1,0:T(8,128)(2,1)S(1)}, bf16[4,112,384]{2,1,0:T(8,128)(2,1)S(1)}, u32[]{:S(2)}, u32[]{:S(2)}) %collective-permute-start.38) | collective-permute-done | bytes 344096 | tf_op jit(solution)/shard_map/ppermute | solution.py:402
  164.2 0.9 collective-permute-start.39
  165.1 1.3 collective-permute-done.34
  166.5 1.1 collective-permute-start.35
  167.6 5.0 %collective-permute-done.29 = bf16[4,128,384]{2,1,0:T(8,128)(2,1)S(1)} collective-permute-done((bf16[4,128,384]{2,1,0:T(8,128)(2,1)S(1)}, bf16[4,128,384]{2,1,0:T(8,128)(2,1)S(1)}, u32[]{:S(2)}, u32[]{:S(2)}) %collective-permute-start.29) | collective-permute-done | bytes 393248 | tf_op jit(solution)/shard_map/ppermute | solution.py:402
  172.7 0.9 collective-permute-start.30
  173.6 1.3 collective-permute-done.25
  175.0 1.1 collective-permute-start.26
  176.1 2.4 %collective-permute-done.39 = bf16[2,112,384]{2,1,0:T(8,128)(2,1)S(1)} collective-permute-done((bf16[2,112,384]{2,1,0:T(8,128)(2,1)S(1)}, bf16[2,112,384]{2,1,0:T(8,128)(2,1)S(1)}, u32[]{:S(2)}, u32[]{:S(2)}) %collective-permute-start.39) | collective-permute-done | bytes 172064 | tf_op jit(solution)/shard_map/ppermute | solution.py:402
  178.6 2.0 %collective-permute-start.40 = (bf16[112,384]{1,0:T(8,128)(2,1)S(1)}, bf16[112,384]{1,0:T(8,128)(2,1)S(1)}, u32[]{:S(2)}, u32[]{:S(2)}) collective-permute-start(bf16[112,384]{1,0:T(8,128)(2,1)S(1)} %get-tuple-element.56), channel_id=1, source_target_pairs={{0,16},{1,17},{2,18},{3,19},{4,20},{5,21},{6,22},{7,23},{8,24},{9,... | collective-permute-start | bytes 258056 | tf_op jit(solution)/shard_map/ppermute | solution.py:402
  180.6 1.1 collective-permute-start.41
  181.7 1.0 collective-permute-start.36
  182.8 1.5 collective-permute-start.31
  184.3 2.2 %collective-permute-start.32 = (bf16[128,384]{1,0:T(8,128)(2,1)S(1)}, bf16[128,384]{1,0:T(8,128)(2,1)S(1)}, u32[]{:S(2)}, u32[]{:S(2)}) collective-permute-start(bf16[128,384]{1,0:T(8,128)(2,1)S(1)} %get-tuple-element.52), channel_id=1, source_target_pairs={{0,24},{1,25},{2,26},{3,27},{4,28},{5,29},{6,30},{7,31},{8,0},{9,1... | collective-permute-start | bytes 294920 | tf_op jit(solution)/shard_map/ppermute | solution.py:402
  186.6 2.2 %collective-permute-done.40 = bf16[112,384]{1,0:T(8,128)(2,1)S(1)} collective-permute-done((bf16[112,384]{1,0:T(8,128)(2,1)S(1)}, bf16[112,384]{1,0:T(8,128)(2,1)S(1)}, u32[]{:S(2)}, u32[]{:S(2)}) %collective-permute-start.40) | collective-permute-done | bytes 86048 | tf_op jit(solution)/shard_map/ppermute | solution.py:402
  188.8 0.3 collective-permute-done.36
  189.1 0.8 dynamic_slice.7
  189.9 4.4 %collective-permute-done.31 = bf16[128,384]{1,0:T(8,128)(2,1)S(1)} collective-permute-done((bf16[128,384]{1,0:T(8,128)(2,1)S(1)}, bf16[128,384]{1,0:T(8,128)(2,1)S(1)}, u32[]{:S(2)}, u32[]{:S(2)}) %collective-permute-start.31) | collective-permute-done | bytes 98336 | tf_op jit(solution)/shard_map/ppermute | solution.py:402
  194.3 1.2 collective-permute-done.27
  195.6 0.8 dynamic_slice.6
  (110 shorter events, 2.5 us)
Async XLA Ops:
  0.6 16.0 %copy-start.10 = (bf16[36936]{0:T(1024)(128)(2,1)S(1)}, bf16[36936]{0:T(1024)(128)(2,1)}, u32[]{:S(2)}) copy-start(bf16[36936]{0:T(1024)(128)(2,1)} %param.9) | copy-start | bytes 221620
  2.7 10.4 %collective-permute-start.1 = (bf16[128,384]{1,0:T(8,128)(2,1)S(1)}, bf16[128,384]{1,0:T(8,128)(2,1)S(1)}, u32[]{:S(2)}, u32[]{:S(2)}) collective-permute-start(bf16[128,384]{1,0:T(8,128)(2,1)S(1)} %reshape.64), channel_id=1, source_target_pairs={{0,16},{1,17},{2,18},{3,19},{4,20},{5,21},{6,22},{7,23},{8,24},{9,... | collective-permute-start | bytes 294920 | tf_op jit(solution)/shard_map/ppermute | solution.py:402
  6.8 6.4 %collective-permute-start.2 = (bf16[128,384]{1,0:T(8,128)(2,1)S(1)}, bf16[128,384]{1,0:T(8,128)(2,1)S(1)}, u32[]{:S(2)}, u32[]{:S(2)}) collective-permute-start(bf16[128,384]{1,0:T(8,128)(2,1)S(1)} %reshape.64), channel_id=1, source_target_pairs={{0,24},{1,25},{2,26},{3,27},{4,28},{5,29},{6,30},{7,31},{8,0},{9,1... | collective-permute-start | bytes 294920 | tf_op jit(solution)/shard_map/ppermute | solution.py:402
  8.2 6.8 %collective-permute-start = (bf16[128,384]{1,0:T(8,128)(2,1)S(1)}, bf16[128,384]{1,0:T(8,128)(2,1)S(1)}, u32[]{:S(2)}, u32[]{:S(2)}) collective-permute-start(bf16[128,384]{1,0:T(8,128)(2,1)S(1)} %reshape.64), channel_id=1, source_target_pairs={{0,8},{1,9},{2,10},{3,11},{4,12},{5,13},{6,14},{7,15},{8,16},{9,17... | collective-permute-start | bytes 294920 | tf_op jit(solution)/shard_map/ppermute | solution.py:402
  13.2 10.0 %collective-permute-start.4 = (bf16[2,128,384]{2,1,0:T(8,128)(2,1)S(1)}, bf16[2,128,384]{2,1,0:T(8,128)(2,1)S(1)}, u32[]{:S(2)}, u32[]{:S(2)}) collective-permute-start(bf16[2,128,384]{2,1,0:T(8,128)(2,1)S(1)} %pad_maximum_fusion.9), channel_id=1, source_target_pairs={{0,4},{1,5},{2,6},{3,7},{4,0},{5,1},{6,2},{7,3},{8,12},{9,13},{10,... | collective-permute-start | bytes 589832 | tf_op jit(solution)/shard_map/ppermute | solution.py:402
  15.1 8.2 %collective-permute-start.3 = (bf16[2,128,384]{2,1,0:T(8,128)(2,1)S(1)}, bf16[2,128,384]{2,1,0:T(8,128)(2,1)S(1)}, u32[]{:S(2)}, u32[]{:S(2)}) collective-permute-start(bf16[2,128,384]{2,1,0:T(8,128)(2,1)S(1)} %pad_maximum_fusion.8), channel_id=1, source_target_pairs={{0,2},{1,3},{2,0},{3,1},{4,6},{5,7},{6,4},{7,5},{8,10},{9,11},{10,... | collective-permute-start | bytes 589832 | tf_op jit(solution)/shard_map/ppermute | solution.py:402
  17.6 9.1 %collective-permute-start.13 = (bf16[112,384]{1,0:T(8,128)(2,1)S(1)}, bf16[112,384]{1,0:T(8,128)(2,1)S(1)}, u32[]{:S(2)}, u32[]{:S(2)}) collective-permute-start(bf16[112,384]{1,0:T(8,128)(2,1)S(1)} %reshape.65), channel_id=1, source_target_pairs={{0,16},{1,17},{2,18},{3,19},{4,20},{5,21},{6,22},{7,23},{8,24},{9,... | collective-permute-start | bytes 258056 | tf_op jit(solution)/shard_map/ppermute | solution.py:402
  21.2 5.6 %collective-permute-start.14 = (bf16[112,384]{1,0:T(8,128)(2,1)S(1)}, bf16[112,384]{1,0:T(8,128)(2,1)S(1)}, u32[]{:S(2)}, u32[]{:S(2)}) collective-permute-start(bf16[112,384]{1,0:T(8,128)(2,1)S(1)} %reshape.65), channel_id=1, source_target_pairs={{0,24},{1,25},{2,26},{3,27},{4,28},{5,29},{6,30},{7,31},{8,0},{9,1... | collective-permute-start | bytes 258056 | tf_op jit(solution)/shard_map/ppermute | solution.py:402
  23.1 6.3 %collective-permute-start.12 = (bf16[112,384]{1,0:T(8,128)(2,1)S(1)}, bf16[112,384]{1,0:T(8,128)(2,1)S(1)}, u32[]{:S(2)}, u32[]{:S(2)}) collective-permute-start(bf16[112,384]{1,0:T(8,128)(2,1)S(1)} %reshape.65), channel_id=1, source_target_pairs={{0,8},{1,9},{2,10},{3,11},{4,12},{5,13},{6,14},{7,15},{8,16},{9,17... | collective-permute-start | bytes 258056 | tf_op jit(solution)/shard_map/ppermute | solution.py:402
  23.3 13.9 %copy-start.6 = (bf16[2,128,384]{2,1,0:T(8,128)(2,1)}, bf16[2,128,384]{2,1,0:T(8,128)(2,1)S(1)}, u32[]{:S(2)}) copy-start(bf16[2,128,384]{2,1,0:T(8,128)(2,1)S(1)} %collective-permute-done.4.refs_5_) | copy-start | bytes 589828
  23.3 13.9 %copy-start.7 = (bf16[2,128,384]{2,1,0:T(8,128)(2,1)}, bf16[2,128,384]{2,1,0:T(8,128)(2,1)S(1)}, u32[]{:S(2)}) copy-start(bf16[2,128,384]{2,1,0:T(8,128)(2,1)S(1)} %collective-permute-done.3.refs_4_) | copy-start | bytes 589828
  23.4 17.7 %copy-start.4 = (bf16[4,128,384]{2,1,0:T(8,128)(2,1)}, bf16[4,128,384]{2,1,0:T(8,128)(2,1)S(1)}, u32[]{:S(2)}) copy-start(bf16[4,128,384]{2,1,0:T(8,128)(2,1)S(1)} %get-tuple-element.54.refs_3_) | copy-start | bytes 1179652
  23.5 14.9 %collective-permute-start.5 = (bf16[4,128,384]{2,1,0:T(8,128)(2,1)S(1)}, bf16[4,128,384]{2,1,0:T(8,128)(2,1)S(1)}, u32[]{:S(2)}, u32[]{:S(2)}) collective-permute-start(bf16[4,128,384]{2,1,0:T(8,128)(2,1)S(1)} %get-tuple-element.55), channel_id=1, source_target_pairs={{0,4},{1,5},{2,6},{3,7},{4,0},{5,1},{6,2},{7,3},{8,12},{9,13},{10,... | collective-permute-start | bytes 1179656 | tf_op jit(solution)/shard_map/ppermute | solution.py:402
  25.0 13.8 %collective-permute-start.6 = (bf16[4,128,384]{2,1,0:T(8,128)(2,1)S(1)}, bf16[4,128,384]{2,1,0:T(8,128)(2,1)S(1)}, u32[]{:S(2)}, u32[]{:S(2)}) collective-permute-start(bf16[4,128,384]{2,1,0:T(8,128)(2,1)S(1)} %get-tuple-element.53), channel_id=1, source_target_pairs={{0,2},{1,3},{2,0},{3,1},{4,6},{5,7},{6,4},{7,5},{8,10},{9,11},{10,... | collective-permute-start | bytes 1179656 | tf_op jit(solution)/shard_map/ppermute | solution.py:402
  26.8 10.4 %collective-permute-start.16 = (bf16[2,112,384]{2,1,0:T(8,128)(2,1)S(1)}, bf16[2,112,384]{2,1,0:T(8,128)(2,1)S(1)}, u32[]{:S(2)}, u32[]{:S(2)}) collective-permute-start(bf16[2,112,384]{2,1,0:T(8,128)(2,1)S(1)} %pad_maximum_fusion.11), channel_id=1, source_target_pairs={{0,4},{1,5},{2,6},{3,7},{4,0},{5,1},{6,2},{7,3},{8,12},{9,13},{10,... | collective-permute-start | bytes 516104 | tf_op jit(solution)/shard_map/ppermute | solution.py:402
  29.4 8.9 %collective-permute-start.15 = (bf16[2,112,384]{2,1,0:T(8,128)(2,1)S(1)}, bf16[2,112,384]{2,1,0:T(8,128)(2,1)S(1)}, u32[]{:S(2)}, u32[]{:S(2)}) collective-permute-start(bf16[2,112,384]{2,1,0:T(8,128)(2,1)S(1)} %pad_maximum_fusion.10), channel_id=1, source_target_pairs={{0,2},{1,3},{2,0},{3,1},{4,6},{5,7},{6,4},{7,5},{8,10},{9,11},{10,... | collective-permute-start | bytes 516104 | tf_op jit(solution)/shard_map/ppermute | solution.py:402
  30.1 9.1 %collective-permute-start.9 = (bf16[2,128,384]{2,1,0:T(8,128)(2,1)S(1)}, bf16[2,128,384]{2,1,0:T(8,128)(2,1)}, u32[]{:S(2)}, u32[]{:S(2)}) collective-permute-start(bf16[2,128,384]{2,1,0:T(8,128)(2,1)S(1)} %collective-permute-done.4.refs_5_), channel_id=1, source_target_pairs={{0,1},{1,0},{2,3},{3,2},{4,5},{5,4},{6,7},{7,6},{8,9},{9,8},{10,11... | collective-permute-start | bytes 589832 | tf_op jit(solution)/shard_map/ppermute | solution.py:402
  37.1 36.1 %copy-start.8 = (bf16[2,112,384]{2,1,0:T(8,128)(2,1)}, bf16[2,112,384]{2,1,0:T(8,128)(2,1)S(1)}, u32[]{:S(2)}) copy-start(bf16[2,112,384]{2,1,0:T(8,128)(2,1)S(1)} %collective-permute-done.16.refs_9_) | copy-start | bytes 516100
  37.1 2.9 %collective-permute-start.8 = (bf16[2,128,384]{2,1,0:T(8,128)(2,1)S(1)}, bf16[2,128,384]{2,1,0:T(8,128)(2,1)}, u32[]{:S(2)}, u32[]{:S(2)}) collective-permute-start(bf16[2,128,384]{2,1,0:T(8,128)(2,1)S(1)} %collective-permute-done.3.refs_4_), channel_id=1, source_target_pairs={{0,1},{1,0},{2,3},{3,2},{4,5},{5,4},{6,7},{7,6},{8,9},{9,8},{10,11... | collective-permute-start | bytes 589832 | tf_op jit(solution)/shard_map/ppermute | solution.py:402
  38.4 34.9 %copy-start.9 = (bf16[2,112,384]{2,1,0:T(8,128)(2,1)}, bf16[2,112,384]{2,1,0:T(8,128)(2,1)S(1)}, u32[]{:S(2)}) copy-start(bf16[2,112,384]{2,1,0:T(8,128)(2,1)S(1)} %collective-permute-done.15.refs_8_) | copy-start | bytes 516100
  38.4 11.8 %collective-permute-start.7 = (bf16[4,128,384]{2,1,0:T(8,128)(2,1)S(1)}, bf16[4,128,384]{2,1,0:T(8,128)(2,1)}, u32[]{:S(2)}, u32[]{:S(2)}) collective-permute-start(bf16[4,128,384]{2,1,0:T(8,128)(2,1)S(1)} %get-tuple-element.54.refs_3_), channel_id=1, source_target_pairs={{0,1},{1,0},{2,3},{3,2},{4,5},{5,4},{6,7},{7,6},{8,9},{9,8},{10,11... | collective-permute-start | bytes 1179656 | tf_op jit(solution)/shard_map/ppermute | solution.py:402
  38.4 12.5 %copy-start.11 = (bf16[4,128,384]{2,1,0:T(8,128)(2,1)}, bf16[4,128,384]{2,1,0:T(8,128)(2,1)S(1)}, u32[]{:S(2)}) copy-start(bf16[4,128,384]{2,1,0:T(8,128)(2,1)S(1)} %collective-permute-done.5.refs_6_) | copy-start | bytes 1179652
  38.4 12.0 %collective-permute-start.10 = (bf16[4,128,384]{2,1,0:T(8,128)(2,1)S(1)}, bf16[4,128,384]{2,1,0:T(8,128)(2,1)}, u32[]{:S(2)}, u32[]{:S(2)}) collective-permute-start(bf16[4,128,384]{2,1,0:T(8,128)(2,1)S(1)} %collective-permute-done.5.refs_6_), channel_id=1, source_target_pairs={{0,1},{1,0},{2,3},{3,2},{4,5},{5,4},{6,7},{7,6},{8,9},{9,8},{10,11... | collective-permute-start | bytes 1179656 | tf_op jit(solution)/shard_map/ppermute | solution.py:402
  38.9 12.0 %copy-start.12 = (bf16[4,128,384]{2,1,0:T(8,128)(2,1)}, bf16[4,128,384]{2,1,0:T(8,128)(2,1)S(1)}, u32[]{:S(2)}) copy-start(bf16[4,128,384]{2,1,0:T(8,128)(2,1)S(1)} %collective-permute-done.6.refs_7_) | copy-start | bytes 1179652
  38.9 11.8 %collective-permute-start.11 = (bf16[4,128,384]{2,1,0:T(8,128)(2,1)S(1)}, bf16[4,128,384]{2,1,0:T(8,128)(2,1)}, u32[]{:S(2)}, u32[]{:S(2)}) collective-permute-start(bf16[4,128,384]{2,1,0:T(8,128)(2,1)S(1)} %collective-permute-done.6.refs_7_), channel_id=1, source_target_pairs={{0,1},{1,0},{2,3},{3,2},{4,5},{5,4},{6,7},{7,6},{8,9},{9,8},{10,11... | collective-permute-start | bytes 1179656 | tf_op jit(solution)/shard_map/ppermute | solution.py:402
  39.1 34.1 %copy-start.5 = (bf16[4,112,384]{2,1,0:T(8,128)(2,1)}, bf16[4,112,384]{2,1,0:T(8,128)(2,1)S(1)}, u32[]{:S(2)}) copy-start(bf16[4,112,384]{2,1,0:T(8,128)(2,1)S(1)} %get-tuple-element.59.refs_7_) | copy-start | bytes 1032196
  39.1 10.5 %collective-permute-start.17 = (bf16[4,112,384]{2,1,0:T(8,128)(2,1)S(1)}, bf16[4,112,384]{2,1,0:T(8,128)(2,1)S(1)}, u32[]{:S(2)}, u32[]{:S(2)}) collective-permute-start(bf16[4,112,384]{2,1,0:T(8,128)(2,1)S(1)} %get-tuple-element.60), channel_id=1, source_target_pairs={{0,4},{1,5},{2,6},{3,7},{4,0},{5,1},{6,2},{7,3},{8,12},{9,13},{10,... | collective-permute-start | bytes 1032200 | tf_op jit(solution)/shard_map/ppermute | solution.py:402
  40.0 9.8 %collective-permute-start.18 = (bf16[4,112,384]{2,1,0:T(8,128)(2,1)S(1)}, bf16[4,112,384]{2,1,0:T(8,128)(2,1)S(1)}, u32[]{:S(2)}, u32[]{:S(2)}) collective-permute-start(bf16[4,112,384]{2,1,0:T(8,128)(2,1)S(1)} %get-tuple-element.58), channel_id=1, source_target_pairs={{0,2},{1,3},{2,0},{3,1},{4,6},{5,7},{6,4},{7,5},{8,10},{9,11},{10,... | collective-permute-start | bytes 1032200 | tf_op jit(solution)/shard_map/ppermute | solution.py:402
  49.6 23.6 %copy-start.13 = (bf16[4,112,384]{2,1,0:T(8,128)(2,1)}, bf16[4,112,384]{2,1,0:T(8,128)(2,1)S(1)}, u32[]{:S(2)}) copy-start(bf16[4,112,384]{2,1,0:T(8,128)(2,1)S(1)} %collective-permute-done.17.refs_10_) | copy-start | bytes 1032196
  49.6 23.7 %collective-permute-start.19 = (bf16[4,112,384]{2,1,0:T(8,128)(2,1)S(1)}, bf16[4,112,384]{2,1,0:T(8,128)(2,1)S(1)}, u32[]{:S(2)}, u32[]{:S(2)}) collective-permute-start(bf16[4,112,384]{2,1,0:T(8,128)(2,1)S(1)} %get-tuple-element.59.refs_7_), channel_id=1, source_target_pairs={{0,1},{1,0},{2,3},{3,2},{4,5},{5,4},{6,7},{7,6},{8,9},{9,8},{10,11... | collective-permute-start | bytes 1032200 | tf_op jit(solution)/shard_map/ppermute | solution.py:402
  49.8 23.4 %copy-start.14 = (bf16[4,112,384]{2,1,0:T(8,128)(2,1)}, bf16[4,112,384]{2,1,0:T(8,128)(2,1)S(1)}, u32[]{:S(2)}) copy-start(bf16[4,112,384]{2,1,0:T(8,128)(2,1)S(1)} %collective-permute-done.18.refs_11_) | copy-start | bytes 1032196
  49.8 23.4 %collective-permute-start.21 = (bf16[2,112,384]{2,1,0:T(8,128)(2,1)S(1)}, bf16[2,112,384]{2,1,0:T(8,128)(2,1)S(1)}, u32[]{:S(2)}, u32[]{:S(2)}) collective-permute-start(bf16[2,112,384]{2,1,0:T(8,128)(2,1)S(1)} %collective-permute-done.16.refs_9_), channel_id=1, source_target_pairs={{0,1},{1,0},{2,3},{3,2},{4,5},{5,4},{6,7},{7,6},{8,9},{9,8},{10,11... | collective-permute-start | bytes 516104 | tf_op jit(solution)/shard_map/ppermute | solution.py:402
  50.1 23.1 %collective-permute-start.20 = (bf16[2,112,384]{2,1,0:T(8,128)(2,1)S(1)}, bf16[2,112,384]{2,1,0:T(8,128)(2,1)S(1)}, u32[]{:S(2)}, u32[]{:S(2)}) collective-permute-start(bf16[2,112,384]{2,1,0:T(8,128)(2,1)S(1)} %collective-permute-done.15.refs_8_), channel_id=1, source_target_pairs={{0,1},{1,0},{2,3},{3,2},{4,5},{5,4},{6,7},{7,6},{8,9},{9,8},{10,11... | collective-permute-start | bytes 516104 | tf_op jit(solution)/shard_map/ppermute | solution.py:402
  50.3 23.0 %collective-permute-start.22 = (bf16[4,112,384]{2,1,0:T(8,128)(2,1)S(1)}, bf16[4,112,384]{2,1,0:T(8,128)(2,1)S(1)}, u32[]{:S(2)}, u32[]{:S(2)}) collective-permute-start(bf16[4,112,384]{2,1,0:T(8,128)(2,1)S(1)} %collective-permute-done.17.refs_10_), channel_id=1, source_target_pairs={{0,1},{1,0},{2,3},{3,2},{4,5},{5,4},{6,7},{7,6},{8,9},{9,8},{10,11... | collective-permute-start | bytes 1032200 | tf_op jit(solution)/shard_map/ppermute | solution.py:402
  50.6 22.7 %collective-permute-start.23 = (bf16[4,112,384]{2,1,0:T(8,128)(2,1)S(1)}, bf16[4,112,384]{2,1,0:T(8,128)(2,1)S(1)}, u32[]{:S(2)}, u32[]{:S(2)}) collective-permute-start(bf16[4,112,384]{2,1,0:T(8,128)(2,1)S(1)} %collective-permute-done.18.refs_11_), channel_id=1, source_target_pairs={{0,1},{1,0},{2,3},{3,2},{4,5},{5,4},{6,7},{7,6},{8,9},{9,8},{10,11... | collective-permute-start | bytes 1032200 | tf_op jit(solution)/shard_map/ppermute | solution.py:402
  73.3 0.7 copy-start.18
  73.3 0.7 copy-start.19
  73.3 0.8 copy-start.15
  73.3 0.9 copy-start.16
  73.3 1.0 copy-start.17
  101.9 43.2 %collective-permute-start.37 = (bf16[8,112,384]{2,1,0:T(8,128)(2,1)}, bf16[8,112,384]{2,1,0:T(8,128)(2,1)S(1)}, u32[]{:S(2)}, u32[]{:S(2)}) collective-permute-start(bf16[8,112,384]{2,1,0:T(8,128)(2,1)} %get-tuple-element.50), channel_id=1, source_target_pairs={{0,1},{1,0},{2,3},{3,2},{4,5},{5,4},{6,7},{7,6},{8,9},{9,8},{10,11... | collective-permute-start | bytes 2064392 | tf_op jit(solution)/shard_map/ppermute | solution.py:402
  116.6 38.6 %collective-permute-start.33 = (bf16[8,112,384]{2,1,0:T(8,128)(2,1)}, bf16[8,112,384]{2,1,0:T(8,128)(2,1)S(1)}, u32[]{:S(2)}, u32[]{:S(2)}) collective-permute-start(bf16[8,112,384]{2,1,0:T(8,128)(2,1)} %get-tuple-element.48), channel_id=1, source_target_pairs={{0,1},{1,0},{2,3},{3,2},{4,5},{5,4},{6,7},{7,6},{8,9},{9,8},{10,11... | collective-permute-start | bytes 2064392 | tf_op jit(solution)/shard_map/ppermute | solution.py:402
  116.7 28.5 %copy-start.3 = (f32[8,112,384]{2,1,0:T(8,128)S(1)}, f32[8,112,384]{2,1,0:T(8,128)}, u32[]{:S(2)}) copy-start(f32[8,112,384]{2,1,0:T(8,128)} %get-tuple-element.49) | copy-start | bytes 4128772
  140.3 16.1 %collective-permute-start.28 = (bf16[8,128,384]{2,1,0:T(8,128)(2,1)}, bf16[8,128,384]{2,1,0:T(8,128)(2,1)S(1)}, u32[]{:S(2)}, u32[]{:S(2)}) collective-permute-start(bf16[8,128,384]{2,1,0:T(8,128)(2,1)} %get-tuple-element.46), channel_id=1, source_target_pairs={{0,1},{1,0},{2,3},{3,2},{4,5},{5,4},{6,7},{7,6},{8,9},{9,8},{10,11... | collective-permute-start | bytes 2359304 | tf_op jit(solution)/shard_map/ppermute | solution.py:402
  145.1 12.9 %collective-permute-start.24 = (bf16[8,128,384]{2,1,0:T(8,128)(2,1)}, bf16[8,128,384]{2,1,0:T(8,128)(2,1)S(1)}, u32[]{:S(2)}, u32[]{:S(2)}) collective-permute-start(bf16[8,128,384]{2,1,0:T(8,128)(2,1)} %get-tuple-element.44), channel_id=1, source_target_pairs={{0,1},{1,0},{2,3},{3,2},{4,5},{5,4},{6,7},{7,6},{8,9},{9,8},{10,11... | collective-permute-start | bytes 2359304 | tf_op jit(solution)/shard_map/ppermute | solution.py:402
  145.2 10.1 %copy-start.2 = (f32[8,112,384]{2,1,0:T(8,128)S(1)}, f32[8,112,384]{2,1,0:T(8,128)}, u32[]{:S(2)}) copy-start(f32[8,112,384]{2,1,0:T(8,128)} %get-tuple-element.47) | copy-start | bytes 4128772
  145.4 18.8 %collective-permute-start.38 = (bf16[4,112,384]{2,1,0:T(8,128)(2,1)S(1)}, bf16[4,112,384]{2,1,0:T(8,128)(2,1)S(1)}, u32[]{:S(2)}, u32[]{:S(2)}) collective-permute-start(bf16[4,112,384]{2,1,0:T(8,128)(2,1)S(1)} %slice.200), channel_id=1, source_target_pairs={{0,4},{1,5},{2,6},{3,7},{4,0},{5,1},{6,2},{7,3},{8,12},{9,13},{10,... | collective-permute-start | bytes 1032200 | tf_op jit(solution)/shard_map/ppermute | solution.py:402
  155.2 1.4 copy-start.1
  155.4 11.0 %collective-permute-start.34 = (bf16[4,112,384]{2,1,0:T(8,128)(2,1)S(1)}, bf16[4,112,384]{2,1,0:T(8,128)(2,1)S(1)}, u32[]{:S(2)}, u32[]{:S(2)}) collective-permute-start(bf16[4,112,384]{2,1,0:T(8,128)(2,1)S(1)} %slice.201), channel_id=1, source_target_pairs={{0,2},{1,3},{2,0},{3,1},{4,6},{5,7},{6,4},{7,5},{8,10},{9,11},{10,... | collective-permute-start | bytes 1032200 | tf_op jit(solution)/shard_map/ppermute | solution.py:402
  156.6 1.4 copy-start
  156.8 15.7 %collective-permute-start.29 = (bf16[4,128,384]{2,1,0:T(8,128)(2,1)S(1)}, bf16[4,128,384]{2,1,0:T(8,128)(2,1)S(1)}, u32[]{:S(2)}, u32[]{:S(2)}) collective-permute-start(bf16[4,128,384]{2,1,0:T(8,128)(2,1)S(1)} %slice.198), channel_id=1, source_target_pairs={{0,4},{1,5},{2,6},{3,7},{4,0},{5,1},{6,2},{7,3},{8,12},{9,13},{10,... | collective-permute-start | bytes 1179656 | tf_op jit(solution)/shard_map/ppermute | solution.py:402
  158.2 16.6 %collective-permute-start.25 = (bf16[4,128,384]{2,1,0:T(8,128)(2,1)S(1)}, bf16[4,128,384]{2,1,0:T(8,128)(2,1)S(1)}, u32[]{:S(2)}, u32[]{:S(2)}) collective-permute-start(bf16[4,128,384]{2,1,0:T(8,128)(2,1)S(1)} %slice.199), channel_id=1, source_target_pairs={{0,2},{1,3},{2,0},{3,1},{4,6},{5,7},{6,4},{7,5},{8,10},{9,11},{10,... | collective-permute-start | bytes 1179656 | tf_op jit(solution)/shard_map/ppermute | solution.py:402
  164.2 14.3 %collective-permute-start.39 = (bf16[2,112,384]{2,1,0:T(8,128)(2,1)S(1)}, bf16[2,112,384]{2,1,0:T(8,128)(2,1)S(1)}, u32[]{:S(2)}, u32[]{:S(2)}) collective-permute-start(bf16[2,112,384]{2,1,0:T(8,128)(2,1)S(1)} %fusion.11), channel_id=1, source_target_pairs={{0,2},{1,3},{2,0},{3,1},{4,6},{5,7},{6,4},{7,5},{8,10},{9,11},{10,... | collective-permute-start | bytes 516104 | tf_op jit(solution)/shard_map/ppermute | solution.py:402
  166.5 15.2 %collective-permute-start.35 = (bf16[2,112,384]{2,1,0:T(8,128)(2,1)S(1)}, bf16[2,112,384]{2,1,0:T(8,128)(2,1)S(1)}, u32[]{:S(2)}, u32[]{:S(2)}) collective-permute-start(bf16[2,112,384]{2,1,0:T(8,128)(2,1)S(1)} %fusion.12), channel_id=1, source_target_pairs={{0,4},{1,5},{2,6},{3,7},{4,0},{5,1},{6,2},{7,3},{8,12},{9,13},{10,... | collective-permute-start | bytes 516104 | tf_op jit(solution)/shard_map/ppermute | solution.py:402
  172.7 10.0 %collective-permute-start.30 = (bf16[2,128,384]{2,1,0:T(8,128)(2,1)S(1)}, bf16[2,128,384]{2,1,0:T(8,128)(2,1)S(1)}, u32[]{:S(2)}, u32[]{:S(2)}) collective-permute-start(bf16[2,128,384]{2,1,0:T(8,128)(2,1)S(1)} %fusion.6), channel_id=1, source_target_pairs={{0,2},{1,3},{2,0},{3,1},{4,6},{5,7},{6,4},{7,5},{8,10},{9,11},{10,... | collective-permute-start | bytes 589832 | tf_op jit(solution)/shard_map/ppermute | solution.py:402
  175.0 9.4 %collective-permute-start.26 = (bf16[2,128,384]{2,1,0:T(8,128)(2,1)S(1)}, bf16[2,128,384]{2,1,0:T(8,128)(2,1)S(1)}, u32[]{:S(2)}, u32[]{:S(2)}) collective-permute-start(bf16[2,128,384]{2,1,0:T(8,128)(2,1)S(1)} %fusion.7), channel_id=1, source_target_pairs={{0,4},{1,5},{2,6},{3,7},{4,0},{5,1},{6,2},{7,3},{8,12},{9,13},{10,... | collective-permute-start | bytes 589832 | tf_op jit(solution)/shard_map/ppermute | solution.py:402
  178.6 10.2 %collective-permute-start.40 = (bf16[112,384]{1,0:T(8,128)(2,1)S(1)}, bf16[112,384]{1,0:T(8,128)(2,1)S(1)}, u32[]{:S(2)}, u32[]{:S(2)}) collective-permute-start(bf16[112,384]{1,0:T(8,128)(2,1)S(1)} %get-tuple-element.56), channel_id=1, source_target_pairs={{0,16},{1,17},{2,18},{3,19},{4,20},{5,21},{6,22},{7,23},{8,24},{9,... | collective-permute-start | bytes 258056 | tf_op jit(solution)/shard_map/ppermute | solution.py:402
  180.6 8.2 %collective-permute-start.41 = (bf16[112,384]{1,0:T(8,128)(2,1)S(1)}, bf16[112,384]{1,0:T(8,128)(2,1)S(1)}, u32[]{:S(2)}, u32[]{:S(2)}) collective-permute-start(bf16[112,384]{1,0:T(8,128)(2,1)S(1)} %get-tuple-element.57), channel_id=1, source_target_pairs={{0,24},{1,25},{2,26},{3,27},{4,28},{5,29},{6,30},{7,31},{8,0},{9,1... | collective-permute-start | bytes 258056 | tf_op jit(solution)/shard_map/ppermute | solution.py:402
  181.7 7.3 %collective-permute-start.36 = (bf16[112,384]{1,0:T(8,128)(2,1)S(1)}, bf16[112,384]{1,0:T(8,128)(2,1)S(1)}, u32[]{:S(2)}, u32[]{:S(2)}) collective-permute-start(bf16[112,384]{1,0:T(8,128)(2,1)S(1)} %fusion.17), channel_id=1, source_target_pairs={{0,8},{1,9},{2,10},{3,11},{4,12},{5,13},{6,14},{7,15},{8,16},{9,17... | collective-permute-start | bytes 258056 | tf_op jit(solution)/shard_map/ppermute | solution.py:402
  182.8 11.5 %collective-permute-start.31 = (bf16[128,384]{1,0:T(8,128)(2,1)S(1)}, bf16[128,384]{1,0:T(8,128)(2,1)S(1)}, u32[]{:S(2)}, u32[]{:S(2)}) collective-permute-start(bf16[128,384]{1,0:T(8,128)(2,1)S(1)} %get-tuple-element.51), channel_id=1, source_target_pairs={{0,16},{1,17},{2,18},{3,19},{4,20},{5,21},{6,22},{7,23},{8,24},{9,... | collective-permute-start | bytes 294920 | tf_op jit(solution)/shard_map/ppermute | solution.py:402
  184.3 10.0 %collective-permute-start.32 = (bf16[128,384]{1,0:T(8,128)(2,1)S(1)}, bf16[128,384]{1,0:T(8,128)(2,1)S(1)}, u32[]{:S(2)}, u32[]{:S(2)}) collective-permute-start(bf16[128,384]{1,0:T(8,128)(2,1)S(1)} %get-tuple-element.52), channel_id=1, source_target_pairs={{0,24},{1,25},{2,26},{3,27},{4,28},{5,29},{6,30},{7,31},{8,0},{9,1... | collective-permute-start | bytes 294920 | tf_op jit(solution)/shard_map/ppermute | solution.py:402
  188.8 6.8 %collective-permute-start.27 = (bf16[128,384]{1,0:T(8,128)(2,1)S(1)}, bf16[128,384]{1,0:T(8,128)(2,1)S(1)}, u32[]{:S(2)}, u32[]{:S(2)}) collective-permute-start(bf16[128,384]{1,0:T(8,128)(2,1)S(1)} %fusion.16), channel_id=1, source_target_pairs={{0,8},{1,9},{2,10},{3,11},{4,12},{5,13},{6,14},{7,15},{8,16},{9,17... | collective-permute-start | bytes 294920 | tf_op jit(solution)/shard_map/ppermute | solution.py:402

commit v2 on v1

--- a/solution.py
+++ b/solution.py
@@ -17,6 +17,8 @@
 FACTOR = HEAD_DIM ** (-0.5)
 GELU_A = 0.7978845608028654
 GELU_B = 0.044715
+CHUNK = 512
+PER_STEP = 2
 
 ADA_AT = 0
 QKV_AT = 6 * D
@@ -74,6 +76,20 @@
     return rstd * (grad - row_mean(grad) - normed * row_mean(grad * normed))
 
 
+def flat(values):
+    return values.reshape(-1, values.shape[-1])
+
+
+def mod_rows(mod_ref, part, step, group):
+    rows = [mod_ref[part, pl.ds(step * group + latent, 1), :] for latent in range(group)]
+    return jnp.stack(rows)
+
+
+def put_mod(ref, part, step, values):
+    for latent in range(values.shape[0]):
+        ref[part, pl.ds(step * values.shape[0] + latent, 1), :] = col_sum(values[latent])
+
+
 def head_masks():
     lane = lax.broadcasted_iota(jnp.int32, (1, LANES), 1) // HEAD_DIM
     return [(lane == head).astype(F32).astype(BF16) for head in range(2)]
@@ -121,57 +137,59 @@
     mod_ref, ada_ref, qkv_w_ref, proj_ref, bias_ref, qkv_ref, probs_ref, mixed_ref, branch_ref = refs[
         n_pieces : n_pieces + 9
     ]
-    rows_ref = refs[n_pieces + 9]
+    rows_ref, score_ref = refs[n_pieces + 9 :]
     step = pl.program_id(0)
+    group, seq = x_ref.shape[0], x_ref.shape[1]
 
     @pl.when(step == 0)
     def _():
         assemble(scal_ref, 1, pieces, rows_ref)
-        for block in range(6):
-            for tile in range(TILES):
+        for tile in range(TILES):
+            proj_ref[:, lanes_of(tile)] = rows_ref[tile, pl.ds(PROJ_AT, D), :].astype(BF16)
+            bias_ref[:, lanes_of(tile)] = rows_ref[tile, pl.ds(B_ADA_AT, 8), :]
+            for block in range(6):
                 ada_ref[block, :, lanes_of(tile)] = rows_ref[
                     tile, pl.ds(ADA_AT + block, D, stride=6), :
                 ].astype(BF16)
-        for block in range(3):
-            for tile in range(TILES):
+            for block in range(3):
                 qkv_w_ref[:, lanes_of(tile, block * D)] = rows_ref[
                     tile, pl.ds(QKV_AT + block, D, stride=3), :
                 ].astype(BF16)
-        for tile in range(TILES):
-            proj_ref[:, lanes_of(tile)] = rows_ref[tile, pl.ds(PROJ_AT, D), :].astype(BF16)
-            bias_ref[:, lanes_of(tile)] = rows_ref[tile, pl.ds(B_ADA_AT, 8), :]
         act = jax.nn.silu(cond_ref[...].astype(F32)).astype(BF16)
         for block in range(6):
-            mod_ref[block] = mm(act, ada_ref[block]) + bias_ref[pl.ds(block, 1), :]
-
-    @pl.when(step < scal_ref[0])
+            mod_ref[block] = mm(act, ada_ref[block]) + bias_ref[block : block + 1, :]
+
+    @pl.when(step * group < scal_ref[0])
     def _():
         masks = head_masks()
-        values = x_ref[0].astype(F32)
+        values = x_ref[...].astype(F32)
         normed, _ = normalize(values)
-        shift = mod_ref[0, pl.ds(step, 1), :]
-        scale = mod_ref[1, pl.ds(step, 1), :]
-        modulated = (normed * (1.0 + scale) + shift).astype(BF16)
+        shift, scale = [mod_rows(mod_ref, part, step, group) for part in range(2)]
+        modulated = flat(normed * (1.0 + scale) + shift).astype(BF16)
         qkv = mm(modulated, qkv_w_ref[...])
         queries = (qkv[:, :D] + bias_ref[6:7, :]).astype(BF16)
         keys_all = qkv[:, D : 2 * D].astype(BF16)
         values_all = (qkv[:, 2 * D :] + bias_ref[7:8, :]).astype(BF16)
-        qkv_ref[0, :, :D] = queries
-        qkv_ref[0, :, D : 2 * D] = keys_all
-        qkv_ref[0, :, 2 * D :] = values_all
-        values_t = values_all.T
-        for pair in range(HEADS // 2):
-            lanes = lanes_of(pair)
-            query, key = queries[:, lanes], keys_all[:, lanes]
-            for half in range(2):
-                head = 2 * pair + half
-                scores = mm_nt(key, query * masks[half]) * FACTOR
+        for latent in range(group):
+            tokens = slice(latent * seq, (latent + 1) * seq)
+            qkv_ref[latent, :, :D] = queries[tokens]
+            qkv_ref[latent, :, D : 2 * D] = keys_all[tokens]
+            qkv_ref[latent, :, 2 * D :] = values_all[tokens]
+            for head in range(HEADS):
+                lanes = lanes_of(head // 2)
+                own = queries[tokens, lanes] * (masks[head % 2] * FACTOR)
+                score_ref[latent, head] = mm_nt(keys_all[tokens, lanes], own)
+        for latent in range(group):
+            tokens = slice(latent * seq, (latent + 1) * seq)
+            values_t = values_all[tokens].T
+            for head in range(HEADS):
+                scores = score_ref[latent, head]
                 expo = jnp.exp(scores - jnp.max(scores, axis=0, keepdims=True))
-                probs = expo * (1.0 / col_sum(expo))
-                probs_ref[0, head] = probs
+                probs_ref[latent, head] = (expo * (1.0 / col_sum(expo))).astype(BF16)
+            for head in range(HEADS):
                 rows = slice(head * HEAD_DIM, (head + 1) * HEAD_DIM)
-                mixed_ref[0, rows, :] = mm(values_t[rows, :], probs.astype(BF16)).astype(BF16)
-        branch_ref[0] = mm_tn(mixed_ref[0], proj_ref[...])
+                mixed_ref[latent, rows, :] = mm(values_t[rows, :], probs_ref[latent, head]).astype(BF16)
+            branch_ref[latent] = mm_tn(mixed_ref[latent], proj_ref[...])
 
 
 def mlp_kernel(n_pieces, n_out, scal_ref, mod_ref, proj_ref, x_ref, branch_ref, mixed_ref, cot_ref, *refs):
@@ -204,56 +222,62 @@
         dproj_ref[...] = jnp.zeros_like(dproj_ref)
         dmod_ref[...] = jnp.zeros_like(dmod_ref)
 
-    @pl.when(step < scal_ref[0])
-    def _():
-        row = pl.ds(step, 1)
-        gate_one, shift, scale, gate_two = [mod_ref[2 + part, row, :] for part in range(4)]
-        branch_one = branch_ref[0] + bias_ref[2:3, :D]
-        middle = x_ref[0].astype(F32) + gate_one * branch_one
+    group, seq = x_ref.shape[0], x_ref.shape[1]
+
+    @pl.when(step * group < scal_ref[0])
+    def _():
+        gate_one, shift, scale, gate_two = [mod_rows(mod_ref, 2 + part, step, group) for part in range(4)]
+        slot = step * group + lax.broadcasted_iota(jnp.int32, (group, 1, 1), 0)
+        live = (slot < scal_ref[0]).astype(F32)
+        branch_one = branch_ref[...] + bias_ref[2:3, :D]
+        middle = x_ref[...].astype(F32) + gate_one * branch_one
         normed, rstd = normalize(middle)
-        modulated = (normed * (1.0 + scale) + shift).astype(BF16)
-        chunk = 512
-        branch_two = jnp.zeros_like(middle)
+        modulated = flat(normed * (1.0 + scale) + shift).astype(BF16)
+        chunk = CHUNK
+        branch_two = jnp.zeros((group * seq, D), F32)
         for start in range(0, FF, chunk):
             part = slice(start, start + chunk)
             pre = mm(modulated, fc1_ref[:, part]) + bias_ref[0:1, part]
             square = pre * pre
-            bend = jnp.tanh(GELU_A * pre * (1.0 + GELU_B * square))
-            half = 0.5 * (1.0 + bend)
+            bend = jnp.tanh(pre * (GELU_A + (GELU_A * GELU_B) * square))
+            half = 0.5 + 0.5 * bend
             act = (pre * half).astype(BF16)
             act_ref[:, part] = act
-            slope_ref[:, part] = half + (0.5 * GELU_A) * pre * (1.0 - bend * bend) * (
-                1.0 + (3.0 * GELU_B) * square
+            slope_ref[:, part] = half + (pre * (0.5 - 0.5 * bend * bend)) * (
+                GELU_A + (3.0 * GELU_A * GELU_B) * square
             )
             branch_two += mm(act, fc2_ref[part, :])
-        branch_two += bias_ref[1:2, :D]
-        out_ref[0] = (middle + gate_two * branch_two).astype(BF16)
-        grad_out = cot_ref[0].astype(F32)
-        dmod_ref[3, row, :] = col_sum(grad_out * branch_two)
-        grad_two = gate_two * grad_out
-        grad_two_low = grad_two.astype(BF16)
-        dbias_ref[1:2, :D] += col_sum(grad_two_low.astype(F32))
-        grad_two_t = grad_two_low.T
+        branch_two = (branch_two + bias_ref[1:2, :D]).reshape(group, seq, D)
+        out_ref[...] = (live * (middle + gate_two * branch_two)).astype(BF16)
+        grad_out = live * cot_ref[...].astype(F32)
+        put_mod(dmod_ref, 3, step, grad_out * branch_two)
+        grad_two = flat(gate_two * grad_out).astype(BF16)
+        dbias_ref[1:2, :D] += col_sum(grad_two.astype(F32))
+        grad_two_t = grad_two.T
         modulated_t = modulated.T
-        grad_mod = jnp.zeros_like(middle)
+        grad_mod = jnp.zeros((group * seq, D), F32)
         for start in range(0, FF, chunk):
             part = slice(start, start + chunk)
-            du = (mm_nt(grad_two_low, fc2_ref[part, :]) * slope_ref[:, part]).astype(BF16)
+            du = (mm_nt(grad_two, fc2_ref[part, :]) * slope_ref[:, part]).astype(BF16)
             dbias_ref[0:1, part] += col_sum(du.astype(F32))
             dfc2_ref[:, part] += mm(grad_two_t, act_ref[:, part])
             dfc1_ref[:, part] += mm(modulated_t, du)
             grad_mod += mm_nt(du, fc1_ref[:, part])
-        dmod_ref[1, row, :] = col_sum(grad_mod)
-        dmod_ref[2, row, :] = col_sum(grad_mod * normed)
+        grad_mod = grad_mod.reshape(group, seq, D)
+        put_mod(dmod_ref, 1, step, grad_mod)
+        put_mod(dmod_ref, 2, step, grad_mod * normed)
         grad_middle = grad_out + normalize_back(grad_mod * (1.0 + scale), normed, rstd)
-        dx_ref[0] = grad_middle
-        dmod_ref[0, row, :] = col_sum(grad_middle * branch_one)
-        grad_one = (gate_one * grad_middle).astype(BF16)
+        dx_ref[...] = grad_middle
+        put_mod(dmod_ref, 0, step, grad_middle * branch_one)
+        grad_one = flat(gate_one * grad_middle).astype(BF16)
         dbias_ref[2:3, :D] += col_sum(grad_one.astype(F32))
-        dproj_ref[...] += mm(mixed_ref[0], grad_one)
-        dmixed_ref[0] = mm_nt(grad_one, proj_ref[...]).astype(BF16)
-
-    @pl.when(step >= scal_ref[0])
+        grad_mixed = mm_nt(grad_one, proj_ref[...]).astype(BF16)
+        for latent in range(group):
+            tokens = slice(latent * seq, (latent + 1) * seq)
+            dproj_ref[...] += mm(mixed_ref[latent], grad_one[tokens])
+            dmixed_ref[latent] = grad_mixed[tokens]
+
+    @pl.when(step * group >= scal_ref[0])
     def _():
         out_ref[...] = jnp.zeros_like(out_ref)
         dx_ref[...] = jnp.zeros_like(dx_ref)
@@ -274,15 +298,46 @@
         emit(scal_ref, 1 + sum(ref.shape[0] for ref in pieces), send_refs, rows_ref)
 
 
-def backward_kernel(
-    n_out, base, scal_ref, cond_ref, mod_ref, ada_ref, qkv_w_ref, dmod_in_ref, dproj_ref,
-    x_ref, qkv_ref, probs_ref, dx_ref, dmixed_ref, *refs
+def attend_back_kernel(scal_ref, qkv_ref, probs_ref, dmixed_ref, dqkv_ref, dprobs_ref, low_ref, dq_t_ref):
+    group, seq = qkv_ref.shape[0], qkv_ref.shape[1]
+
+    @pl.when(pl.program_id(0) * group < scal_ref[0])
+    def _():
+        masks = head_masks()
+        for latent in range(group):
+            keys_t = qkv_ref[latent, :, D : 2 * D].T
+            for head in range(HEADS):
+                own = dmixed_ref[latent, :, lanes_of(head // 2)] * masks[head % 2]
+                dprobs_ref[head] = mm_nt(qkv_ref[latent, :, lanes_of(head // 2, 2 * D)], own)
+            for head in range(HEADS):
+                probs, grad_probs = probs_ref[latent, head].astype(F32), dprobs_ref[head]
+                low_ref[head] = (probs * (grad_probs - col_sum(probs * grad_probs))).astype(BF16)
+            for pair in range(HEADS // 2):
+                query = qkv_ref[latent, :, lanes_of(pair)]
+                grad = dmixed_ref[latent, :, lanes_of(pair)]
+                grad_key = jnp.zeros((seq, LANES), F32)
+                grad_value = jnp.zeros((seq, LANES), F32)
+                for half in range(2):
+                    head = 2 * pair + half
+                    rows = slice(head * HEAD_DIM, (head + 1) * HEAD_DIM)
+                    grad_value += mm(probs_ref[latent, head], grad * masks[half])
+                    grad_key += mm(low_ref[head], query * masks[half])
+                    dq_t_ref[rows, :] = mm(keys_t[rows, :], low_ref[head])
+                dqkv_ref[latent, :, lanes_of(pair, D)] = (grad_key * FACTOR).astype(BF16)
+                dqkv_ref[latent, :, lanes_of(pair, 2 * D)] = grad_value.astype(BF16)
+            dqkv_ref[latent, :, :D] = (dq_t_ref[...] * FACTOR).astype(BF16).T
+
+
+def finish_kernel(
+    n_out, base, scal_ref, mod_ref, qkv_w_ref, cond_ref, ada_ref, dmod_in_ref, dproj_ref,
+    x_ref, dqkv_ref, dx_ref, *refs
 ):
     grad_x_ref, grad_cond_ref = refs[:2]
     send_refs = refs[2 : 2 + n_out]
-    rows_ref, dqkv_w_ref, dmod_ref, dbias_ref, dqkv_ref, dq_t_ref = refs[2 + n_out :]
+    rows_ref, dqkv_w_ref, dmod_ref, dbias_ref = refs[2 + n_out :]
     step = pl.program_id(0)
     last = pl.num_programs(0) - 1
+    group, seq = x_ref.shape[0], x_ref.shape[1]
 
     @pl.when(step == 0)
     def _():
@@ -290,44 +345,20 @@
         dmod_ref[...] = jnp.zeros_like(dmod_ref)
         dbias_ref[...] = jnp.zeros_like(dbias_ref)
 
-    @pl.when(step < scal_ref[0])
-    def _():
-        masks = head_masks()
-        row = pl.ds(step, 1)
-        shift = mod_ref[0, row, :]
-        scale = mod_ref[1, row, :]
-        normed, rstd = normalize(x_ref[0].astype(F32))
-        modulated = (normed * (1.0 + scale) + shift).astype(BF16)
-        keys_t = qkv_ref[0, :, D : 2 * D].T
-        for pair in range(HEADS // 2):
-            query = qkv_ref[0, :, lanes_of(pair)]
-            value = qkv_ref[0, :, lanes_of(pair, 2 * D)]
-            grad = dmixed_ref[0, :, lanes_of(pair)]
-            grad_key = jnp.zeros((query.shape[0], LANES), F32)
-            grad_value = jnp.zeros((query.shape[0], LANES), F32)
-            for half in range(2):
-                head = 2 * pair + half
-                rows = slice(head * HEAD_DIM, (head + 1) * HEAD_DIM)
-                query_own = query * masks[half]
-                grad_own = grad * masks[half]
-                probs = probs_ref[0, head]
-                grad_value += mm(probs.astype(BF16), grad_own)
-                grad_probs = mm_nt(value, grad_own)
-                grad_scores = (probs * (grad_probs - col_sum(probs * grad_probs))).astype(BF16)
-                grad_key += mm(grad_scores, query_own)
-                dq_t_ref[rows, :] = mm(keys_t[rows, :], grad_scores)
-            dqkv_ref[:, lanes_of(pair, D)] = (grad_key * FACTOR).astype(BF16)
-            dqkv_ref[:, lanes_of(pair, 2 * D)] = grad_value.astype(BF16)
-        dqkv_ref[:, :D] = (dq_t_ref[...] * FACTOR).astype(BF16).T
-        grad_qkv = dqkv_ref[...]
+    @pl.when(step * group < scal_ref[0])
+    def _():
+        shift, scale = [mod_rows(mod_ref, part, step, group) for part in range(2)]
+        normed, rstd = normalize(x_ref[...].astype(F32))
+        modulated = flat(normed * (1.0 + scale) + shift).astype(BF16)
+        grad_qkv = flat(dqkv_ref[...])
         dbias_ref[0:1, :] += col_sum(grad_qkv.astype(F32))
         dqkv_w_ref[...] += mm(modulated.T, grad_qkv)
-        grad_mod = mm_nt(grad_qkv, qkv_w_ref[...])
-        dmod_ref[0, row, :] = col_sum(grad_mod)
-        dmod_ref[1, row, :] = col_sum(grad_mod * normed)
-        grad_x_ref[0] = dx_ref[0] + normalize_back(grad_mod * (1.0 + scale), normed, rstd)
-
-    @pl.when(step >= scal_ref[0])
+        grad_mod = mm_nt(grad_qkv, qkv_w_ref[...]).reshape(group, seq, D)
+        put_mod(dmod_ref, 0, step, grad_mod)
+        put_mod(dmod_ref, 1, step, grad_mod * normed)
+        grad_x_ref[...] = dx_ref[...] + normalize_back(grad_mod * (1.0 + scale), normed, rstd)
+
+    @pl.when(step * group >= scal_ref[0])
     def _():
         grad_x_ref[...] = jnp.zeros_like(grad_x_ref)
 
@@ -366,7 +397,15 @@
     def gather(self, piece):
         return [lax.all_gather(piece, AXIS, axis=0)]
 
-    def scatter(self, parts):
+    def pass_on(self, held):
+        return held
+
+    def begin(self, parts):
+        return parts
+
+    middle = send = begin
+
+    def end(self, parts):
         return lax.psum_scatter(parts[0], AXIS, scatter_dimension=0)
 
 
@@ -408,23 +447,38 @@
         by_y = self.shift(second, dy=1)
         by_xy = self.shift(jnp.concatenate([first, by_x]), dy=1)
         by_yx = self.shift(jnp.concatenate([second, by_y]), dx=1)
-        held = [own, by_x, by_y, by_xy, by_yx]
+        return [own, by_x, by_y, by_xy, by_yx]
+
+    def pass_on(self, held):
         return held + [self.shift(array, dc=1) for array in held]
 
-    def scatter(self, parts):
-        def send(values, **how):
+    def begin(self, parts):
+        send_a, send_b, keep_a, keep_b = parts
+        return self.shift(send_a, dc=1), self.shift(send_b, dc=1), keep_a, keep_b
+
+    def middle(self, state):
+        got_a, got_b, keep_a, keep_b = state
+        shape = keep_a.shape[1:]
+        sum_a = (keep_a + got_a.astype(F32)).reshape((2, 4) + shape)
+        sum_b = (keep_b + got_b.astype(F32)).reshape((2, 4) + shape)
+        return sum_a[0], sum_b[0], sum_a[1].astype(BF16), sum_b[1].astype(BF16)
+
+    def send(self, state):
+        sum_a, sum_b, out_a, out_b = state
+        return sum_a, sum_b, self.shift(out_a, dx=1), self.shift(out_b, dy=1)
+
+    def end(self, state):
+        def swap(values, **how):
             return self.shift(values.astype(BF16), **how).astype(F32)
 
-        send_a, send_b, keep_a, keep_b = parts
-        shape = keep_a.shape[1:]
-        sum_a = (keep_a + send(send_a, dc=1)).reshape((2, 4) + shape)
-        sum_b = (keep_b + send(send_b, dc=1)).reshape((2, 4) + shape)
-        sum_a = (sum_a[0] + send(sum_a[1], dx=1)).reshape((2, 2) + shape)
-        sum_b = (sum_b[0] + send(sum_b[1], dy=1)).reshape((2, 2) + shape)
-        sum_a = sum_a[:, 0] + send(sum_a[:, 1], dy=1)
-        sum_b = sum_b[:, 0] + send(sum_b[:, 1], dx=1)
+        sum_a, sum_b, got_a, got_b = state
+        shape = sum_a.shape[1:]
+        sum_a = (sum_a + got_a.astype(F32)).reshape((2, 2) + shape)
+        sum_b = (sum_b + got_b.astype(F32)).reshape((2, 2) + shape)
+        sum_a = sum_a[:, 0] + swap(sum_a[:, 1], dy=1)
+        sum_b = sum_b[:, 0] + swap(sum_b[:, 1], dx=1)
         return (
-            sum_a[0] + send(sum_a[1], dz=1) + send(sum_b[0], dz=2) + send(sum_b[1], dz=3)
+            sum_a[0] + swap(sum_a[1], dz=1) + swap(sum_b[0], dz=2) + swap(sum_b[1], dz=3)
         )
 
 
@@ -444,7 +498,7 @@
 
 def by_latent(*shape):
     zeros = (0,) * len(shape)
-    return pl.BlockSpec((1,) + shape, lambda step, scal: (step,) + zeros)
+    return pl.BlockSpec((PER_STEP,) + shape, lambda step, scal: (step,) + zeros)
 
 
 def call(kernel, count, in_specs, out_specs, out_shape, scratch, args, flops):
@@ -481,7 +535,7 @@
             return jnp.concatenate([counts.astype(jnp.int32), size * ids // GROUP]).astype(jnp.int32)
 
         attn_scal, mlp_scal = scalars(attn_size), scalars(mlp_size)
-        attn_pieces = plan.gather(to_piece(attn_params, attn_height, me))
+        attn_pieces = plan.pass_on(plan.gather(to_piece(attn_params, attn_height, me)))
         mlp_pieces = plan.gather(to_piece(mlp_params, mlp_height, me))
 
         def struct(shape, kind):
@@ -489,9 +543,10 @@
 
         n_pieces = len(attn_pieces)
         n_out = len(plan.slots)
+        steps = count // PER_STEP
         mod, ada, qkv_w, proj, _, qkv, probs, mixed, branch = call(
             lambda *refs: forward_kernel(n_pieces, *refs),
-            count,
+            steps,
             [whole(), by_latent(seq, D)] + [whole()] * n_pieces,
             [whole()] * 5
             + [
@@ -507,17 +562,22 @@
                 struct((D, D), BF16),
                 struct((8, D), F32),
                 struct((count, seq, 3 * D), BF16),
-                struct((count, HEADS, seq, seq), F32),
+                struct((count, HEADS, seq, seq), BF16),
                 struct((count, D, seq), BF16),
                 struct((count, seq, D), F32),
             ],
-            [pltpu.VMEM((TILES, ATTN_ROWS + attn_height, LANES), F32)],
+            [
+                pltpu.VMEM((TILES, ATTN_ROWS + attn_height, LANES), F32),
+                pltpu.VMEM((PER_STEP, HEADS, seq, seq), F32),
+            ],
             [attn_scal, condition, latents] + attn_pieces,
             15 * 10**9,
         )
+        mlp_pieces, mod = lax.optimization_barrier((mlp_pieces, mod))
+        mlp_pieces = plan.pass_on(mlp_pieces)
         results = call(
             lambda *refs: mlp_kernel(n_pieces, n_out, *refs),
-            count,
+            steps,
             [whole(), whole(), by_latent(seq, D), by_latent(seq, D), by_latent(D, seq), by_latent(seq, D)]
             + [whole()] * n_pieces,
             [by_latent(seq, D), by_latent(seq, D), by_latent(seq, D), whole(), whole()]
@@ -535,8 +595,8 @@
                 pltpu.VMEM((D, FF), BF16),
                 pltpu.VMEM((FF, D), BF16),
                 pltpu.VMEM((8, FF), F32),
-                pltpu.VMEM((seq, FF), BF16),
-                pltpu.VMEM((seq, FF), F32),
+                pltpu.VMEM((PER_STEP * seq, FF), BF16),
+                pltpu.VMEM((PER_STEP * seq, FF), F32),
                 pltpu.VMEM((D, FF), F32),
                 pltpu.VMEM((D, FF), F32),
                 pltpu.VMEM((8, FF), F32),
@@ -545,18 +605,29 @@
             30 * 10**9,
         )
         output, grad_middle, grad_mixed, dmod, dproj = results[:5]
-        grad_mlp = plan.scatter(results[5:])
+        sums = plan.begin(results[5:])
+        grad_qkv, = call(
+            attend_back_kernel,
+            steps,
+            [by_latent(seq, 3 * D), by_latent(HEADS, seq, seq), by_latent(seq, D)],
+            [by_latent(seq, 3 * D)],
+            [struct((count, seq, 3 * D), BF16)],
+            [
+                pltpu.VMEM((HEADS, seq, seq), F32),
+                pltpu.VMEM((HEADS, seq, seq), BF16),
+                pltpu.VMEM((D, seq), F32),
+            ],
+            [attn_scal, qkv, probs, grad_mixed],
+            13 * 10**9,
+        )
+        sums, grad_qkv = lax.optimization_barrier((sums, grad_qkv))
+        sums = plan.middle(sums)
+        sums, grad_qkv = lax.optimization_barrier((sums, grad_qkv))
+        sums = plan.send(sums)
         results = call(
-            lambda *refs: backward_kernel(n_out, 1 + devices, *refs),
-            count,
-            [whole()] * 6
-            + [
-                by_latent(seq, D),
-                by_latent(seq, 3 * D),
-                by_latent(HEADS, seq, seq),
-                by_latent(seq, D),
-                by_latent(seq, D),
-            ],
+            lambda *refs: finish_kernel(n_out, 1 + devices, *refs),
+            steps,
+            [whole()] * 6 + [by_latent(seq, D), by_latent(seq, 3 * D), by_latent(seq, D)],
             [by_latent(seq, D), whole()] + [whole()] * n_out,
             [struct((count, seq, D), F32), struct((count, D), F32)]
             + [struct((slots, attn_height, D), kind) for slots, kind in plan.slots],
@@ -565,14 +636,13 @@
                 pltpu.VMEM((D, 3 * D), F32),
                 pltpu.VMEM((2, count, D), F32),
                 pltpu.VMEM((8, 3 * D), F32),
-                pltpu.VMEM((seq, 3 * D), BF16),
-                pltpu.VMEM((D, seq), F32),
             ],
-            [attn_scal, condition, mod, ada, qkv_w, dmod, dproj, latents, qkv, probs, grad_middle, grad_mixed],
-            30 * 10**9,
+            [attn_scal, mod, qkv_w, condition, ada, dmod, dproj, latents, grad_qkv, grad_middle],
+            15 * 10**9,
         )
         grad_latents, grad_condition = results[:2]
-        grad_attn = plan.scatter(results[2:])
+        grad_mlp = plan.end(sums)
+        grad_attn = plan.end(plan.send(plan.middle(plan.begin(results[2:]))))
         return (
             output,
             grad_latents,

time: 196 us -> 173 us (0.88)
  starting transfers between devices: 67.3 us -> 35.7 us
  Pallas kernels: 73.6 us -> 82.3 us
    ppermute x42, starting transfers between devices: 67.3 us -> 35.7 us  [shift(): return lax.ppermute(values, AXIS, pairs)]
    pallas_call x3 -> x4, Pallas kernels: 73.6 us -> 82.3 us  [call(): pl.pallas_call(kernel, grid_spec=pltpu.PrefetchScalarGridSpec(num_scalar_...]
  transfers between devices with their start and end apart: 42 -> 42, of which waited for: 17 -> 17; matrix products, arithmetic and copies ran while one was open for 2% -> 3% of each run, Pallas kernels for 23% -> 27%
where the time goes in v2:
time: 173 us; the launch traced here: 174 us
  Pallas kernels  82.3 us (48%)
  waiting for transfers between devices  44.1 us (25%)
  starting transfers between devices  35.7 us (21%)
  local copies, waits for them, and re-layouts  7.16 us (4%)
  other arithmetic  2.64 us (2%)
  between operations  1.86 us (1%)
    pallas_call x4, Pallas kernels, call(): pl.pallas_call(kernel, grid_spec=pltpu.PrefetchScalarGridSpec(num_scalar_...  82.3 us
    ppermute x42, waiting for transfers between devices, shift(): return lax.ppermute(values, AXIS, pairs)  44.1 us
    ppermute x42, starting transfers between devices, shift(): return lax.ppermute(values, AXIS, pairs)  35.7 us
  transfers between devices with their start and end apart: 42, of which 17 were waited for; matrix products, arithmetic and copies ran while one was open for 3% of the time, Pallas kernels for 27%

profile of v2, /device:TPU:0, one launch (start us, length us, event | category | flops | bytes accessed | tf_op | source)
XLA Modules:
  0.0 173.7 jit_solution(14241763864564601523)
XLA Ops:
  0.7 2.0 %dynamic_update_slice.7 = bf16[49152]{0:T(1024)(128)(2,1)S(1)} dynamic-update-slice(bf16[49152]{0:T(1024)(128)(2,1)S(1)} %broadcast_in_dim.7, bf16[46176]{0:T(1024)(128)(2,1)} %param.8, s32[]{:T(128)S(6)} %select_n.615) | dynamic-update-slice | bytes 184708 | tf_op jit(solution)/shard_map/dynamic_update_slice | solution.py:488
  2.7 5.1 %collective-permute-start.9 = (bf16[128,384]{1,0:T(8,128)(2,1)S(1)}, bf16[128,384]{1,0:T(8,128)(2,1)S(1)}, u32[]{:S(2)}, u32[]{:S(2)}) collective-permute-start(bf16[128,384]{1,0:T(8,128)(2,1)S(1)} %reshape.65), channel_id=1, source_target_pairs={{0,24},{1,25},{2,26},{3,27},{4,28},{5,29},{6,30},{7,31},{8,0},{9,1... | collective-permute-start | bytes 294920 | tf_op jit(solution)/shard_map/ppermute | solution.py:441
  7.8 1.0 collective-permute-start.7
  8.9 2.1 %collective-permute-done.9 = bf16[128,384]{1,0:T(8,128)(2,1)S(1)} collective-permute-done((bf16[128,384]{1,0:T(8,128)(2,1)S(1)}, bf16[128,384]{1,0:T(8,128)(2,1)S(1)}, u32[]{:S(2)}, u32[]{:S(2)}) %collective-permute-start.9) | collective-permute-done | bytes 98336 | tf_op jit(solution)/shard_map/ppermute | solution.py:441
  11.0 5.6 %collective-permute-done.8 = bf16[128,384]{1,0:T(8,128)(2,1)S(1)} collective-permute-done((bf16[128,384]{1,0:T(8,128)(2,1)S(1)}, bf16[128,384]{1,0:T(8,128)(2,1)S(1)}, u32[]{:S(2)}, u32[]{:S(2)}) %collective-permute-start.8) | collective-permute-done | bytes 98336 | tf_op jit(solution)/shard_map/ppermute | solution.py:441
  16.6 1.6 collective-permute-start.11
  18.2 1.6 collective-permute-start.10
  19.8 3.2 %collective-permute-done.11.refs_5_ = bf16[2,128,384]{2,1,0:T(8,128)(2,1)S(1)} collective-permute-done((bf16[2,128,384]{2,1,0:T(8,128)(2,1)S(1)}, bf16[2,128,384]{2,1,0:T(8,128)(2,1)S(1)}, u32[]{:S(2)}, u32[]{:S(2)}) %collective-permute-start.11) | collective-permute-done | bytes 196640 | tf_op jit(solution)/shard_map/ppermute | solution.py:441
  23.0 1.3 collective-permute-done.10.refs_4_
  24.5 1.6 collective-permute-start.13
  26.1 0.5 collective-permute-start.12
  26.6 0.9 dynamic_update_slice.6
  27.5 2.3 %collective-permute-start.2 = (bf16[112,384]{1,0:T(8,128)(2,1)S(1)}, bf16[112,384]{1,0:T(8,128)(2,1)S(1)}, u32[]{:S(2)}, u32[]{:S(2)}) collective-permute-start(bf16[112,384]{1,0:T(8,128)(2,1)S(1)} %reshape.64), channel_id=1, source_target_pairs={{0,24},{1,25},{2,26},{3,27},{4,28},{5,29},{6,30},{7,31},{8,0},{9,1... | collective-permute-start | bytes 258056 | tf_op jit(solution)/shard_map/ppermute | solution.py:441
  29.8 1.4 collective-permute-start
  32.1 0.9 collective-permute-done.2
  33.0 3.3 %collective-permute-done.1 = bf16[112,384]{1,0:T(8,128)(2,1)S(1)} collective-permute-done((bf16[112,384]{1,0:T(8,128)(2,1)S(1)}, bf16[112,384]{1,0:T(8,128)(2,1)S(1)}, u32[]{:S(2)}, u32[]{:S(2)}) %collective-permute-start.1) | collective-permute-done | bytes 86048 | tf_op jit(solution)/shard_map/ppermute | solution.py:441
  36.3 1.6 collective-permute-start.4
  37.9 0.6 collective-permute-start.3
  38.5 0.5 collective-permute-start.18
  39.1 2.6 %collective-permute-done.4.refs_9_ = bf16[2,112,384]{2,1,0:T(8,128)(2,1)S(1)} collective-permute-done((bf16[2,112,384]{2,1,0:T(8,128)(2,1)S(1)}, bf16[2,112,384]{2,1,0:T(8,128)(2,1)S(1)}, u32[]{:S(2)}, u32[]{:S(2)}) %collective-permute-start.4) | collective-permute-done | bytes 172064 | tf_op jit(solution)/shard_map/ppermute | solution.py:441
  41.8 1.6 collective-permute-done.3.refs_8_
  43.4 0.7 pad_add_fusion.1.refs_0_.scal_ref
  44.2 0.6 collective-permute-start.6
  44.8 0.5 collective-permute-start.5
  45.5 0.7 copy-done.14
  46.2 18.8 %shard_map.101 = (f32[6,8,384]{2,1,0:T(8,128)}, bf16[6,384,384]{2,1,0:T(8,128)(2,1)}, bf16[384,1152]{1,0:T(8,128)(2,1)}, bf16[384,384]{1,0:T(8,128)(2,1)}, f32[8...) custom-call(s32[65]{0:T(128)} %pad_add_fusion.1.refs_0_.scal_ref, ...), custom_call_target="tpu_custom_call" | custom-call | flops 15000000512 | bytes 20971520 | tf_op jit(solution)/shard_map/pallas_call | solution.py:505
  65.1 0.3 collective-permute-start.19
  65.3 0.3 collective-permute-start.22
  65.6 0.2 collective-permute-start.23
  65.8 0.3 collective-permute-start.20
  66.1 0.2 collective-permute-start.21
  66.3 0.6 pad_add_fusion.refs_0_
  66.9 1.1 collective-permute-done.20.refs_13_
  68.0 0.2 collective-permute-done.21.refs_14_
  68.3 0.4 copy-done.22
  68.7 0.2 copy-done.23
  68.9 0.2 copy-done.17
  69.3 35.5 %shard_map.102 = (bf16[8,256,384]{2,1,0:T(8,128)(2,1)}, f32[8,256,384]{2,1,0:T(8,128)}, bf16[8,256,384]{2,1,0:T(8,128)(2,1)}, f32[4,8,384]{2,1,0:T(8,128)}, f32[...) custom-call(s32[65]{0:T(128)} %pad_add_fusion.refs_0_, ...), custom_call_target="tpu_custom_call" | custom-call | flops 30000001024 | bytes 20971520 | tf_op jit(solution)/shard_map/pallas_call | solution.py:505
  104.8 0.3 collective-permute-start.24
  105.0 0.3 collective-permute-start.25
  105.4 12.1 %shard_map.103.refs_8_ = bf16[8,256,1152]{2,1,0:T(8,128)(2,1)} custom-call(s32[65]{0:T(128)} %pad_add_fusion.1.refs_0_.scal_ref, bf16[8,256,1152]{2,1,0:T(8,128)(2,1)} %get-tuple-element.63.qkv_ref, bf16[8,6,256,256]{3,2,1,0:T(8,128)(2,1)} %get-tuple-element.64.probs_ref, bf16[8,256,384]{2,1,0:T(8,128)(2,1)} %get-tuple-element.65.dmixed_ref), custom_call_target="tpu_custom_call" | custom-call | flops 12999999488 | bytes 20971520 | tf_op jit(solution)/shard_map/pallas_call | solution.py:505
  117.5 0.2 convert_add_fusion.2
  118.1 15.9 %shard_map.104 = (f32[8,256,384]{2,1,0:T(8,128)}, f32[8,384]{1,0:T(8,128)}, bf16[8,128,384]{2,1,0:T(8,128)(2,1)}, bf16[8,128,384]{2,1,0:T(8,128)(2,1)}, f32[8,128,384]{2,1,0:T(8,128)}, /*index=5*/f32[8,128,384]{2,1,0:T(8,128)}) custom-call(s32[65]{0:T(128)} %pad_add_fusion.1.refs_0_.scal_ref, f32[6,8,384]{2,1,0:T(8,128)} %get-tuple-element.45.refs_1_, ...), custom_call_target="tpu_custom_call" | custom-call | flops 15000000512 | bytes 20971520 | tf_op jit(solution)/shard_map/pallas_call | solution.py:505
  134.0 1.4 collective-permute-start.26
  135.8 1.4 collective-permute-start.39
  137.2 5.1 %collective-permute-done.36 = bf16[2,112,384]{2,1,0:T(8,128)(2,1)S(1)} collective-permute-done((bf16[2,112,384]{2,1,0:T(8,128)(2,1)S(1)}, bf16[2,112,384]{2,1,0:T(8,128)(2,1)S(1)}, u32[]{:S(2)}, u32[]{:S(2)}) %collective-permute-start.36) | collective-permute-done | bytes 172064 | tf_op jit(solution)/shard_map/ppermute | solution.py:441
  142.4 0.4 collective-permute-start.37
  143.2 0.5 collective-permute-start.27
  143.7 0.9 collective-permute-start.40
  144.5 2.8 %collective-permute-start.41 = (bf16[112,384]{1,0:T(8,128)(2,1)S(1)}, bf16[112,384]{1,0:T(8,128)(2,1)S(1)}, u32[]{:S(2)}, u32[]{:S(2)}) collective-permute-start(bf16[112,384]{1,0:T(8,128)(2,1)S(1)} %get-tuple-element.89), channel_id=1, source_target_pairs={{0,24},{1,25},{2,26},{3,27},{4,28},{5,29},{6,30},{7,31},{8,0},{9,1... | collective-permute-start | bytes 258056 | tf_op jit(solution)/shard_map/ppermute | solution.py:441
  147.5 0.6 collective-permute-start.31
  148.1 5.4 %collective-permute-done.27 = bf16[4,128,384]{2,1,0:T(8,128)(2,1)S(1)} collective-permute-done((bf16[4,128,384]{2,1,0:T(8,128)(2,1)S(1)}, bf16[4,128,384]{2,1,0:T(8,128)(2,1)S(1)}, u32[]{:S(2)}, u32[]{:S(2)}) %collective-permute-start.27) | collective-permute-done | bytes 393248 | tf_op jit(solution)/shard_map/ppermute | solution.py:441
  153.6 1.5 collective-permute-start.28
  155.2 4.4 %collective-permute-done.31 = bf16[4,128,384]{2,1,0:T(8,128)(2,1)S(1)} collective-permute-done((bf16[4,128,384]{2,1,0:T(8,128)(2,1)S(1)}, bf16[4,128,384]{2,1,0:T(8,128)(2,1)S(1)}, u32[]{:S(2)}, u32[]{:S(2)}) %collective-permute-start.31) | collective-permute-done | bytes 393248 | tf_op jit(solution)/shard_map/ppermute | solution.py:441
  159.7 1.6 collective-permute-start.32
  161.2 0.4 collective-permute-done.28
  161.7 0.6 collective-permute-start.29
  162.3 3.1 %collective-permute-done.32 = bf16[2,128,384]{2,1,0:T(8,128)(2,1)S(1)} collective-permute-done((bf16[2,128,384]{2,1,0:T(8,128)(2,1)S(1)}, bf16[2,128,384]{2,1,0:T(8,128)(2,1)S(1)}, u32[]{:S(2)}, u32[]{:S(2)}) %collective-permute-start.32) | collective-permute-done | bytes 196640 | tf_op jit(solution)/shard_map/ppermute | solution.py:441
  165.5 1.7 %collective-permute-start.33 = (bf16[128,384]{1,0:T(8,128)(2,1)S(1)}, bf16[128,384]{1,0:T(8,128)(2,1)S(1)}, u32[]{:S(2)}, u32[]{:S(2)}) collective-permute-start(bf16[128,384]{1,0:T(8,128)(2,1)S(1)} %get-tuple-element.83), channel_id=1, source_target_pairs={{0,16},{1,17},{2,18},{3,19},{4,20},{5,21},{6,22},{7,23},{8,24},{9,... | collective-permute-start | bytes 294920 | tf_op jit(solution)/shard_map/ppermute | solution.py:441
  167.2 1.2 collective-permute-start.34
  168.5 0.8 dynamic_slice.7
  169.3 2.9 %collective-permute-done.33 = bf16[128,384]{1,0:T(8,128)(2,1)S(1)} collective-permute-done((bf16[128,384]{1,0:T(8,128)(2,1)S(1)}, bf16[128,384]{1,0:T(8,128)(2,1)S(1)}, u32[]{:S(2)}, u32[]{:S(2)}) %collective-permute-start.33) | collective-permute-done | bytes 98336 | tf_op jit(solution)/shard_map/ppermute | solution.py:441
  172.2 0.7 collective-permute-done.34
  172.9 0.8 dynamic_slice.6
  (121 shorter events, 2.9 us)
Async XLA Ops:
  2.7 23.9 %copy-start.10 = (bf16[36936]{0:T(1024)(128)(2,1)S(1)}, bf16[36936]{0:T(1024)(128)(2,1)}, u32[]{:S(2)}) copy-start(bf16[36936]{0:T(1024)(128)(2,1)} %param.9) | copy-start | bytes 221620
  2.7 8.3 %collective-permute-start.9 = (bf16[128,384]{1,0:T(8,128)(2,1)S(1)}, bf16[128,384]{1,0:T(8,128)(2,1)S(1)}, u32[]{:S(2)}, u32[]{:S(2)}) collective-permute-start(bf16[128,384]{1,0:T(8,128)(2,1)S(1)} %reshape.65), channel_id=1, source_target_pairs={{0,24},{1,25},{2,26},{3,27},{4,28},{5,29},{6,30},{7,31},{8,0},{9,1... | collective-permute-start | bytes 294920 | tf_op jit(solution)/shard_map/ppermute | solution.py:441
  7.8 8.8 %collective-permute-start.8 = (bf16[128,384]{1,0:T(8,128)(2,1)S(1)}, bf16[128,384]{1,0:T(8,128)(2,1)S(1)}, u32[]{:S(2)}, u32[]{:S(2)}) collective-permute-start(bf16[128,384]{1,0:T(8,128)(2,1)S(1)} %reshape.65), channel_id=1, source_target_pairs={{0,16},{1,17},{2,18},{3,19},{4,20},{5,21},{6,22},{7,23},{8,24},{9,... | collective-permute-start | bytes 294920 | tf_op jit(solution)/shard_map/ppermute | solution.py:441
  7.8 10.4 %collective-permute-start.7 = (bf16[128,384]{1,0:T(8,128)(2,1)S(1)}, bf16[128,384]{1,0:T(8,128)(2,1)S(1)}, u32[]{:S(2)}, u32[]{:S(2)}) collective-permute-start(bf16[128,384]{1,0:T(8,128)(2,1)S(1)} %reshape.65), channel_id=1, source_target_pairs={{0,8},{1,9},{2,10},{3,11},{4,12},{5,13},{6,14},{7,15},{8,16},{9,17... | collective-permute-start | bytes 294920 | tf_op jit(solution)/shard_map/ppermute | solution.py:441
  16.6 6.4 %collective-permute-start.11 = (bf16[2,128,384]{2,1,0:T(8,128)(2,1)S(1)}, bf16[2,128,384]{2,1,0:T(8,128)(2,1)S(1)}, u32[]{:S(2)}, u32[]{:S(2)}) collective-permute-start(bf16[2,128,384]{2,1,0:T(8,128)(2,1)S(1)} %pad_maximum_fusion.9), channel_id=1, source_target_pairs={{0,4},{1,5},{2,6},{3,7},{4,0},{5,1},{6,2},{7,3},{8,12},{9,13},{10,... | collective-permute-start | bytes 589832 | tf_op jit(solution)/shard_map/ppermute | solution.py:441
  18.2 6.1 %collective-permute-start.10 = (bf16[2,128,384]{2,1,0:T(8,128)(2,1)S(1)}, bf16[2,128,384]{2,1,0:T(8,128)(2,1)S(1)}, u32[]{:S(2)}, u32[]{:S(2)}) collective-permute-start(bf16[2,128,384]{2,1,0:T(8,128)(2,1)S(1)} %pad_maximum_fusion.8), channel_id=1, source_target_pairs={{0,2},{1,3},{2,0},{3,1},{4,6},{5,7},{6,4},{7,5},{8,10},{9,11},{10,... | collective-permute-start | bytes 589832 | tf_op jit(solution)/shard_map/ppermute | solution.py:441
  23.0 18.7 %copy-start.6 = (bf16[2,128,384]{2,1,0:T(8,128)(2,1)}, bf16[2,128,384]{2,1,0:T(8,128)(2,1)S(1)}, u32[]{:S(2)}) copy-start(bf16[2,128,384]{2,1,0:T(8,128)(2,1)S(1)} %collective-permute-done.11.refs_5_) | copy-start | bytes 589828
  24.3 19.0 %copy-start.7 = (bf16[2,128,384]{2,1,0:T(8,128)(2,1)}, bf16[2,128,384]{2,1,0:T(8,128)(2,1)S(1)}, u32[]{:S(2)}) copy-start(bf16[2,128,384]{2,1,0:T(8,128)(2,1)S(1)} %collective-permute-done.10.refs_4_) | copy-start | bytes 589828
  24.5 19.7 %copy-start.4 = (bf16[4,128,384]{2,1,0:T(8,128)(2,1)}, bf16[4,128,384]{2,1,0:T(8,128)(2,1)S(1)}, u32[]{:S(2)}) copy-start(bf16[4,128,384]{2,1,0:T(8,128)(2,1)S(1)} %get-tuple-element.86.refs_3_) | copy-start | bytes 1179652
  24.5 14.0 %collective-permute-start.13 = (bf16[4,128,384]{2,1,0:T(8,128)(2,1)S(1)}, bf16[4,128,384]{2,1,0:T(8,128)(2,1)S(1)}, u32[]{:S(2)}, u32[]{:S(2)}) collective-permute-start(bf16[4,128,384]{2,1,0:T(8,128)(2,1)S(1)} %get-tuple-element.85), channel_id=1, source_target_pairs={{0,2},{1,3},{2,0},{3,1},{4,6},{5,7},{6,4},{7,5},{8,10},{9,11},{10,... | collective-permute-start | bytes 1179656 | tf_op jit(solution)/shard_map/ppermute | solution.py:441
  26.1 13.0 %collective-permute-start.12 = (bf16[4,128,384]{2,1,0:T(8,128)(2,1)S(1)}, bf16[4,128,384]{2,1,0:T(8,128)(2,1)S(1)}, u32[]{:S(2)}, u32[]{:S(2)}) collective-permute-start(bf16[4,128,384]{2,1,0:T(8,128)(2,1)S(1)} %get-tuple-element.87), channel_id=1, source_target_pairs={{0,4},{1,5},{2,6},{3,7},{4,0},{5,1},{6,2},{7,3},{8,12},{9,13},{10,... | collective-permute-start | bytes 1179656 | tf_op jit(solution)/shard_map/ppermute | solution.py:441
  27.5 5.5 %collective-permute-start.2 = (bf16[112,384]{1,0:T(8,128)(2,1)S(1)}, bf16[112,384]{1,0:T(8,128)(2,1)S(1)}, u32[]{:S(2)}, u32[]{:S(2)}) collective-permute-start(bf16[112,384]{1,0:T(8,128)(2,1)S(1)} %reshape.64), channel_id=1, source_target_pairs={{0,24},{1,25},{2,26},{3,27},{4,28},{5,29},{6,30},{7,31},{8,0},{9,1... | collective-permute-start | bytes 258056 | tf_op jit(solution)/shard_map/ppermute | solution.py:441
  29.8 6.4 %collective-permute-start.1 = (bf16[112,384]{1,0:T(8,128)(2,1)S(1)}, bf16[112,384]{1,0:T(8,128)(2,1)S(1)}, u32[]{:S(2)}, u32[]{:S(2)}) collective-permute-start(bf16[112,384]{1,0:T(8,128)(2,1)S(1)} %reshape.64), channel_id=1, source_target_pairs={{0,16},{1,17},{2,18},{3,19},{4,20},{5,21},{6,22},{7,23},{8,24},{9,... | collective-permute-start | bytes 258056 | tf_op jit(solution)/shard_map/ppermute | solution.py:441
  29.8 8.0 %collective-permute-start = (bf16[112,384]{1,0:T(8,128)(2,1)S(1)}, bf16[112,384]{1,0:T(8,128)(2,1)S(1)}, u32[]{:S(2)}, u32[]{:S(2)}) collective-permute-start(bf16[112,384]{1,0:T(8,128)(2,1)S(1)} %reshape.64), channel_id=1, source_target_pairs={{0,8},{1,9},{2,10},{3,11},{4,12},{5,13},{6,14},{7,15},{8,16},{9,17... | collective-permute-start | bytes 258056 | tf_op jit(solution)/shard_map/ppermute | solution.py:441
  36.3 5.5 %collective-permute-start.4 = (bf16[2,112,384]{2,1,0:T(8,128)(2,1)S(1)}, bf16[2,112,384]{2,1,0:T(8,128)(2,1)S(1)}, u32[]{:S(2)}, u32[]{:S(2)}) collective-permute-start(bf16[2,112,384]{2,1,0:T(8,128)(2,1)S(1)} %pad_maximum_fusion.11), channel_id=1, source_target_pairs={{0,4},{1,5},{2,6},{3,7},{4,0},{5,1},{6,2},{7,3},{8,12},{9,13},{10,... | collective-permute-start | bytes 516104 | tf_op jit(solution)/shard_map/ppermute | solution.py:441
  37.9 5.5 %collective-permute-start.3 = (bf16[2,112,384]{2,1,0:T(8,128)(2,1)S(1)}, bf16[2,112,384]{2,1,0:T(8,128)(2,1)S(1)}, u32[]{:S(2)}, u32[]{:S(2)}) collective-permute-start(bf16[2,112,384]{2,1,0:T(8,128)(2,1)S(1)} %pad_maximum_fusion.10), channel_id=1, source_target_pairs={{0,2},{1,3},{2,0},{3,1},{4,6},{5,7},{6,4},{7,5},{8,10},{9,11},{10,... | collective-permute-start | bytes 516104 | tf_op jit(solution)/shard_map/ppermute | solution.py:441
  38.5 6.8 %collective-permute-start.14 = (bf16[4,128,384]{2,1,0:T(8,128)(2,1)S(1)}, bf16[4,128,384]{2,1,0:T(8,128)(2,1)S(1)}, u32[]{:S(2)}, u32[]{:S(2)}) collective-permute-start(bf16[4,128,384]{2,1,0:T(8,128)(2,1)S(1)} %get-tuple-element.86.refs_3_), channel_id=1, source_target_pairs={{0,1},{1,0},{2,3},{3,2},{4,5},{5,4},{6,7},{7,6},{8,9},{9,8},{10,11... | collective-permute-start | bytes 1179656 | tf_op jit(solution)/shard_map/ppermute | solution.py:441
  38.5 7.7 %copy-start.11 = (bf16[4,128,384]{2,1,0:T(8,128)(2,1)}, bf16[4,128,384]{2,1,0:T(8,128)(2,1)S(1)}, u32[]{:S(2)}) copy-start(bf16[4,128,384]{2,1,0:T(8,128)(2,1)S(1)} %collective-permute-done.13.refs_7_) | copy-start | bytes 1179652
  38.5 6.8 %collective-permute-start.18 = (bf16[4,128,384]{2,1,0:T(8,128)(2,1)S(1)}, bf16[4,128,384]{2,1,0:T(8,128)(2,1)S(1)}, u32[]{:S(2)}, u32[]{:S(2)}) collective-permute-start(bf16[4,128,384]{2,1,0:T(8,128)(2,1)S(1)} %collective-permute-done.13.refs_7_), channel_id=1, source_target_pairs={{0,1},{1,0},{2,3},{3,2},{4,5},{5,4},{6,7},{7,6},{8,9},{9,8},{10,11... | collective-permute-start | bytes 1179656 | tf_op jit(solution)/shard_map/ppermute | solution.py:441
  39.0 7.2 %copy-start.12 = (bf16[4,128,384]{2,1,0:T(8,128)(2,1)}, bf16[4,128,384]{2,1,0:T(8,128)(2,1)S(1)}, u32[]{:S(2)}) copy-start(bf16[4,128,384]{2,1,0:T(8,128)(2,1)S(1)} %collective-permute-done.12.refs_6_) | copy-start | bytes 1179652
  39.0 7.2 %collective-permute-start.17 = (bf16[4,128,384]{2,1,0:T(8,128)(2,1)S(1)}, bf16[4,128,384]{2,1,0:T(8,128)(2,1)}, u32[]{:S(2)}, u32[]{:S(2)}) collective-permute-start(bf16[4,128,384]{2,1,0:T(8,128)(2,1)S(1)} %collective-permute-done.12.refs_6_), channel_id=1, source_target_pairs={{0,1},{1,0},{2,3},{3,2},{4,5},{5,4},{6,7},{7,6},{8,9},{9,8},{10,11... | collective-permute-start | bytes 1179656 | tf_op jit(solution)/shard_map/ppermute | solution.py:441
  41.8 24.4 %copy-start.8 = (bf16[2,112,384]{2,1,0:T(8,128)(2,1)}, bf16[2,112,384]{2,1,0:T(8,128)(2,1)S(1)}, u32[]{:S(2)}) copy-start(bf16[2,112,384]{2,1,0:T(8,128)(2,1)S(1)} %collective-permute-done.4.refs_9_) | copy-start | bytes 516100
  41.8 2.4 %collective-permute-start.16 = (bf16[2,128,384]{2,1,0:T(8,128)(2,1)S(1)}, bf16[2,128,384]{2,1,0:T(8,128)(2,1)S(1)}, u32[]{:S(2)}, u32[]{:S(2)}) collective-permute-start(bf16[2,128,384]{2,1,0:T(8,128)(2,1)S(1)} %collective-permute-done.11.refs_5_), channel_id=1, source_target_pairs={{0,1},{1,0},{2,3},{3,2},{4,5},{5,4},{6,7},{7,6},{8,9},{9,8},{10,11... | collective-permute-start | bytes 589832 | tf_op jit(solution)/shard_map/ppermute | solution.py:441
  43.4 22.5 %copy-start.9 = (bf16[2,112,384]{2,1,0:T(8,128)(2,1)}, bf16[2,112,384]{2,1,0:T(8,128)(2,1)S(1)}, u32[]{:S(2)}) copy-start(bf16[2,112,384]{2,1,0:T(8,128)(2,1)S(1)} %collective-permute-done.3.refs_8_) | copy-start | bytes 516100
  43.4 1.4 collective-permute-start.15
  44.2 20.9 %copy-start.5 = (bf16[4,112,384]{2,1,0:T(8,128)(2,1)}, bf16[4,112,384]{2,1,0:T(8,128)(2,1)S(1)}, u32[]{:S(2)}) copy-start(bf16[4,112,384]{2,1,0:T(8,128)(2,1)S(1)} %get-tuple-element.49.refs_7_) | copy-start | bytes 1032196
  44.2 1.1 copy-start.20
  44.2 20.8 %collective-permute-start.6 = (bf16[4,112,384]{2,1,0:T(8,128)(2,1)S(1)}, bf16[4,112,384]{2,1,0:T(8,128)(2,1)S(1)}, u32[]{:S(2)}, u32[]{:S(2)}) collective-permute-start(bf16[4,112,384]{2,1,0:T(8,128)(2,1)S(1)} %get-tuple-element.90), channel_id=1, source_target_pairs={{0,2},{1,3},{2,0},{3,1},{4,6},{5,7},{6,4},{7,5},{8,10},{9,11},{10,... | collective-permute-start | bytes 1032200 | tf_op jit(solution)/shard_map/ppermute | solution.py:441
  44.8 20.2 %collective-permute-start.5 = (bf16[4,112,384]{2,1,0:T(8,128)(2,1)S(1)}, bf16[4,112,384]{2,1,0:T(8,128)(2,1)S(1)}, u32[]{:S(2)}, u32[]{:S(2)}) collective-permute-start(bf16[4,112,384]{2,1,0:T(8,128)(2,1)S(1)} %get-tuple-element.92), channel_id=1, source_target_pairs={{0,4},{1,5},{2,6},{3,7},{4,0},{5,1},{6,2},{7,3},{8,12},{9,13},{10,... | collective-permute-start | bytes 1032200 | tf_op jit(solution)/shard_map/ppermute | solution.py:441
  45.3 0.9 copy-start.13
  45.5 0.7 copy-start.14
  65.0 3.3 %copy-start.15 = (bf16[4,112,384]{2,1,0:T(8,128)(2,1)}, bf16[4,112,384]{2,1,0:T(8,128)(2,1)S(1)}, u32[]{:S(2)}) copy-start(bf16[4,112,384]{2,1,0:T(8,128)(2,1)S(1)} %collective-permute-done.6.refs_11_) | copy-start | bytes 1032196
  65.0 3.3 %copy-start.16 = (bf16[4,112,384]{2,1,0:T(8,128)(2,1)}, bf16[4,112,384]{2,1,0:T(8,128)(2,1)S(1)}, u32[]{:S(2)}) copy-start(bf16[4,112,384]{2,1,0:T(8,128)(2,1)S(1)} %collective-permute-done.5.refs_10_) | copy-start | bytes 1032196
  65.1 3.2 %collective-permute-start.19 = (bf16[4,112,384]{2,1,0:T(8,128)(2,1)S(1)}, bf16[4,112,384]{2,1,0:T(8,128)(2,1)S(1)}, u32[]{:S(2)}, u32[]{:S(2)}) collective-permute-start(bf16[4,112,384]{2,1,0:T(8,128)(2,1)S(1)} %get-tuple-element.49.refs_7_), channel_id=1, source_target_pairs={{0,1},{1,0},{2,3},{3,2},{4,5},{5,4},{6,7},{7,6},{8,9},{9,8},{10,11... | collective-permute-start | bytes 1032200 | tf_op jit(solution)/shard_map/ppermute | solution.py:441
  65.3 2.9 %collective-permute-start.22 = (bf16[4,112,384]{2,1,0:T(8,128)(2,1)S(1)}, bf16[4,112,384]{2,1,0:T(8,128)(2,1)S(1)}, u32[]{:S(2)}, u32[]{:S(2)}) collective-permute-start(bf16[4,112,384]{2,1,0:T(8,128)(2,1)S(1)} %collective-permute-done.5.refs_10_), channel_id=1, source_target_pairs={{0,1},{1,0},{2,3},{3,2},{4,5},{5,4},{6,7},{7,6},{8,9},{9,8},{10,11... | collective-permute-start | bytes 1032200 | tf_op jit(solution)/shard_map/ppermute | solution.py:441
  65.6 2.6 %collective-permute-start.23 = (bf16[4,112,384]{2,1,0:T(8,128)(2,1)S(1)}, bf16[4,112,384]{2,1,0:T(8,128)(2,1)S(1)}, u32[]{:S(2)}, u32[]{:S(2)}) collective-permute-start(bf16[4,112,384]{2,1,0:T(8,128)(2,1)S(1)} %collective-permute-done.6.refs_11_), channel_id=1, source_target_pairs={{0,1},{1,0},{2,3},{3,2},{4,5},{5,4},{6,7},{7,6},{8,9},{9,8},{10,11... | collective-permute-start | bytes 1032200 | tf_op jit(solution)/shard_map/ppermute | solution.py:441
  65.8 2.2 %collective-permute-start.20 = (bf16[2,112,384]{2,1,0:T(8,128)(2,1)S(1)}, bf16[2,112,384]{2,1,0:T(8,128)(2,1)S(1)}, u32[]{:S(2)}, u32[]{:S(2)}) collective-permute-start(bf16[2,112,384]{2,1,0:T(8,128)(2,1)S(1)} %collective-permute-done.3.refs_8_), channel_id=1, source_target_pairs={{0,1},{1,0},{2,3},{3,2},{4,5},{5,4},{6,7},{7,6},{8,9},{9,8},{10,11... | collective-permute-start | bytes 516104 | tf_op jit(solution)/shard_map/ppermute | solution.py:441
  66.1 2.1 %collective-permute-start.21 = (bf16[2,112,384]{2,1,0:T(8,128)(2,1)S(1)}, bf16[2,112,384]{2,1,0:T(8,128)(2,1)S(1)}, u32[]{:S(2)}, u32[]{:S(2)}) collective-permute-start(bf16[2,112,384]{2,1,0:T(8,128)(2,1)S(1)} %collective-permute-done.4.refs_9_), channel_id=1, source_target_pairs={{0,1},{1,0},{2,3},{3,2},{4,5},{5,4},{6,7},{7,6},{8,9},{9,8},{10,11... | collective-permute-start | bytes 516104 | tf_op jit(solution)/shard_map/ppermute | solution.py:441
  68.0 0.7 copy-start.22
  68.3 0.8 copy-start.17
  68.3 0.9 copy-start.18
  68.3 1.0 copy-start.19
  104.8 12.7 %collective-permute-start.24 = (bf16[8,112,384]{2,1,0:T(8,128)(2,1)}, bf16[8,112,384]{2,1,0:T(8,128)(2,1)S(1)}, u32[]{:S(2)}, u32[]{:S(2)}) collective-permute-start(bf16[8,112,384]{2,1,0:T(8,128)(2,1)} %get-tuple-element.59), channel_id=1, source_target_pairs={{0,1},{1,0},{2,3},{3,2},{4,5},{5,4},{6,7},{7,6},{8,9},{9,8},{10,11... | collective-permute-start | bytes 2064392 | tf_op jit(solution)/shard_map/ppermute | solution.py:441
  105.0 12.4 %collective-permute-start.25 = (bf16[8,112,384]{2,1,0:T(8,128)(2,1)}, bf16[8,112,384]{2,1,0:T(8,128)(2,1)S(1)}, u32[]{:S(2)}, u32[]{:S(2)}) collective-permute-start(bf16[8,112,384]{2,1,0:T(8,128)(2,1)} %get-tuple-element.60), channel_id=1, source_target_pairs={{0,1},{1,0},{2,3},{3,2},{4,5},{5,4},{6,7},{7,6},{8,9},{9,8},{10,11... | collective-permute-start | bytes 2064392 | tf_op jit(solution)/shard_map/ppermute | solution.py:441
  105.3 12.1 %copy-start.2 = (f32[8,112,384]{2,1,0:T(8,128)S(1)}, f32[8,112,384]{2,1,0:T(8,128)}, u32[]{:S(2)}) copy-start(f32[8,112,384]{2,1,0:T(8,128)} %get-tuple-element.66) | copy-start | bytes 4128772
  105.3 12.1 %copy-start.3 = (f32[8,112,384]{2,1,0:T(8,128)S(1)}, f32[8,112,384]{2,1,0:T(8,128)}, u32[]{:S(2)}) copy-start(f32[8,112,384]{2,1,0:T(8,128)} %get-tuple-element.68) | copy-start | bytes 4128772
  117.9 17.5 %collective-permute-start.35 = (bf16[4,112,384]{2,1,0:T(8,128)(2,1)S(1)}, bf16[4,112,384]{2,1,0:T(8,128)(2,1)S(1)}, u32[]{:S(2)}, u32[]{:S(2)}) collective-permute-start(bf16[4,112,384]{2,1,0:T(8,128)(2,1)S(1)} %slice.199), channel_id=1, source_target_pairs={{0,2},{1,3},{2,0},{3,1},{4,6},{5,7},{6,4},{7,5},{8,10},{9,11},{10,... | collective-permute-start | bytes 1032200 | tf_op jit(solution)/shard_map/ppermute | solution.py:441
  118.0 17.7 %collective-permute-start.38 = (bf16[4,112,384]{2,1,0:T(8,128)(2,1)S(1)}, bf16[4,112,384]{2,1,0:T(8,128)(2,1)S(1)}, u32[]{:S(2)}, u32[]{:S(2)}) collective-permute-start(bf16[4,112,384]{2,1,0:T(8,128)(2,1)S(1)} %slice.198), channel_id=1, source_target_pairs={{0,4},{1,5},{2,6},{3,7},{4,0},{5,1},{6,2},{7,3},{8,12},{9,13},{10,... | collective-permute-start | bytes 1032200 | tf_op jit(solution)/shard_map/ppermute | solution.py:441
  134.0 8.9 %collective-permute-start.26 = (bf16[8,128,384]{2,1,0:T(8,128)(2,1)}, bf16[8,128,384]{2,1,0:T(8,128)(2,1)S(1)}, u32[]{:S(2)}, u32[]{:S(2)}) collective-permute-start(bf16[8,128,384]{2,1,0:T(8,128)(2,1)} %get-tuple-element.76), channel_id=1, source_target_pairs={{0,1},{1,0},{2,3},{3,2},{4,5},{5,4},{6,7},{7,6},{8,9},{9,8},{10,11... | collective-permute-start | bytes 2359304 | tf_op jit(solution)/shard_map/ppermute | solution.py:441
  135.4 11.9 %collective-permute-start.30 = (bf16[8,128,384]{2,1,0:T(8,128)(2,1)}, bf16[8,128,384]{2,1,0:T(8,128)(2,1)S(1)}, u32[]{:S(2)}, u32[]{:S(2)}) collective-permute-start(bf16[8,128,384]{2,1,0:T(8,128)(2,1)} %get-tuple-element.78), channel_id=1, source_target_pairs={{0,1},{1,0},{2,3},{3,2},{4,5},{5,4},{6,7},{7,6},{8,9},{9,8},{10,11... | collective-permute-start | bytes 2359304 | tf_op jit(solution)/shard_map/ppermute | solution.py:441
  135.6 7.4 %copy-start.1 = (f32[8,128,384]{2,1,0:T(8,128)S(1)}, f32[8,128,384]{2,1,0:T(8,128)}, u32[]{:S(2)}) copy-start(f32[8,128,384]{2,1,0:T(8,128)} %get-tuple-element.75) | copy-start | bytes 4718596
  135.6 6.8 %collective-permute-start.36 = (bf16[2,112,384]{2,1,0:T(8,128)(2,1)S(1)}, bf16[2,112,384]{2,1,0:T(8,128)(2,1)S(1)}, u32[]{:S(2)}, u32[]{:S(2)}) collective-permute-start(bf16[2,112,384]{2,1,0:T(8,128)(2,1)S(1)} %fusion.12), channel_id=1, source_target_pairs={{0,4},{1,5},{2,6},{3,7},{4,0},{5,1},{6,2},{7,3},{8,12},{9,13},{10,... | collective-permute-start | bytes 516104 | tf_op jit(solution)/shard_map/ppermute | solution.py:441
  135.8 7.0 %collective-permute-start.39 = (bf16[2,112,384]{2,1,0:T(8,128)(2,1)S(1)}, bf16[2,112,384]{2,1,0:T(8,128)(2,1)S(1)}, u32[]{:S(2)}, u32[]{:S(2)}) collective-permute-start(bf16[2,112,384]{2,1,0:T(8,128)(2,1)S(1)} %fusion.11), channel_id=1, source_target_pairs={{0,2},{1,3},{2,0},{3,1},{4,6},{5,7},{6,4},{7,5},{8,10},{9,11},{10,... | collective-permute-start | bytes 516104 | tf_op jit(solution)/shard_map/ppermute | solution.py:441
  142.4 24.8 %collective-permute-start.37 = (bf16[112,384]{1,0:T(8,128)(2,1)S(1)}, bf16[112,384]{1,0:T(8,128)(2,1)S(1)}, u32[]{:S(2)}, u32[]{:S(2)}) collective-permute-start(bf16[112,384]{1,0:T(8,128)(2,1)S(1)} %fusion.17), channel_id=1, source_target_pairs={{0,8},{1,9},{2,10},{3,11},{4,12},{5,13},{6,14},{7,15},{8,16},{9,17... | collective-permute-start | bytes 258056 | tf_op jit(solution)/shard_map/ppermute | solution.py:441
  143.0 4.4 %copy-start = (f32[8,128,384]{2,1,0:T(8,128)S(1)}, f32[8,128,384]{2,1,0:T(8,128)}, u32[]{:S(2)}) copy-start(f32[8,128,384]{2,1,0:T(8,128)} %get-tuple-element.77) | copy-start | bytes 4718596
  143.2 10.4 %collective-permute-start.27 = (bf16[4,128,384]{2,1,0:T(8,128)(2,1)S(1)}, bf16[4,128,384]{2,1,0:T(8,128)(2,1)S(1)}, u32[]{:S(2)}, u32[]{:S(2)}) collective-permute-start(bf16[4,128,384]{2,1,0:T(8,128)(2,1)S(1)} %slice.197), channel_id=1, source_target_pairs={{0,2},{1,3},{2,0},{3,1},{4,6},{5,7},{6,4},{7,5},{8,10},{9,11},{10,... | collective-permute-start | bytes 1179656 | tf_op jit(solution)/shard_map/ppermute | solution.py:441
  143.7 24.7 %collective-permute-start.40 = (bf16[112,384]{1,0:T(8,128)(2,1)S(1)}, bf16[112,384]{1,0:T(8,128)(2,1)S(1)}, u32[]{:S(2)}, u32[]{:S(2)}) collective-permute-start(bf16[112,384]{1,0:T(8,128)(2,1)S(1)} %get-tuple-element.88), channel_id=1, source_target_pairs={{0,16},{1,17},{2,18},{3,19},{4,20},{5,21},{6,22},{7,23},{8,24},{9,... | collective-permute-start | bytes 258056 | tf_op jit(solution)/shard_map/ppermute | solution.py:441
  144.5 23.9 %collective-permute-start.41 = (bf16[112,384]{1,0:T(8,128)(2,1)S(1)}, bf16[112,384]{1,0:T(8,128)(2,1)S(1)}, u32[]{:S(2)}, u32[]{:S(2)}) collective-permute-start(bf16[112,384]{1,0:T(8,128)(2,1)S(1)} %get-tuple-element.89), channel_id=1, source_target_pairs={{0,24},{1,25},{2,26},{3,27},{4,28},{5,29},{6,30},{7,31},{8,0},{9,1... | collective-permute-start | bytes 258056 | tf_op jit(solution)/shard_map/ppermute | solution.py:441
  147.5 12.0 %collective-permute-start.31 = (bf16[4,128,384]{2,1,0:T(8,128)(2,1)S(1)}, bf16[4,128,384]{2,1,0:T(8,128)(2,1)S(1)}, u32[]{:S(2)}, u32[]{:S(2)}) collective-permute-start(bf16[4,128,384]{2,1,0:T(8,128)(2,1)S(1)} %slice.196), channel_id=1, source_target_pairs={{0,4},{1,5},{2,6},{3,7},{4,0},{5,1},{6,2},{7,3},{8,12},{9,13},{10,... | collective-permute-start | bytes 1179656 | tf_op jit(solution)/shard_map/ppermute | solution.py:441
  153.6 8.0 %collective-permute-start.28 = (bf16[2,128,384]{2,1,0:T(8,128)(2,1)S(1)}, bf16[2,128,384]{2,1,0:T(8,128)(2,1)S(1)}, u32[]{:S(2)}, u32[]{:S(2)}) collective-permute-start(bf16[2,128,384]{2,1,0:T(8,128)(2,1)S(1)} %fusion.7), channel_id=1, source_target_pairs={{0,4},{1,5},{2,6},{3,7},{4,0},{5,1},{6,2},{7,3},{8,12},{9,13},{10,... | collective-permute-start | bytes 589832 | tf_op jit(solution)/shard_map/ppermute | solution.py:441
  159.7 5.7 %collective-permute-start.32 = (bf16[2,128,384]{2,1,0:T(8,128)(2,1)S(1)}, bf16[2,128,384]{2,1,0:T(8,128)(2,1)S(1)}, u32[]{:S(2)}, u32[]{:S(2)}) collective-permute-start(bf16[2,128,384]{2,1,0:T(8,128)(2,1)S(1)} %fusion.6), channel_id=1, source_target_pairs={{0,2},{1,3},{2,0},{3,1},{4,6},{5,7},{6,4},{7,5},{8,10},{9,11},{10,... | collective-permute-start | bytes 589832 | tf_op jit(solution)/shard_map/ppermute | solution.py:441
  161.7 7.5 %collective-permute-start.29 = (bf16[128,384]{1,0:T(8,128)(2,1)S(1)}, bf16[128,384]{1,0:T(8,128)(2,1)S(1)}, u32[]{:S(2)}, u32[]{:S(2)}) collective-permute-start(bf16[128,384]{1,0:T(8,128)(2,1)S(1)} %fusion.16), channel_id=1, source_target_pairs={{0,8},{1,9},{2,10},{3,11},{4,12},{5,13},{6,14},{7,15},{8,16},{9,17... | collective-permute-start | bytes 294920 | tf_op jit(solution)/shard_map/ppermute | solution.py:441
  165.5 6.7 %collective-permute-start.33 = (bf16[128,384]{1,0:T(8,128)(2,1)S(1)}, bf16[128,384]{1,0:T(8,128)(2,1)S(1)}, u32[]{:S(2)}, u32[]{:S(2)}) collective-permute-start(bf16[128,384]{1,0:T(8,128)(2,1)S(1)} %get-tuple-element.83), channel_id=1, source_target_pairs={{0,16},{1,17},{2,18},{3,19},{4,20},{5,21},{6,22},{7,23},{8,24},{9,... | collective-permute-start | bytes 294920 | tf_op jit(solution)/shard_map/ppermute | solution.py:441
  167.2 5.6 %collective-permute-start.34 = (bf16[128,384]{1,0:T(8,128)(2,1)S(1)}, bf16[128,384]{1,0:T(8,128)(2,1)S(1)}, u32[]{:S(2)}, u32[]{:S(2)}) collective-permute-start(bf16[128,384]{1,0:T(8,128)(2,1)S(1)} %get-tuple-element.84), channel_id=1, source_target_pairs={{0,24},{1,25},{2,26},{3,27},{4,28},{5,29},{6,30},{7,31},{8,0},{9,1... | collective-permute-start | bytes 294920 | tf_op jit(solution)/shard_map/ppermute | solution.py:441
  (2 other events, 1.3 us)

commit v3 on v2

--- a/solution.py
+++ b/solution.py
@@ -17,8 +17,11 @@
 FACTOR = HEAD_DIM ** (-0.5)
 GELU_A = 0.7978845608028654
 GELU_B = 0.044715
-CHUNK = 512
-PER_STEP = 2
+CHUNK = 1536
+FORWARD_STEP = 2
+MLP_STEP = 2
+ATTEND_STEP = 2
+FINISH_STEP = 2
 
 ADA_AT = 0
 QKV_AT = 6 * D
@@ -197,7 +200,7 @@
     outs = refs[n_pieces : n_pieces + 5 + n_out]
     out_ref, dx_ref, dmixed_ref, dmod_ref, dproj_ref = outs[:5]
     send_refs = outs[5:]
-    rows_ref, fc1_ref, fc2_ref, bias_ref, act_ref, slope_ref, dfc1_ref, dfc2_ref, dbias_ref = refs[
+    rows_ref, fc1_ref, fc2_ref, bias_ref, act_ref, slope_ref, du_ref, dfc1_ref, dfc2_ref, dbias_ref = refs[
         n_pieces + 5 + n_out :
     ]
     step = pl.program_id(0)
@@ -234,7 +237,6 @@
         normed, rstd = normalize(middle)
         modulated = flat(normed * (1.0 + scale) + shift).astype(BF16)
         chunk = CHUNK
-        branch_two = jnp.zeros((group * seq, D), F32)
         for start in range(0, FF, chunk):
             part = slice(start, start + chunk)
             pre = mm(modulated, fc1_ref[:, part]) + bias_ref[0:1, part]
@@ -246,7 +248,7 @@
             slope_ref[:, part] = half + (pre * (0.5 - 0.5 * bend * bend)) * (
                 GELU_A + (3.0 * GELU_A * GELU_B) * square
             )
-            branch_two += mm(act, fc2_ref[part, :])
+        branch_two = mm(act_ref[...], fc2_ref[...])
         branch_two = (branch_two + bias_ref[1:2, :D]).reshape(group, seq, D)
         out_ref[...] = (live * (middle + gate_two * branch_two)).astype(BF16)
         grad_out = live * cot_ref[...].astype(F32)
@@ -255,15 +257,14 @@
         dbias_ref[1:2, :D] += col_sum(grad_two.astype(F32))
         grad_two_t = grad_two.T
         modulated_t = modulated.T
-        grad_mod = jnp.zeros((group * seq, D), F32)
         for start in range(0, FF, chunk):
             part = slice(start, start + chunk)
             du = (mm_nt(grad_two, fc2_ref[part, :]) * slope_ref[:, part]).astype(BF16)
             dbias_ref[0:1, part] += col_sum(du.astype(F32))
-            dfc2_ref[:, part] += mm(grad_two_t, act_ref[:, part])
-            dfc1_ref[:, part] += mm(modulated_t, du)
-            grad_mod += mm_nt(du, fc1_ref[:, part])
-        grad_mod = grad_mod.reshape(group, seq, D)
+            du_ref[:, part] = du
+        grad_mod = mm_nt(du_ref[...], fc1_ref[...]).reshape(group, seq, D)
+        dfc2_ref[...] += mm(grad_two_t, act_ref[...])
+        dfc1_ref[...] += mm(modulated_t, du_ref[...])
         put_mod(dmod_ref, 1, step, grad_mod)
         put_mod(dmod_ref, 2, step, grad_mod * normed)
         grad_middle = grad_out + normalize_back(grad_mod * (1.0 + scale), normed, rstd)
@@ -394,11 +395,17 @@
         self.gathered = self.sent = [jnp.int32(index) for index in range(count)]
         self.slots = [(count, F32)]
 
+    def start(self, piece):
+        return piece
+
     def gather(self, piece):
         return [lax.all_gather(piece, AXIS, axis=0)]
 
     def pass_on(self, held):
         return held
+
+    def join(self, own, others):
+        return own
 
     def begin(self, parts):
         return parts
@@ -417,6 +424,9 @@
         def device(dz, dy, dx, dc):
             return (((z + dz) % 4 * 2 + (y + dy) % 2) * 2 + (x + dx) % 2) * 2 + (core + dc) % 2
 
+        self.order(device)
+
+    def order(self, device):
         gathered = []
         for dc in range(2):
             gathered += [device(-k, 0, 0, dc) for k in (0, 1, 2, 3)]
@@ -440,8 +450,10 @@
             pairs.append((source, target))
         return lax.ppermute(values, AXIS, pairs)
 
-    def gather(self, piece):
-        own = jnp.stack([piece] + [self.shift(piece, dz=k) for k in (1, 2, 3)])
+    def start(self, piece):
+        return jnp.stack([piece] + [self.shift(piece, dz=k) for k in (1, 2, 3)])
+
+    def gather(self, own):
         first, second = own[:2], own[2:]
         by_x = self.shift(first, dx=1)
         by_y = self.shift(second, dy=1)
@@ -482,6 +494,43 @@
         )
 
 
+class Straight(Stages):
+    def order(self, device):
+        sides = [(0, 0), (0, 1), (1, 0), (1, 1)]
+        self.gathered = [device(-k, dy, dx, dc) for dc in (0, 1) for dy, dx in sides for k in range(4)]
+        self.sent = [device(k, dy, dx, dc) for dc in (1, 0) for dy, dx in sides for k in range(4)]
+        self.slots = [(16, BF16), (16, F32)]
+
+    def join(self, own, others):
+        half = len(others) // 2
+        return own[:1] + others[:half] + own[1:] + others[half:]
+
+    def gather(self, own):
+        return [own, self.shift(own, dx=1), self.shift(own, dy=1), self.shift(own, dx=1, dy=1)]
+
+    def begin(self, parts):
+        return self.shift(parts[0], dc=1), parts[1]
+
+    def middle(self, state):
+        got, keep = state
+        total = (keep + got.astype(F32)).reshape((4, 4) + keep.shape[1:])
+        return total[0], total[1].astype(BF16), total[2].astype(BF16), total[3].astype(BF16)
+
+    def send(self, state):
+        total, by_x, by_y, by_both = state
+        return total, self.shift(by_x, dx=1), self.shift(by_y, dy=1), self.shift(by_both, dx=1, dy=1)
+
+    def end(self, state):
+        total = state[0]
+        for got in state[1:]:
+            total = total + got.astype(F32)
+        low = total[1:].astype(BF16)
+        out = total[0]
+        for k in (1, 2, 3):
+            out = out + self.shift(low[k - 1], dz=k).astype(F32)
+        return out
+
+
 def to_piece(share, rows, me):
     size = share.shape[0]
     flat = jnp.zeros((rows * D,), share.dtype)
@@ -496,9 +545,9 @@
     return pl.BlockSpec(memory_space=pltpu.VMEM)
 
 
-def by_latent(*shape):
+def by_latent(group, *shape):
     zeros = (0,) * len(shape)
-    return pl.BlockSpec((PER_STEP,) + shape, lambda step, scal: (step,) + zeros)
+    return pl.BlockSpec((group,) + shape, lambda step, scal: (step,) + zeros)
 
 
 def call(kernel, count, in_specs, out_specs, out_shape, scratch, args, flops):
@@ -525,35 +574,44 @@
     def body(latents, condition, attn_params, mlp_params, counts, cotangent):
         count, seq = latents.shape[0], latents.shape[1]
         me = lax.axis_index(AXIS)
-        plan = (Stages if devices == 32 else Direct)(devices, me)
+        known = devices == 32
+        plan = (Stages if known else Direct)(devices, me)
+        mlp_plan = (Straight if known else Direct)(devices, me)
         attn_size, mlp_size = attn_params.shape[0], mlp_params.shape[0]
         attn_height = piece_rows(attn_size, devices)
         mlp_height = piece_rows(mlp_size, devices)
 
-        def scalars(size):
-            ids = jnp.stack(plan.gathered + plan.sent)
+        def scalars(size, order):
+            ids = jnp.stack(order.gathered + order.sent)
             return jnp.concatenate([counts.astype(jnp.int32), size * ids // GROUP]).astype(jnp.int32)
 
-        attn_scal, mlp_scal = scalars(attn_size), scalars(mlp_size)
-        attn_pieces = plan.pass_on(plan.gather(to_piece(attn_params, attn_height, me)))
-        mlp_pieces = plan.gather(to_piece(mlp_params, mlp_height, me))
+        attn_scal, mlp_scal = scalars(attn_size, plan), scalars(mlp_size, mlp_plan)
+        attn_own, mlp_piece = plan.start(to_piece(attn_params, attn_height, me)), to_piece(mlp_params, mlp_height, me)
+        attn_own, mlp_piece = lax.optimization_barrier((attn_own, mlp_piece))
+        attn_pieces = plan.gather(attn_own)
+        mlp_own = mlp_plan.start(mlp_piece)
+        mlp_own, attn_pieces, attn_scal, mlp_scal = lax.optimization_barrier(
+            (mlp_own, attn_pieces, attn_scal, mlp_scal)
+        )
+        attn_pieces = plan.pass_on(attn_pieces)
+        mlp_pieces = mlp_plan.gather(mlp_own)
 
         def struct(shape, kind):
             return jax.ShapeDtypeStruct(shape, kind)
 
         n_pieces = len(attn_pieces)
-        n_out = len(plan.slots)
-        steps = count // PER_STEP
+        n_mlp_pieces = len(mlp_pieces) * (2 if known else 1)
+        n_out, n_mlp_out = len(plan.slots), len(mlp_plan.slots)
         mod, ada, qkv_w, proj, _, qkv, probs, mixed, branch = call(
             lambda *refs: forward_kernel(n_pieces, *refs),
-            steps,
-            [whole(), by_latent(seq, D)] + [whole()] * n_pieces,
+            count // FORWARD_STEP,
+            [whole(), by_latent(FORWARD_STEP, seq, D)] + [whole()] * n_pieces,
             [whole()] * 5
             + [
-                by_latent(seq, 3 * D),
-                by_latent(HEADS, seq, seq),
-                by_latent(D, seq),
-                by_latent(seq, D),
+                by_latent(FORWARD_STEP, seq, 3 * D),
+                by_latent(FORWARD_STEP, HEADS, seq, seq),
+                by_latent(FORWARD_STEP, D, seq),
+                by_latent(FORWARD_STEP, seq, D),
             ],
             [
                 struct((6, count, D), F32),
@@ -568,20 +626,21 @@
             ],
             [
                 pltpu.VMEM((TILES, ATTN_ROWS + attn_height, LANES), F32),
-                pltpu.VMEM((PER_STEP, HEADS, seq, seq), F32),
+                pltpu.VMEM((FORWARD_STEP, HEADS, seq, seq), F32),
             ],
             [attn_scal, condition, latents] + attn_pieces,
             15 * 10**9,
         )
-        mlp_pieces, mod = lax.optimization_barrier((mlp_pieces, mod))
-        mlp_pieces = plan.pass_on(mlp_pieces)
+        mlp_own = mlp_plan.pass_on(mlp_pieces[:1])
+        mlp_pieces, mod = lax.optimization_barrier((mlp_pieces[1:], mod))
+        mlp_pieces = mlp_plan.join(mlp_own, mlp_plan.pass_on(mlp_pieces))
         results = call(
-            lambda *refs: mlp_kernel(n_pieces, n_out, *refs),
-            steps,
-            [whole(), whole(), by_latent(seq, D), by_latent(seq, D), by_latent(D, seq), by_latent(seq, D)]
-            + [whole()] * n_pieces,
-            [by_latent(seq, D), by_latent(seq, D), by_latent(seq, D), whole(), whole()]
-            + [whole()] * n_out,
+            lambda *refs: mlp_kernel(n_mlp_pieces, n_mlp_out, *refs),
+            count // MLP_STEP,
+            [whole(), whole(), by_latent(MLP_STEP, seq, D), by_latent(MLP_STEP, seq, D), by_latent(MLP_STEP, D, seq), by_latent(MLP_STEP, seq, D)]
+            + [whole()] * n_mlp_pieces,
+            [by_latent(MLP_STEP, seq, D), by_latent(MLP_STEP, seq, D), by_latent(MLP_STEP, seq, D), whole(), whole()]
+            + [whole()] * n_mlp_out,
             [
                 struct((count, seq, D), BF16),
                 struct((count, seq, D), F32),
@@ -589,14 +648,15 @@
                 struct((4, count, D), F32),
                 struct((D, D), F32),
             ]
-            + [struct((slots, mlp_height, D), kind) for slots, kind in plan.slots],
+            + [struct((slots, mlp_height, D), kind) for slots, kind in mlp_plan.slots],
             [
                 pltpu.VMEM((TILES, MLP_ROWS + 2 + mlp_height, LANES), F32),
                 pltpu.VMEM((D, FF), BF16),
                 pltpu.VMEM((FF, D), BF16),
                 pltpu.VMEM((8, FF), F32),
-                pltpu.VMEM((PER_STEP * seq, FF), BF16),
-                pltpu.VMEM((PER_STEP * seq, FF), F32),
+                pltpu.VMEM((MLP_STEP * seq, FF), BF16),
+                pltpu.VMEM((MLP_STEP * seq, FF), F32),
+                pltpu.VMEM((MLP_STEP * seq, FF), BF16),
                 pltpu.VMEM((D, FF), F32),
                 pltpu.VMEM((D, FF), F32),
                 pltpu.VMEM((8, FF), F32),
@@ -605,12 +665,12 @@
             30 * 10**9,
         )
         output, grad_middle, grad_mixed, dmod, dproj = results[:5]
-        sums = plan.begin(results[5:])
+        sums = mlp_plan.begin(results[5:])
         grad_qkv, = call(
             attend_back_kernel,
-            steps,
-            [by_latent(seq, 3 * D), by_latent(HEADS, seq, seq), by_latent(seq, D)],
-            [by_latent(seq, 3 * D)],
+            count // ATTEND_STEP,
+            [by_latent(ATTEND_STEP, seq, 3 * D), by_latent(ATTEND_STEP, HEADS, seq, seq), by_latent(ATTEND_STEP, seq, D)],
+            [by_latent(ATTEND_STEP, seq, 3 * D)],
             [struct((count, seq, 3 * D), BF16)],
             [
                 pltpu.VMEM((HEADS, seq, seq), F32),
@@ -621,14 +681,14 @@
             13 * 10**9,
         )
         sums, grad_qkv = lax.optimization_barrier((sums, grad_qkv))
-        sums = plan.middle(sums)
+        sums = mlp_plan.middle(sums)
         sums, grad_qkv = lax.optimization_barrier((sums, grad_qkv))
-        sums = plan.send(sums)
+        sums = mlp_plan.send(sums)
         results = call(
             lambda *refs: finish_kernel(n_out, 1 + devices, *refs),
-            steps,
-            [whole()] * 6 + [by_latent(seq, D), by_latent(seq, 3 * D), by_latent(seq, D)],
-            [by_latent(seq, D), whole()] + [whole()] * n_out,
+            count // FINISH_STEP,
+            [whole()] * 6 + [by_latent(FINISH_STEP, seq, D), by_latent(FINISH_STEP, seq, 3 * D), by_latent(FINISH_STEP, seq, D)],
+            [by_latent(FINISH_STEP, seq, D), whole()] + [whole()] * n_out,
             [struct((count, seq, D), F32), struct((count, D), F32)]
             + [struct((slots, attn_height, D), kind) for slots, kind in plan.slots],
             [
@@ -641,8 +701,9 @@
             15 * 10**9,
         )
         grad_latents, grad_condition = results[:2]
-        grad_mlp = plan.end(sums)
-        grad_attn = plan.end(plan.send(plan.middle(plan.begin(results[2:]))))
+        sums, attn_parts = lax.optimization_barrier((sums, results[2:]))
+        grad_attn = plan.end(plan.send(plan.middle(plan.begin(attn_parts))))
+        grad_mlp = mlp_plan.end(sums)
         return (
             output,
             grad_latents,

time: 173 us -> 164 us (0.948)
  starting transfers between devices: 35.7 us -> 63.7 us
  Pallas kernels: 82.3 us -> 55 us
  waiting for transfers between devices: 44.1 us -> 34.2 us
    ppermute x42 -> x38, starting transfers between devices: 35.7 us -> 63.7 us  [shift(): return lax.ppermute(values, AXIS, pairs)]
    pallas_call x4, Pallas kernels: 82.3 us -> 55 us  [call(): pl.pallas_call(kernel, grid_spec=pltpu.PrefetchScalarGridSpec(num_scalar_...]
    ppermute x42 -> x38, waiting for transfers between devices: 44.1 us -> 34.2 us  [shift(): return lax.ppermute(values, AXIS, pairs)]
  transfers between devices with their start and end apart: 42 -> 38, of which waited for: 17 -> 21; matrix products, arithmetic and copies ran while one was open for 3% -> 3% of each run, Pallas kernels for 27% -> 22%
where the time goes in v3:
time: 164 us; the launch traced here: 165 us
  starting transfers between devices  63.7 us (39%)
  Pallas kernels  55 us (34%)
  waiting for transfers between devices  34.2 us (21%)
  local copies, waits for them, and re-layouts  7.92 us (5%)
  other arithmetic  1.99 us (1%)
  between operations  1.78 us (1%)
    ppermute x38, starting transfers between devices, shift(): return lax.ppermute(values, AXIS, pairs)  63.7 us
    pallas_call x4, Pallas kernels, call(): pl.pallas_call(kernel, grid_spec=pltpu.PrefetchScalarGridSpec(num_scalar_...  55 us
    ppermute x38, waiting for transfers between devices, shift(): return lax.ppermute(values, AXIS, pairs)  34.2 us
    dynamic_update_slice x2, local copies, waits for them, and re-layouts, to_piece(): lax.dynamic_update_slice(flat, share, (size * me % GROUP,)).reshape(rows, D)  3.89 us
  transfers between devices with their start and end apart: 38, of which 21 were waited for; matrix products, arithmetic and copies ran while one was open for 3% of the time, Pallas kernels for 22%

profile of v3, /device:TPU:0, one launch (start us, length us, event | category | flops | bytes accessed | tf_op | source)
XLA Modules:
  0.0 164.6 jit_solution(15651857032554214403)
XLA Ops:
  0.7 2.0 %dynamic_update_slice.6 = bf16[49152]{0:T(1024)(128)(2,1)S(1)} dynamic-update-slice(bf16[49152]{0:T(1024)(128)(2,1)S(1)} %broadcast_in_dim.6, bf16[46176]{0:T(1024)(128)(2,1)} %param.8, s32[]{:T(128)S(6)} %select_n.1113) | dynamic-update-slice | bytes 184708 | tf_op jit(solution)/shard_map/dynamic_update_slice | solution.py:537
  2.7 5.1 %collective-permute-start.2 = (bf16[128,384]{1,0:T(8,128)(2,1)S(1)}, bf16[128,384]{1,0:T(8,128)(2,1)S(1)}, u32[]{:S(2)}, u32[]{:S(2)}) collective-permute-start(bf16[128,384]{1,0:T(8,128)(2,1)S(1)} %reshape.52), channel_id=1, source_target_pairs={{0,24},{1,25},{2,26},{3,27},{4,28},{5,29},{6,30},{7,31},{8,0},{9,1... | collective-permute-start | bytes 294920 | tf_op jit(solution)/shard_map/ppermute | solution.py:451
  7.8 1.0 collective-permute-start
  8.9 1.9 %dynamic_update_slice.7 = bf16[43008]{0:T(1024)(128)(2,1)S(1)} dynamic-update-slice(bf16[43008]{0:T(1024)(128)(2,1)S(1)} %broadcast_in_dim.7, bf16[36936]{0:T(1024)(128)(2,1)} %param.9, s32[]{:T(128)S(6)} %select_n.1115) | dynamic-update-slice | bytes 147748 | tf_op jit(solution)/shard_map/dynamic_update_slice | solution.py:537
  10.9 0.1 stack.338
  11.1 5.5 %collective-permute-done.1 = bf16[128,384]{1,0:T(8,128)(2,1)S(1)} collective-permute-done((bf16[128,384]{1,0:T(8,128)(2,1)S(1)}, bf16[128,384]{1,0:T(8,128)(2,1)S(1)}, u32[]{:S(2)}, u32[]{:S(2)}) %collective-permute-start.1) | collective-permute-done | bytes 98336 | tf_op jit(solution)/shard_map/ppermute | solution.py:451
  16.7 1.6 collective-permute-start.7
  18.3 1.5 collective-permute-start.6
  19.8 0.2 stack.339
  20.6 3.7 %collective-permute-done.6.refs_4_ = bf16[2,128,384]{2,1,0:T(8,128)(2,1)S(1)} collective-permute-done((bf16[2,128,384]{2,1,0:T(8,128)(2,1)S(1)}, bf16[2,128,384]{2,1,0:T(8,128)(2,1)S(1)}, u32[]{:S(2)}, u32[]{:S(2)}) %collective-permute-start.6) | collective-permute-done | bytes 196640 | tf_op jit(solution)/shard_map/ppermute | solution.py:451
  24.4 0.6 collective-permute-start.8
  25.0 1.6 collective-permute-start.9
  26.6 1.6 collective-permute-start.5
  28.2 0.5 collective-permute-start.4
  28.7 1.9 %collective-permute-start.3 = (bf16[112,384]{1,0:T(8,128)(2,1)S(1)}, bf16[112,384]{1,0:T(8,128)(2,1)S(1)}, u32[]{:S(2)}, u32[]{:S(2)}) collective-permute-start(bf16[112,384]{1,0:T(8,128)(2,1)S(1)} %reshape.53), channel_id=1, source_target_pairs={{0,8},{1,9},{2,10},{3,11},{4,12},{5,13},{6,14},{7,15},{8,16},{9,17... | collective-permute-start | bytes 258056 | tf_op jit(solution)/shard_map/ppermute | solution.py:451
  30.7 0.7 pad_add_fusion
  31.3 0.7 collective-permute-done.5
  32.1 3.3 %collective-permute-done.4 = bf16[112,384]{1,0:T(8,128)(2,1)S(1)} collective-permute-done((bf16[112,384]{1,0:T(8,128)(2,1)S(1)}, bf16[112,384]{1,0:T(8,128)(2,1)S(1)}, u32[]{:S(2)}, u32[]{:S(2)}) %collective-permute-start.4) | collective-permute-done | bytes 86048 | tf_op jit(solution)/shard_map/ppermute | solution.py:451
  35.5 0.5 collective-permute-start.16
  36.1 0.4 collective-permute-start.14
  36.6 2.0 %collective-permute-done.14.refs_9_ = bf16[2,128,384]{2,1,0:T(8,128)(2,1)S(1)} collective-permute-done((bf16[2,128,384]{2,1,0:T(8,128)(2,1)S(1)}, bf16[2,128,384]{2,1,0:T(8,128)(2,1)S(1)}, u32[]{:S(2)}, u32[]{:S(2)}) %collective-permute-start.14) | collective-permute-done | bytes 196640 | tf_op jit(solution)/shard_map/ppermute | solution.py:451
  38.8 0.1 collective-permute-done.15.refs_10_
  38.9 1.5 collective-permute-start.12
  40.4 0.5 collective-permute-start.11
  40.9 1.6 collective-permute-start.10
  42.6 0.8 copy-done.11
  43.3 13.9 %shard_map.101 = (f32[6,8,384]{2,1,0:T(8,128)}, bf16[6,384,384]{2,1,0:T(8,128)(2,1)}, bf16[384,1152]{1,0:T(8,128)(2,1)}, bf16[384,384]{1,0:T(8,128)(2,1)}, f32[8...) custom-call(s32[65]{0:T(128)} %get-tuple-element.60.refs_0_.scal_ref, ...), custom_call_target="tpu_custom_call" | custom-call | flops 15000000512 | bytes 20971520 | tf_op jit(solution)/shard_map/pallas_call | solution.py:554
  57.3 0.2 collective-permute-done.11.refs_9_
  57.6 2.5 %collective-permute-start.19 = (bf16[4,112,384]{2,1,0:T(8,128)(2,1)}, bf16[4,112,384]{2,1,0:T(8,128)(2,1)S(1)}, u32[]{:S(2)}, u32[]{:S(2)}) collective-permute-start(bf16[4,112,384]{2,1,0:T(8,128)(2,1)} %collective-permute-done.10.refs_8_), channel_id=1, source_target_pairs={{0,1},{1,0},{2,3},{3,2},{4,5},{5,4},{6,7},{7,6},{8,9},{9,8},{10,11... | collective-permute-start | bytes 1032200 | tf_op jit(solution)/shard_map/ppermute | solution.py:451
  60.2 0.4 collective-permute-start.21
  60.6 1.0 collective-permute-done.19.refs_12_
  61.6 0.5 collective-permute-done.20.refs_13_
  62.1 0.3 collective-permute-done.21.refs_14_
  62.4 0.4 copy-done.15
  62.8 0.3 copy-done.16
  63.1 18.5 %shard_map.102 = (bf16[8,256,384]{2,1,0:T(8,128)(2,1)}, f32[8,256,384]{2,1,0:T(8,128)}, bf16[8,256,384]{2,1,0:T(8,128)(2,1)}, f32[4,8,384]{2,1,0:T(8,128)}, f32[...) custom-call(s32[65]{0:T(128)} %get-tuple-element.58.refs_0_, ...), custom_call_target="tpu_custom_call" | custom-call | flops 30000001024 | bytes 20971520 | tf_op jit(solution)/shard_map/pallas_call | solution.py:554
  81.7 9.2 %collective-permute-start.22 = (bf16[16,112,384]{2,1,0:T(8,128)(2,1)}, bf16[16,112,384]{2,1,0:T(8,128)(2,1)S(1)}, u32[]{:S(2)}, u32[]{:S(2)}) collective-permute-start(bf16[16,112,384]{2,1,0:T(8,128)(2,1)} %get-tuple-element.79), channel_id=1, source_target_pairs={{0,1},{1,0},{2,3},{3,2},{4,5},{5,4},{6,7},{7,6},{8,9},{9,8},{10,11... | collective-permute-start | bytes 4128776 | tf_op jit(solution)/shard_map/ppermute | solution.py:451
  90.9 9.7 %shard_map.103.refs_8_ = bf16[8,256,1152]{2,1,0:T(8,128)(2,1)} custom-call(s32[65]{0:T(128)} %get-tuple-element.60.refs_0_.scal_ref, bf16[8,256,1152]{2,1,0:T(8,128)(2,1)} %get-tuple-element.81.qkv_ref, bf16[8,6,256,256]{3,2,1,0:T(8,128)(2,1)} %get-tuple-element.82.probs_ref, bf16[8,256,384]{2,1,0:T(8,128)(2,1)} %get-tuple-element.83.dmixed_ref), custom_call_target="tpu_custom_call" | custom-call | flops 12999999488 | bytes 20971520 | tf_op jit(solution)/shard_map/pallas_call | solution.py:554
  100.6 0.3 fusion.13
  101.1 2.3 %collective-permute-start.23 = (bf16[4,112,384]{2,1,0:T(8,128)(2,1)S(1)}, bf16[4,112,384]{2,1,0:T(8,128)(2,1)S(1)}, u32[]{:S(2)}, u32[]{:S(2)}) collective-permute-start(bf16[4,112,384]{2,1,0:T(8,128)(2,1)S(1)} %get-tuple-element.92), channel_id=1, source_target_pairs={{0,2},{1,3},{2,0},{3,1},{4,6},{5,7},{6,4},{7,5},{8,10},{9,11},{10,... | collective-permute-start | bytes 1032200 | tf_op jit(solution)/shard_map/ppermute | solution.py:451
  103.3 10.1 %collective-permute-start.24 = (bf16[4,112,384]{2,1,0:T(8,128)(2,1)S(1)}, bf16[4,112,384]{2,1,0:T(8,128)(2,1)S(1)}, u32[]{:S(2)}, u32[]{:S(2)}) collective-permute-start(bf16[4,112,384]{2,1,0:T(8,128)(2,1)S(1)} %get-tuple-element.93), channel_id=1, source_target_pairs={{0,4},{1,5},{2,6},{3,7},{4,0},{5,1},{6,2},{7,3},{8,12},{9,13},{10,... | collective-permute-start | bytes 1032200 | tf_op jit(solution)/shard_map/ppermute | solution.py:451
  113.4 1.4 collective-permute-start.25
  114.8 12.9 %shard_map.104 = (f32[8,256,384]{2,1,0:T(8,128)}, f32[8,384]{1,0:T(8,128)}, bf16[8,128,384]{2,1,0:T(8,128)(2,1)}, bf16[8,128,384]{2,1,0:T(8,128)(2,1)}, f32[8,128,384]{2,1,0:T(8,128)}, /*index=5*/f32[8,128,384]{2,1,0:T(8,128)}) custom-call(s32[65]{0:T(128)} %get-tuple-element.60.refs_0_.scal_ref, f32[6,8,384]{2,1,0:T(8,128)} %get-tuple-element.67.refs_1_, ...), custom_call_target="tpu_custom_call" | custom-call | flops 15000000512 | bytes 20971520 | tf_op jit(solution)/shard_map/pallas_call | solution.py:554
  127.6 0.6 collective-permute-done.24
  128.2 0.7 collective-permute-done.25
  129.0 0.5 collective-permute-start.30
  129.5 0.2 fusion.12
  129.7 1.8 %collective-permute-done.26 = bf16[8,128,384]{2,1,0:T(8,128)(2,1)S(1)} collective-permute-done((bf16[8,128,384]{2,1,0:T(8,128)(2,1)}, bf16[8,128,384]{2,1,0:T(8,128)(2,1)S(1)}, u32[]{:S(2)}, u32[]{:S(2)}) %collective-permute-start.26) | collective-permute-done | bytes 786464 | tf_op jit(solution)/shard_map/ppermute | solution.py:451
  131.7 1.5 collective-permute-start.27
  133.3 3.8 %collective-permute-start.37 = (bf16[112,384]{1,0:T(8,128)(2,1)S(1)}, bf16[112,384]{1,0:T(8,128)(2,1)S(1)}, u32[]{:S(2)}, u32[]{:S(2)}) collective-permute-start(bf16[112,384]{1,0:T(8,128)(2,1)S(1)} %get-tuple-element.117), channel_id=1, source_target_pairs={{0,24},{1,25},{2,26},{3,27},{4,28},{5,29},{6,30},{7,31},{8,0},{9,1... | collective-permute-start | bytes 258056 | tf_op jit(solution)/shard_map/ppermute | solution.py:451
  137.3 2.3 %collective-permute-start.31 = (bf16[4,128,384]{2,1,0:T(8,128)(2,1)S(1)}, bf16[4,128,384]{2,1,0:T(8,128)(2,1)S(1)}, u32[]{:S(2)}, u32[]{:S(2)}) collective-permute-start(bf16[4,128,384]{2,1,0:T(8,128)(2,1)S(1)} %slice.165), channel_id=1, source_target_pairs={{0,4},{1,5},{2,6},{3,7},{4,0},{5,1},{6,2},{7,3},{8,12},{9,13},{10,... | collective-permute-start | bytes 1179656 | tf_op jit(solution)/shard_map/ppermute | solution.py:451
  139.6 3.3 %collective-permute-done.27 = bf16[4,128,384]{2,1,0:T(8,128)(2,1)S(1)} collective-permute-done((bf16[4,128,384]{2,1,0:T(8,128)(2,1)S(1)}, bf16[4,128,384]{2,1,0:T(8,128)(2,1)S(1)}, u32[]{:S(2)}, u32[]{:S(2)}) %collective-permute-start.27) | collective-permute-done | bytes 393248 | tf_op jit(solution)/shard_map/ppermute | solution.py:451
  143.0 3.7 %collective-permute-start.28 = (bf16[2,128,384]{2,1,0:T(8,128)(2,1)S(1)}, bf16[2,128,384]{2,1,0:T(8,128)(2,1)S(1)}, u32[]{:S(2)}, u32[]{:S(2)}) collective-permute-start(bf16[2,128,384]{2,1,0:T(8,128)(2,1)S(1)} %fusion.4), channel_id=1, source_target_pairs={{0,4},{1,5},{2,6},{3,7},{4,0},{5,1},{6,2},{7,3},{8,12},{9,13},{10,... | collective-permute-start | bytes 589832 | tf_op jit(solution)/shard_map/ppermute | solution.py:451
  146.7 2.9 %collective-permute-done.31 = bf16[4,128,384]{2,1,0:T(8,128)(2,1)S(1)} collective-permute-done((bf16[4,128,384]{2,1,0:T(8,128)(2,1)S(1)}, bf16[4,128,384]{2,1,0:T(8,128)(2,1)S(1)}, u32[]{:S(2)}, u32[]{:S(2)}) %collective-permute-start.31) | collective-permute-done | bytes 393248 | tf_op jit(solution)/shard_map/ppermute | solution.py:451
  149.7 2.1 %collective-permute-start.32 = (bf16[2,128,384]{2,1,0:T(8,128)(2,1)S(1)}, bf16[2,128,384]{2,1,0:T(8,128)(2,1)S(1)}, u32[]{:S(2)}, u32[]{:S(2)}) collective-permute-start(bf16[2,128,384]{2,1,0:T(8,128)(2,1)S(1)} %fusion.3), channel_id=1, source_target_pairs={{0,2},{1,3},{2,0},{3,1},{4,6},{5,7},{6,4},{7,5},{8,10},{9,11},{10,... | collective-permute-start | bytes 589832 | tf_op jit(solution)/shard_map/ppermute | solution.py:451
  151.8 0.9 collective-permute-done.28
  152.7 0.6 collective-permute-start.29
  153.3 2.1 %collective-permute-done.32 = bf16[2,128,384]{2,1,0:T(8,128)(2,1)S(1)} collective-permute-done((bf16[2,128,384]{2,1,0:T(8,128)(2,1)S(1)}, bf16[2,128,384]{2,1,0:T(8,128)(2,1)S(1)}, u32[]{:S(2)}, u32[]{:S(2)}) %collective-permute-start.32) | collective-permute-done | bytes 196640 | tf_op jit(solution)/shard_map/ppermute | solution.py:451
  155.5 3.0 %collective-permute-start.33 = (bf16[128,384]{1,0:T(8,128)(2,1)S(1)}, bf16[128,384]{1,0:T(8,128)(2,1)S(1)}, u32[]{:S(2)}, u32[]{:S(2)}) collective-permute-start(bf16[128,384]{1,0:T(8,128)(2,1)S(1)} %get-tuple-element.119), channel_id=1, source_target_pairs={{0,16},{1,17},{2,18},{3,19},{4,20},{5,21},{6,22},{7,23},{8,24},{9,... | collective-permute-start | bytes 294920 | tf_op jit(solution)/shard_map/ppermute | solution.py:451
  158.6 0.8 dynamic_slice.7
  159.4 0.8 collective-permute-done.29
  160.2 3.2 %collective-permute-done.33 = bf16[128,384]{1,0:T(8,128)(2,1)S(1)} collective-permute-done((bf16[128,384]{1,0:T(8,128)(2,1)S(1)}, bf16[128,384]{1,0:T(8,128)(2,1)S(1)}, u32[]{:S(2)}, u32[]{:S(2)}) %collective-permute-start.33) | collective-permute-done | bytes 98336 | tf_op jit(solution)/shard_map/ppermute | solution.py:451
  163.3 0.4 collective-permute-done.34
  163.8 0.8 dynamic_slice.6
  (94 shorter events, 2.2 us)
Async XLA Ops:
  2.7 8.3 %collective-permute-start.2 = (bf16[128,384]{1,0:T(8,128)(2,1)S(1)}, bf16[128,384]{1,0:T(8,128)(2,1)S(1)}, u32[]{:S(2)}, u32[]{:S(2)}) collective-permute-start(bf16[128,384]{1,0:T(8,128)(2,1)S(1)} %reshape.52), channel_id=1, source_target_pairs={{0,24},{1,25},{2,26},{3,27},{4,28},{5,29},{6,30},{7,31},{8,0},{9,1... | collective-permute-start | bytes 294920 | tf_op jit(solution)/shard_map/ppermute | solution.py:451
  7.8 8.8 %collective-permute-start.1 = (bf16[128,384]{1,0:T(8,128)(2,1)S(1)}, bf16[128,384]{1,0:T(8,128)(2,1)S(1)}, u32[]{:S(2)}, u32[]{:S(2)}) collective-permute-start(bf16[128,384]{1,0:T(8,128)(2,1)S(1)} %reshape.52), channel_id=1, source_target_pairs={{0,16},{1,17},{2,18},{3,19},{4,20},{5,21},{6,22},{7,23},{8,24},{9,... | collective-permute-start | bytes 294920 | tf_op jit(solution)/shard_map/ppermute | solution.py:451
  7.8 8.8 %collective-permute-start = (bf16[128,384]{1,0:T(8,128)(2,1)S(1)}, bf16[128,384]{1,0:T(8,128)(2,1)S(1)}, u32[]{:S(2)}, u32[]{:S(2)}) collective-permute-start(bf16[128,384]{1,0:T(8,128)(2,1)S(1)} %reshape.52), channel_id=1, source_target_pairs={{0,8},{1,9},{2,10},{3,11},{4,12},{5,13},{6,14},{7,15},{8,16},{9,17... | collective-permute-start | bytes 294920 | tf_op jit(solution)/shard_map/ppermute | solution.py:451
  16.6 25.9 %copy-start.1 = (bf16[4,128,384]{2,1,0:T(8,128)(2,1)}, bf16[4,128,384]{2,1,0:T(8,128)(2,1)S(1)}, u32[]{:S(2)}) copy-start(bf16[4,128,384]{2,1,0:T(8,128)(2,1)S(1)} %pad_maximum_fusion.refs_3_) | copy-start | bytes 1179652
  16.7 8.3 %collective-permute-start.7 = (bf16[2,128,384]{2,1,0:T(8,128)(2,1)S(1)}, bf16[2,128,384]{2,1,0:T(8,128)(2,1)S(1)}, u32[]{:S(2)}, u32[]{:S(2)}) collective-permute-start(bf16[2,128,384]{2,1,0:T(8,128)(2,1)S(1)} %get-tuple-element.114), channel_id=1, source_target_pairs={{0,4},{1,5},{2,6},{3,7},{4,0},{5,1},{6,2},{7,3},{8,12},{9,13},{10,... | collective-permute-start | bytes 589832 | tf_op jit(solution)/shard_map/ppermute | solution.py:451
  18.3 6.1 %collective-permute-start.6 = (bf16[2,128,384]{2,1,0:T(8,128)(2,1)S(1)}, bf16[2,128,384]{2,1,0:T(8,128)(2,1)S(1)}, u32[]{:S(2)}, u32[]{:S(2)}) collective-permute-start(bf16[2,128,384]{2,1,0:T(8,128)(2,1)S(1)} %get-tuple-element.115), channel_id=1, source_target_pairs={{0,2},{1,3},{2,0},{3,1},{4,6},{5,7},{6,4},{7,5},{8,10},{9,11},{10,... | collective-permute-start | bytes 589832 | tf_op jit(solution)/shard_map/ppermute | solution.py:451
  24.3 18.2 %copy-start.6 = (bf16[2,128,384]{2,1,0:T(8,128)(2,1)}, bf16[2,128,384]{2,1,0:T(8,128)(2,1)S(1)}, u32[]{:S(2)}) copy-start(bf16[2,128,384]{2,1,0:T(8,128)(2,1)S(1)} %collective-permute-done.6.refs_4_) | copy-start | bytes 589828
  24.4 11.0 %collective-permute-start.8 = (bf16[4,128,384]{2,1,0:T(8,128)(2,1)S(1)}, bf16[4,128,384]{2,1,0:T(8,128)(2,1)S(1)}, u32[]{:S(2)}, u32[]{:S(2)}) collective-permute-start(bf16[4,128,384]{2,1,0:T(8,128)(2,1)S(1)} %pad_maximum_fusion.1), channel_id=1, source_target_pairs={{0,4},{1,5},{2,6},{3,7},{4,0},{5,1},{6,2},{7,3},{8,12},{9,13},{10,... | collective-permute-start | bytes 1179656 | tf_op jit(solution)/shard_map/ppermute | solution.py:451
  25.0 17.5 %copy-start.5 = (bf16[2,128,384]{2,1,0:T(8,128)(2,1)}, bf16[2,128,384]{2,1,0:T(8,128)(2,1)S(1)}, u32[]{:S(2)}) copy-start(bf16[2,128,384]{2,1,0:T(8,128)(2,1)S(1)} %collective-permute-done.7.refs_5_) | copy-start | bytes 589828
  25.0 10.4 %collective-permute-start.9 = (bf16[4,128,384]{2,1,0:T(8,128)(2,1)S(1)}, bf16[4,128,384]{2,1,0:T(8,128)(2,1)S(1)}, u32[]{:S(2)}, u32[]{:S(2)}) collective-permute-start(bf16[4,128,384]{2,1,0:T(8,128)(2,1)S(1)} %pad_maximum_fusion.2), channel_id=1, source_target_pairs={{0,2},{1,3},{2,0},{3,1},{4,6},{5,7},{6,4},{7,5},{8,10},{9,11},{10,... | collective-permute-start | bytes 1179656 | tf_op jit(solution)/shard_map/ppermute | solution.py:451
  26.6 5.5 %collective-permute-start.5 = (bf16[112,384]{1,0:T(8,128)(2,1)S(1)}, bf16[112,384]{1,0:T(8,128)(2,1)S(1)}, u32[]{:S(2)}, u32[]{:S(2)}) collective-permute-start(bf16[112,384]{1,0:T(8,128)(2,1)S(1)} %reshape.53), channel_id=1, source_target_pairs={{0,24},{1,25},{2,26},{3,27},{4,28},{5,29},{6,30},{7,31},{8,0},{9,1... | collective-permute-start | bytes 258056 | tf_op jit(solution)/shard_map/ppermute | solution.py:451
  28.2 7.1 %collective-permute-start.4 = (bf16[112,384]{1,0:T(8,128)(2,1)S(1)}, bf16[112,384]{1,0:T(8,128)(2,1)S(1)}, u32[]{:S(2)}, u32[]{:S(2)}) collective-permute-start(bf16[112,384]{1,0:T(8,128)(2,1)S(1)} %reshape.53), channel_id=1, source_target_pairs={{0,16},{1,17},{2,18},{3,19},{4,20},{5,21},{6,22},{7,23},{8,24},{9,... | collective-permute-start | bytes 258056 | tf_op jit(solution)/shard_map/ppermute | solution.py:451
  28.7 6.6 %collective-permute-start.3 = (bf16[112,384]{1,0:T(8,128)(2,1)S(1)}, bf16[112,384]{1,0:T(8,128)(2,1)S(1)}, u32[]{:S(2)}, u32[]{:S(2)}) collective-permute-start(bf16[112,384]{1,0:T(8,128)(2,1)S(1)} %reshape.53), channel_id=1, source_target_pairs={{0,8},{1,9},{2,10},{3,11},{4,12},{5,13},{6,14},{7,15},{8,16},{9,17... | collective-permute-start | bytes 258056 | tf_op jit(solution)/shard_map/ppermute | solution.py:451
  35.4 21.9 %copy-start.4 = (bf16[4,112,384]{2,1,0:T(8,128)(2,1)}, bf16[4,112,384]{2,1,0:T(8,128)(2,1)S(1)}, u32[]{:S(2)}) copy-start(bf16[4,112,384]{2,1,0:T(8,128)(2,1)S(1)} %pad_maximum_fusion.3.refs_7_) | copy-start | bytes 1032196
  35.4 7.1 %copy-start.7 = (bf16[4,128,384]{2,1,0:T(8,128)(2,1)}, bf16[4,128,384]{2,1,0:T(8,128)(2,1)S(1)}, u32[]{:S(2)}) copy-start(bf16[4,128,384]{2,1,0:T(8,128)(2,1)S(1)} %collective-permute-done.8.refs_6_) | copy-start | bytes 1179652
  35.4 7.1 %copy-start.8 = (bf16[4,128,384]{2,1,0:T(8,128)(2,1)}, bf16[4,128,384]{2,1,0:T(8,128)(2,1)S(1)}, u32[]{:S(2)}) copy-start(bf16[4,128,384]{2,1,0:T(8,128)(2,1)S(1)} %collective-permute-done.9.refs_7_) | copy-start | bytes 1179652
  35.5 5.0 %collective-permute-start.13 = (bf16[4,128,384]{2,1,0:T(8,128)(2,1)S(1)}, bf16[4,128,384]{2,1,0:T(8,128)(2,1)S(1)}, u32[]{:S(2)}, u32[]{:S(2)}) collective-permute-start(bf16[4,128,384]{2,1,0:T(8,128)(2,1)S(1)} %pad_maximum_fusion.refs_3_), channel_id=1, source_target_pairs={{0,1},{1,0},{2,3},{3,2},{4,5},{5,4},{6,7},{7,6},{8,9},{9,8},{10,11... | collective-permute-start | bytes 1179656 | tf_op jit(solution)/shard_map/ppermute | solution.py:451
  35.5 5.4 %collective-permute-start.16 = (bf16[4,128,384]{2,1,0:T(8,128)(2,1)S(1)}, bf16[4,128,384]{2,1,0:T(8,128)(2,1)S(1)}, u32[]{:S(2)}, u32[]{:S(2)}) collective-permute-start(bf16[4,128,384]{2,1,0:T(8,128)(2,1)S(1)} %collective-permute-done.8.refs_6_), channel_id=1, source_target_pairs={{0,1},{1,0},{2,3},{3,2},{4,5},{5,4},{6,7},{7,6},{8,9},{9,8},{10,11... | collective-permute-start | bytes 1179656 | tf_op jit(solution)/shard_map/ppermute | solution.py:451
  36.0 6.5 %collective-permute-start.17 = (bf16[4,128,384]{2,1,0:T(8,128)(2,1)S(1)}, bf16[4,128,384]{2,1,0:T(8,128)(2,1)S(1)}, u32[]{:S(2)}, u32[]{:S(2)}) collective-permute-start(bf16[4,128,384]{2,1,0:T(8,128)(2,1)S(1)} %collective-permute-done.9.refs_7_), channel_id=1, source_target_pairs={{0,1},{1,0},{2,3},{3,2},{4,5},{5,4},{6,7},{7,6},{8,9},{9,8},{10,11... | collective-permute-start | bytes 1179656 | tf_op jit(solution)/shard_map/ppermute | solution.py:451
  36.1 2.5 %collective-permute-start.14 = (bf16[2,128,384]{2,1,0:T(8,128)(2,1)S(1)}, bf16[2,128,384]{2,1,0:T(8,128)(2,1)S(1)}, u32[]{:S(2)}, u32[]{:S(2)}) collective-permute-start(bf16[2,128,384]{2,1,0:T(8,128)(2,1)S(1)} %collective-permute-done.6.refs_4_), channel_id=1, source_target_pairs={{0,1},{1,0},{2,3},{3,2},{4,5},{5,4},{6,7},{7,6},{8,9},{9,8},{10,11... | collective-permute-start | bytes 589832 | tf_op jit(solution)/shard_map/ppermute | solution.py:451
  36.5 2.4 %collective-permute-start.15 = (bf16[2,128,384]{2,1,0:T(8,128)(2,1)S(1)}, bf16[2,128,384]{2,1,0:T(8,128)(2,1)S(1)}, u32[]{:S(2)}, u32[]{:S(2)}) collective-permute-start(bf16[2,128,384]{2,1,0:T(8,128)(2,1)S(1)} %collective-permute-done.7.refs_5_), channel_id=1, source_target_pairs={{0,1},{1,0},{2,3},{3,2},{4,5},{5,4},{6,7},{7,6},{8,9},{9,8},{10,11... | collective-permute-start | bytes 589832 | tf_op jit(solution)/shard_map/ppermute | solution.py:451
  38.6 3.9 %copy-start.17 = (bf16[2,128,384]{2,1,0:T(8,128)(2,1)}, bf16[2,128,384]{2,1,0:T(8,128)(2,1)S(1)}, u32[]{:S(2)}) copy-start(bf16[2,128,384]{2,1,0:T(8,128)(2,1)S(1)} %collective-permute-done.14.refs_9_) | copy-start | bytes 589828
  38.6 22.0 %collective-permute-start.18 = (bf16[4,112,384]{2,1,0:T(8,128)(2,1)S(1)}, bf16[4,112,384]{2,1,0:T(8,128)(2,1)S(1)}, u32[]{:S(2)}, u32[]{:S(2)}) collective-permute-start(bf16[4,112,384]{2,1,0:T(8,128)(2,1)S(1)} %pad_maximum_fusion.3.refs_7_), channel_id=1, source_target_pairs={{0,1},{1,0},{2,3},{3,2},{4,5},{5,4},{6,7},{7,6},{8,9},{9,8},{10,11... | collective-permute-start | bytes 1032200 | tf_op jit(solution)/shard_map/ppermute | solution.py:451
  38.9 2.0 %copy-start.18 = (bf16[2,128,384]{2,1,0:T(8,128)(2,1)}, bf16[2,128,384]{2,1,0:T(8,128)(2,1)S(1)}, u32[]{:S(2)}) copy-start(bf16[2,128,384]{2,1,0:T(8,128)(2,1)S(1)} %collective-permute-done.15.refs_10_) | copy-start | bytes 589828
  38.9 18.4 %collective-permute-start.12 = (bf16[4,112,384]{2,1,0:T(8,128)(2,1)S(1)}, bf16[4,112,384]{2,1,0:T(8,128)(2,1)S(1)}, u32[]{:S(2)}, u32[]{:S(2)}) collective-permute-start(bf16[4,112,384]{2,1,0:T(8,128)(2,1)S(1)} %pad_maximum_fusion.3.refs_7_), channel_id=1, source_target_pairs={{0,6},{1,7},{2,4},{3,5},{4,2},{5,3},{6,0},{7,1},{8,14},{9,15},{10,... | collective-permute-start | bytes 1032200 | tf_op jit(solution)/shard_map/ppermute | solution.py:451
  40.4 2.1 %copy-start.9 = (bf16[4,128,384]{2,1,0:T(8,128)(2,1)}, bf16[4,128,384]{2,1,0:T(8,128)(2,1)S(1)}, u32[]{:S(2)}) copy-start(bf16[4,128,384]{2,1,0:T(8,128)(2,1)S(1)} %collective-permute-done.13.refs_8_) | copy-start | bytes 1179652
  40.4 17.1 %collective-permute-start.11 = (bf16[4,112,384]{2,1,0:T(8,128)(2,1)S(1)}, bf16[4,112,384]{2,1,0:T(8,128)(2,1)}, u32[]{:S(2)}, u32[]{:S(2)}) collective-permute-start(bf16[4,112,384]{2,1,0:T(8,128)(2,1)S(1)} %pad_maximum_fusion.3.refs_7_), channel_id=1, source_target_pairs={{0,4},{1,5},{2,6},{3,7},{4,0},{5,1},{6,2},{7,3},{8,12},{9,13},{10,... | collective-permute-start | bytes 1032200 | tf_op jit(solution)/shard_map/ppermute | solution.py:451
  40.9 1.6 copy-start.10
  40.9 16.7 %collective-permute-start.10 = (bf16[4,112,384]{2,1,0:T(8,128)(2,1)S(1)}, bf16[4,112,384]{2,1,0:T(8,128)(2,1)}, u32[]{:S(2)}, u32[]{:S(2)}) collective-permute-start(bf16[4,112,384]{2,1,0:T(8,128)(2,1)S(1)} %pad_maximum_fusion.3.refs_7_), channel_id=1, source_target_pairs={{0,2},{1,3},{2,0},{3,1},{4,6},{5,7},{6,4},{7,5},{8,10},{9,11},{10,... | collective-permute-start | bytes 1032200 | tf_op jit(solution)/shard_map/ppermute | solution.py:451
  42.6 0.8 copy-start.11
  57.3 5.1 %copy-start.13 = (bf16[4,112,384]{2,1,0:T(8,128)(2,1)}, bf16[4,112,384]{2,1,0:T(8,128)(2,1)S(1)}, u32[]{:S(2)}) copy-start(bf16[4,112,384]{2,1,0:T(8,128)(2,1)S(1)} %collective-permute-done.12.refs_10_) | copy-start | bytes 1032196
  57.6 4.0 %collective-permute-start.19 = (bf16[4,112,384]{2,1,0:T(8,128)(2,1)}, bf16[4,112,384]{2,1,0:T(8,128)(2,1)S(1)}, u32[]{:S(2)}, u32[]{:S(2)}) collective-permute-start(bf16[4,112,384]{2,1,0:T(8,128)(2,1)} %collective-permute-done.10.refs_8_), channel_id=1, source_target_pairs={{0,1},{1,0},{2,3},{3,2},{4,5},{5,4},{6,7},{7,6},{8,9},{9,8},{10,11... | collective-permute-start | bytes 1032200 | tf_op jit(solution)/shard_map/ppermute | solution.py:451
  60.1 2.0 %collective-permute-start.20 = (bf16[4,112,384]{2,1,0:T(8,128)(2,1)}, bf16[4,112,384]{2,1,0:T(8,128)(2,1)S(1)}, u32[]{:S(2)}, u32[]{:S(2)}) collective-permute-start(bf16[4,112,384]{2,1,0:T(8,128)(2,1)} %collective-permute-done.11.refs_9_), channel_id=1, source_target_pairs={{0,1},{1,0},{2,3},{3,2},{4,5},{5,4},{6,7},{7,6},{8,9},{9,8},{10,11... | collective-permute-start | bytes 1032200 | tf_op jit(solution)/shard_map/ppermute | solution.py:451
  60.2 2.2 %collective-permute-start.21 = (bf16[4,112,384]{2,1,0:T(8,128)(2,1)S(1)}, bf16[4,112,384]{2,1,0:T(8,128)(2,1)S(1)}, u32[]{:S(2)}, u32[]{:S(2)}) collective-permute-start(bf16[4,112,384]{2,1,0:T(8,128)(2,1)S(1)} %collective-permute-done.12.refs_10_), channel_id=1, source_target_pairs={{0,1},{1,0},{2,3},{3,2},{4,5},{5,4},{6,7},{7,6},{8,9},{9,8},{10,11... | collective-permute-start | bytes 1032200 | tf_op jit(solution)/shard_map/ppermute | solution.py:451
  60.6 1.8 %copy-start.12 = (bf16[4,112,384]{2,1,0:T(8,128)(2,1)}, bf16[4,112,384]{2,1,0:T(8,128)(2,1)S(1)}, u32[]{:S(2)}) copy-start(bf16[4,112,384]{2,1,0:T(8,128)(2,1)S(1)} %collective-permute-done.18.refs_11_) | copy-start | bytes 1032196
  61.6 0.8 copy-start.14
  62.1 0.7 copy-start.15
  62.4 0.7 copy-start.16
  81.7 18.9 %collective-permute-start.22 = (bf16[16,112,384]{2,1,0:T(8,128)(2,1)}, bf16[16,112,384]{2,1,0:T(8,128)(2,1)S(1)}, u32[]{:S(2)}, u32[]{:S(2)}) collective-permute-start(bf16[16,112,384]{2,1,0:T(8,128)(2,1)} %get-tuple-element.79), channel_id=1, source_target_pairs={{0,1},{1,0},{2,3},{3,2},{4,5},{5,4},{6,7},{7,6},{8,9},{9,8},{10,11... | collective-permute-start | bytes 4128776 | tf_op jit(solution)/shard_map/ppermute | solution.py:451
  90.9 9.7 %copy-start = (f32[16,112,384]{2,1,0:T(8,128)S(1)}, f32[16,112,384]{2,1,0:T(8,128)}, u32[]{:S(2)}) copy-start(f32[16,112,384]{2,1,0:T(8,128)} %get-tuple-element.84) | copy-start | bytes 8257540
  101.1 26.6 %collective-permute-start.23 = (bf16[4,112,384]{2,1,0:T(8,128)(2,1)S(1)}, bf16[4,112,384]{2,1,0:T(8,128)(2,1)S(1)}, u32[]{:S(2)}, u32[]{:S(2)}) collective-permute-start(bf16[4,112,384]{2,1,0:T(8,128)(2,1)S(1)} %get-tuple-element.92), channel_id=1, source_target_pairs={{0,2},{1,3},{2,0},{3,1},{4,6},{5,7},{6,4},{7,5},{8,10},{9,11},{10,... | collective-permute-start | bytes 1032200 | tf_op jit(solution)/shard_map/ppermute | solution.py:451
  103.3 24.9 %collective-permute-start.24 = (bf16[4,112,384]{2,1,0:T(8,128)(2,1)S(1)}, bf16[4,112,384]{2,1,0:T(8,128)(2,1)S(1)}, u32[]{:S(2)}, u32[]{:S(2)}) collective-permute-start(bf16[4,112,384]{2,1,0:T(8,128)(2,1)S(1)} %get-tuple-element.93), channel_id=1, source_target_pairs={{0,4},{1,5},{2,6},{3,7},{4,0},{5,1},{6,2},{7,3},{8,12},{9,13},{10,... | collective-permute-start | bytes 1032200 | tf_op jit(solution)/shard_map/ppermute | solution.py:451
  113.4 15.6 %collective-permute-start.25 = (bf16[4,112,384]{2,1,0:T(8,128)(2,1)S(1)}, bf16[4,112,384]{2,1,0:T(8,128)(2,1)S(1)}, u32[]{:S(2)}, u32[]{:S(2)}) collective-permute-start(bf16[4,112,384]{2,1,0:T(8,128)(2,1)S(1)} %get-tuple-element.94), channel_id=1, source_target_pairs={{0,6},{1,7},{2,4},{3,5},{4,2},{5,3},{6,0},{7,1},{8,14},{9,15},{10,... | collective-permute-start | bytes 1032200 | tf_op jit(solution)/shard_map/ppermute | solution.py:451
  127.6 3.9 %copy-start.3 = (f32[8,128,384]{2,1,0:T(8,128)S(1)}, f32[8,128,384]{2,1,0:T(8,128)}, u32[]{:S(2)}) copy-start(f32[8,128,384]{2,1,0:T(8,128)} %get-tuple-element.99) | copy-start | bytes 4718596
  129.0 2.5 %collective-permute-start.26 = (bf16[8,128,384]{2,1,0:T(8,128)(2,1)}, bf16[8,128,384]{2,1,0:T(8,128)(2,1)S(1)}, u32[]{:S(2)}, u32[]{:S(2)}) collective-permute-start(bf16[8,128,384]{2,1,0:T(8,128)(2,1)} %get-tuple-element.100), channel_id=1, source_target_pairs={{0,1},{1,0},{2,3},{3,2},{4,5},{5,4},{6,7},{7,6},{8,9},{9,8},{10,11... | collective-permute-start | bytes 2359304 | tf_op jit(solution)/shard_map/ppermute | solution.py:451
  129.0 8.1 %collective-permute-start.30 = (bf16[8,128,384]{2,1,0:T(8,128)(2,1)}, bf16[8,128,384]{2,1,0:T(8,128)(2,1)S(1)}, u32[]{:S(2)}, u32[]{:S(2)}) collective-permute-start(bf16[8,128,384]{2,1,0:T(8,128)(2,1)} %get-tuple-element.102), channel_id=1, source_target_pairs={{0,1},{1,0},{2,3},{3,2},{4,5},{5,4},{6,7},{7,6},{8,9},{9,8},{10,11... | collective-permute-start | bytes 2359304 | tf_op jit(solution)/shard_map/ppermute | solution.py:451
  131.5 5.6 %copy-start.2 = (f32[8,128,384]{2,1,0:T(8,128)S(1)}, f32[8,128,384]{2,1,0:T(8,128)}, u32[]{:S(2)}) copy-start(f32[8,128,384]{2,1,0:T(8,128)} %get-tuple-element.101) | copy-start | bytes 4718596
  131.7 11.2 %collective-permute-start.27 = (bf16[4,128,384]{2,1,0:T(8,128)(2,1)S(1)}, bf16[4,128,384]{2,1,0:T(8,128)(2,1)S(1)}, u32[]{:S(2)}, u32[]{:S(2)}) collective-permute-start(bf16[4,128,384]{2,1,0:T(8,128)(2,1)S(1)} %slice.166), channel_id=1, source_target_pairs={{0,2},{1,3},{2,0},{3,1},{4,6},{5,7},{6,4},{7,5},{8,10},{9,11},{10,... | collective-permute-start | bytes 1179656 | tf_op jit(solution)/shard_map/ppermute | solution.py:451
  133.2 25.3 %collective-permute-start.35 = (bf16[112,384]{1,0:T(8,128)(2,1)S(1)}, bf16[112,384]{1,0:T(8,128)(2,1)S(1)}, u32[]{:S(2)}, u32[]{:S(2)}) collective-permute-start(bf16[112,384]{1,0:T(8,128)(2,1)S(1)} %get-tuple-element.116), channel_id=1, source_target_pairs={{0,8},{1,9},{2,10},{3,11},{4,12},{5,13},{6,14},{7,15},{8,16},{9,17... | collective-permute-start | bytes 258056 | tf_op jit(solution)/shard_map/ppermute | solution.py:451
  133.3 25.2 %collective-permute-start.37 = (bf16[112,384]{1,0:T(8,128)(2,1)S(1)}, bf16[112,384]{1,0:T(8,128)(2,1)S(1)}, u32[]{:S(2)}, u32[]{:S(2)}) collective-permute-start(bf16[112,384]{1,0:T(8,128)(2,1)S(1)} %get-tuple-element.117), channel_id=1, source_target_pairs={{0,24},{1,25},{2,26},{3,27},{4,28},{5,29},{6,30},{7,31},{8,0},{9,1... | collective-permute-start | bytes 258056 | tf_op jit(solution)/shard_map/ppermute | solution.py:451
  137.1 21.4 %collective-permute-start.36 = (bf16[112,384]{1,0:T(8,128)(2,1)S(1)}, bf16[112,384]{1,0:T(8,128)(2,1)S(1)}, u32[]{:S(2)}, u32[]{:S(2)}) collective-permute-start(bf16[112,384]{1,0:T(8,128)(2,1)S(1)} %get-tuple-element.118), channel_id=1, source_target_pairs={{0,16},{1,17},{2,18},{3,19},{4,20},{5,21},{6,22},{7,23},{8,24},{9,... | collective-permute-start | bytes 258056 | tf_op jit(solution)/shard_map/ppermute | solution.py:451
  137.3 12.2 %collective-permute-start.31 = (bf16[4,128,384]{2,1,0:T(8,128)(2,1)S(1)}, bf16[4,128,384]{2,1,0:T(8,128)(2,1)S(1)}, u32[]{:S(2)}, u32[]{:S(2)}) collective-permute-start(bf16[4,128,384]{2,1,0:T(8,128)(2,1)S(1)} %slice.165), channel_id=1, source_target_pairs={{0,4},{1,5},{2,6},{3,7},{4,0},{5,1},{6,2},{7,3},{8,12},{9,13},{10,... | collective-permute-start | bytes 1179656 | tf_op jit(solution)/shard_map/ppermute | solution.py:451
  143.0 9.6 %collective-permute-start.28 = (bf16[2,128,384]{2,1,0:T(8,128)(2,1)S(1)}, bf16[2,128,384]{2,1,0:T(8,128)(2,1)S(1)}, u32[]{:S(2)}, u32[]{:S(2)}) collective-permute-start(bf16[2,128,384]{2,1,0:T(8,128)(2,1)S(1)} %fusion.4), channel_id=1, source_target_pairs={{0,4},{1,5},{2,6},{3,7},{4,0},{5,1},{6,2},{7,3},{8,12},{9,13},{10,... | collective-permute-start | bytes 589832 | tf_op jit(solution)/shard_map/ppermute | solution.py:451
  149.7 5.8 %collective-permute-start.32 = (bf16[2,128,384]{2,1,0:T(8,128)(2,1)S(1)}, bf16[2,128,384]{2,1,0:T(8,128)(2,1)S(1)}, u32[]{:S(2)}, u32[]{:S(2)}) collective-permute-start(bf16[2,128,384]{2,1,0:T(8,128)(2,1)S(1)} %fusion.3), channel_id=1, source_target_pairs={{0,2},{1,3},{2,0},{3,1},{4,6},{5,7},{6,4},{7,5},{8,10},{9,11},{10,... | collective-permute-start | bytes 589832 | tf_op jit(solution)/shard_map/ppermute | solution.py:451
  152.7 7.5 %collective-permute-start.29 = (bf16[128,384]{1,0:T(8,128)(2,1)S(1)}, bf16[128,384]{1,0:T(8,128)(2,1)S(1)}, u32[]{:S(2)}, u32[]{:S(2)}) collective-permute-start(bf16[128,384]{1,0:T(8,128)(2,1)S(1)} %fusion.11), channel_id=1, source_target_pairs={{0,8},{1,9},{2,10},{3,11},{4,12},{5,13},{6,14},{7,15},{8,16},{9,17... | collective-permute-start | bytes 294920 | tf_op jit(solution)/shard_map/ppermute | solution.py:451
  155.5 7.8 %collective-permute-start.33 = (bf16[128,384]{1,0:T(8,128)(2,1)S(1)}, bf16[128,384]{1,0:T(8,128)(2,1)S(1)}, u32[]{:S(2)}, u32[]{:S(2)}) collective-permute-start(bf16[128,384]{1,0:T(8,128)(2,1)S(1)} %get-tuple-element.119), channel_id=1, source_target_pairs={{0,16},{1,17},{2,18},{3,19},{4,20},{5,21},{6,22},{7,23},{8,24},{9,... | collective-permute-start | bytes 294920 | tf_op jit(solution)/shard_map/ppermute | solution.py:451
  158.5 5.3 %collective-permute-start.34 = (bf16[128,384]{1,0:T(8,128)(2,1)S(1)}, bf16[128,384]{1,0:T(8,128)(2,1)S(1)}, u32[]{:S(2)}, u32[]{:S(2)}) collective-permute-start(bf16[128,384]{1,0:T(8,128)(2,1)S(1)} %get-tuple-element.120), channel_id=1, source_target_pairs={{0,24},{1,25},{2,26},{3,27},{4,28},{5,29},{6,30},{7,31},{8,0},{9,1... | collective-permute-start | bytes 294920 | tf_op jit(solution)/shard_map/ppermute | solution.py:451

commit v4 on v3

--- a/solution.py
+++ b/solution.py
@@ -137,10 +137,11 @@
 
 def forward_kernel(n_pieces, scal_ref, cond_ref, x_ref, *refs):
     pieces = refs[:n_pieces]
-    mod_ref, ada_ref, qkv_w_ref, proj_ref, bias_ref, qkv_ref, probs_ref, mixed_ref, branch_ref = refs[
+    mod_ref, ada_hbm_ref, qkv_w_ref, proj_ref, bias_ref, qkv_ref, probs_ref, mixed_ref, branch_ref = refs[
         n_pieces : n_pieces + 9
     ]
-    rows_ref, score_ref = refs[n_pieces + 9 :]
+    rows_ref, score_ref, ada_ref, ada_sem = refs[n_pieces + 9 :]
+    store = pltpu.make_async_copy(ada_ref, ada_hbm_ref, ada_sem)
     step = pl.program_id(0)
     group, seq = x_ref.shape[0], x_ref.shape[1]
 
@@ -158,6 +159,7 @@
                 qkv_w_ref[:, lanes_of(tile, block * D)] = rows_ref[
                     tile, pl.ds(QKV_AT + block, D, stride=3), :
                 ].astype(BF16)
+        store.start()
         act = jax.nn.silu(cond_ref[...].astype(F32)).astype(BF16)
         for block in range(6):
             mod_ref[block] = mm(act, ada_ref[block]) + bias_ref[block : block + 1, :]
@@ -193,6 +195,10 @@
                 rows = slice(head * HEAD_DIM, (head + 1) * HEAD_DIM)
                 mixed_ref[latent, rows, :] = mm(values_t[rows, :], probs_ref[latent, head]).astype(BF16)
             branch_ref[latent] = mm_tn(mixed_ref[latent], proj_ref[...])
+
+    @pl.when(step == pl.num_programs(0) - 1)
+    def _():
+        store.wait()
 
 
 def mlp_kernel(n_pieces, n_out, scal_ref, mod_ref, proj_ref, x_ref, branch_ref, mixed_ref, cot_ref, *refs):
@@ -330,18 +336,20 @@
 
 
 def finish_kernel(
-    n_out, base, scal_ref, mod_ref, qkv_w_ref, cond_ref, ada_ref, dmod_in_ref, dproj_ref,
+    n_out, base, scal_ref, mod_ref, qkv_w_ref, cond_ref, ada_hbm_ref, dmod_in_ref, dproj_ref,
     x_ref, dqkv_ref, dx_ref, *refs
 ):
     grad_x_ref, grad_cond_ref = refs[:2]
     send_refs = refs[2 : 2 + n_out]
-    rows_ref, dqkv_w_ref, dmod_ref, dbias_ref = refs[2 + n_out :]
+    rows_ref, dqkv_w_ref, dmod_ref, dbias_ref, ada_ref, ada_sem = refs[2 + n_out :]
+    fetch = pltpu.make_async_copy(ada_hbm_ref, ada_ref, ada_sem)
     step = pl.program_id(0)
     last = pl.num_programs(0) - 1
     group, seq = x_ref.shape[0], x_ref.shape[1]
 
     @pl.when(step == 0)
     def _():
+        fetch.start()
         dqkv_w_ref[...] = jnp.zeros_like(dqkv_w_ref)
         dmod_ref[...] = jnp.zeros_like(dmod_ref)
         dbias_ref[...] = jnp.zeros_like(dbias_ref)
@@ -365,6 +373,7 @@
 
     @pl.when(step == last)
     def _():
+        fetch.wait()
         cond = cond_ref[...].astype(F32)
         gate = jax.nn.sigmoid(cond)
         act = (cond * gate).astype(BF16)
@@ -440,7 +449,7 @@
             sent += [device(k, dy, dx, dc) for dx in (0, 1) for k in (0, 1) for dy in (0, 1)]
             sent += [device(k, dy, dx, dc) for dy in (0, 1) for k in (2, 3) for dx in (0, 1)]
         self.sent = sent
-        self.slots = [(8, BF16), (8, BF16), (8, F32), (8, F32)]
+        self.slots = [(8, BF16)] * 4
 
     def shift(self, values, dz=0, dy=0, dx=0, dc=0):
         pairs = []
@@ -471,8 +480,8 @@
     def middle(self, state):
         got_a, got_b, keep_a, keep_b = state
         shape = keep_a.shape[1:]
-        sum_a = (keep_a + got_a.astype(F32)).reshape((2, 4) + shape)
-        sum_b = (keep_b + got_b.astype(F32)).reshape((2, 4) + shape)
+        sum_a = (keep_a.astype(F32) + got_a.astype(F32)).reshape((2, 4) + shape)
+        sum_b = (keep_b.astype(F32) + got_b.astype(F32)).reshape((2, 4) + shape)
         return sum_a[0], sum_b[0], sum_a[1].astype(BF16), sum_b[1].astype(BF16)
 
     def send(self, state):
@@ -499,7 +508,7 @@
         sides = [(0, 0), (0, 1), (1, 0), (1, 1)]
         self.gathered = [device(-k, dy, dx, dc) for dc in (0, 1) for dy, dx in sides for k in range(4)]
         self.sent = [device(k, dy, dx, dc) for dc in (1, 0) for dy, dx in sides for k in range(4)]
-        self.slots = [(16, BF16), (16, F32)]
+        self.slots = [(16, BF16)] * 2
 
     def join(self, own, others):
         half = len(others) // 2
@@ -513,7 +522,7 @@
 
     def middle(self, state):
         got, keep = state
-        total = (keep + got.astype(F32)).reshape((4, 4) + keep.shape[1:])
+        total = (keep.astype(F32) + got.astype(F32)).reshape((4, 4) + keep.shape[1:])
         return total[0], total[1].astype(BF16), total[2].astype(BF16), total[3].astype(BF16)
 
     def send(self, state):
@@ -606,7 +615,7 @@
             lambda *refs: forward_kernel(n_pieces, *refs),
             count // FORWARD_STEP,
             [whole(), by_latent(FORWARD_STEP, seq, D)] + [whole()] * n_pieces,
-            [whole()] * 5
+            [whole(), pl.BlockSpec(memory_space=pl.ANY)] + [whole()] * 3
             + [
                 by_latent(FORWARD_STEP, seq, 3 * D),
                 by_latent(FORWARD_STEP, HEADS, seq, seq),
@@ -627,6 +636,8 @@
             [
                 pltpu.VMEM((TILES, ATTN_ROWS + attn_height, LANES), F32),
                 pltpu.VMEM((FORWARD_STEP, HEADS, seq, seq), F32),
+                pltpu.VMEM((6, D, D), BF16),
+                pltpu.SemaphoreType.DMA,
             ],
             [attn_scal, condition, latents] + attn_pieces,
             15 * 10**9,
@@ -687,7 +698,7 @@
         results = call(
             lambda *refs: finish_kernel(n_out, 1 + devices, *refs),
             count // FINISH_STEP,
-            [whole()] * 6 + [by_latent(FINISH_STEP, seq, D), by_latent(FINISH_STEP, seq, 3 * D), by_latent(FINISH_STEP, seq, D)],
+            [whole()] * 3 + [pl.BlockSpec(memory_space=pl.ANY)] + [whole()] * 2 + [by_latent(FINISH_STEP, seq, D), by_latent(FINISH_STEP, seq, 3 * D), by_latent(FINISH_STEP, seq, D)],
             [by_latent(FINISH_STEP, seq, D), whole()] + [whole()] * n_out,
             [struct((count, seq, D), F32), struct((count, D), F32)]
             + [struct((slots, attn_height, D), kind) for slots, kind in plan.slots],
@@ -696,13 +707,17 @@
                 pltpu.VMEM((D, 3 * D), F32),
                 pltpu.VMEM((2, count, D), F32),
                 pltpu.VMEM((8, 3 * D), F32),
+                pltpu.VMEM((6, D, D), BF16),
+                pltpu.SemaphoreType.DMA,
             ],
             [attn_scal, mod, qkv_w, condition, ada, dmod, dproj, latents, grad_qkv, grad_middle],
             15 * 10**9,
         )
         grad_latents, grad_condition = results[:2]
         sums, attn_parts = lax.optimization_barrier((sums, results[2:]))
-        grad_attn = plan.end(plan.send(plan.middle(plan.begin(attn_parts))))
+        attn_parts = plan.middle(plan.begin(attn_parts))
+        out_last, sums = lax.optimization_barrier((attn_parts[-1], sums))
+        grad_attn = plan.end(plan.send([*attn_parts[:-1], out_last]))
         grad_mlp = mlp_plan.end(sums)
         return (
             output,

time: 164 us -> 161 us (0.982)
  starting transfers between devices: 63.7 us -> 45.6 us
  Pallas kernels: 55 us -> 67 us
    ppermute x38, starting transfers between devices: 63.7 us -> 45.6 us  [shift(): return lax.ppermute(values, AXIS, pairs)]
    pallas_call x4, Pallas kernels: 55 us -> 67 us  [call(): pl.pallas_call(kernel, grid_spec=pltpu.PrefetchScalarGridSpec(num_scalar_...]
  transfers between devices with their start and end apart: 38 -> 38, of which waited for: 21 -> 17; matrix products, arithmetic and copies ran while one was open for 3% -> 4% of each run, Pallas kernels for 22% -> 25%
where the time goes in v4:
time: 161 us; the launch traced here: 160 us
  Pallas kernels  67 us (42%)
  starting transfers between devices  45.6 us (28%)
  waiting for transfers between devices  34.5 us (21%)
  local copies, waits for them, and re-layouts  7.9 us (5%)
  other arithmetic  3.17 us (2%)
  between operations  1.8 us (1%)
    pallas_call x4, Pallas kernels, call(): pl.pallas_call(kernel, grid_spec=pltpu.PrefetchScalarGridSpec(num_scalar_...  67 us
    ppermute x38, starting transfers between devices, shift(): return lax.ppermute(values, AXIS, pairs)  45.6 us
    ppermute x38, waiting for transfers between devices, shift(): return lax.ppermute(values, AXIS, pairs)  34.5 us
    dynamic_update_slice x2, local copies, waits for them, and re-layouts, to_piece(): lax.dynamic_update_slice(flat, share, (size * me % GROUP,)).reshape(rows, D)  3.89 us
  transfers between devices with their start and end apart: 38, of which 17 were waited for; matrix products, arithmetic and copies ran while one was open for 4% of the time, Pallas kernels for 25%

profile of v4, /device:TPU:0, one launch (start us, length us, event | category | flops | bytes accessed | tf_op | source)
XLA Modules:
  0.0 160.1 jit_solution(12800652784752094261)
XLA Ops:
  0.7 2.0 %dynamic_update_slice.6 = bf16[49152]{0:T(1024)(128)(2,1)S(1)} dynamic-update-slice(bf16[49152]{0:T(1024)(128)(2,1)S(1)} %broadcast_in_dim.6, bf16[46176]{0:T(1024)(128)(2,1)} %param.8, s32[]{:T(128)S(6)} %select_n.1113) | dynamic-update-slice | bytes 184708 | tf_op jit(solution)/shard_map/dynamic_update_slice | solution.py:546
  2.7 5.1 %collective-permute-start.2 = (bf16[128,384]{1,0:T(8,128)(2,1)S(1)}, bf16[128,384]{1,0:T(8,128)(2,1)S(1)}, u32[]{:S(2)}, u32[]{:S(2)}) collective-permute-start(bf16[128,384]{1,0:T(8,128)(2,1)S(1)} %reshape.52), channel_id=1, source_target_pairs={{0,24},{1,25},{2,26},{3,27},{4,28},{5,29},{6,30},{7,31},{8,0},{9,1... | collective-permute-start | bytes 294920 | tf_op jit(solution)/shard_map/ppermute | solution.py:460
  7.8 1.0 collective-permute-start
  8.9 1.9 %dynamic_update_slice.7 = bf16[43008]{0:T(1024)(128)(2,1)S(1)} dynamic-update-slice(bf16[43008]{0:T(1024)(128)(2,1)S(1)} %broadcast_in_dim.7, bf16[36936]{0:T(1024)(128)(2,1)} %param.9, s32[]{:T(128)S(6)} %select_n.1115) | dynamic-update-slice | bytes 147748 | tf_op jit(solution)/shard_map/dynamic_update_slice | solution.py:546
  10.9 0.1 stack.338
  11.1 5.5 %collective-permute-done.1 = bf16[128,384]{1,0:T(8,128)(2,1)S(1)} collective-permute-done((bf16[128,384]{1,0:T(8,128)(2,1)S(1)}, bf16[128,384]{1,0:T(8,128)(2,1)S(1)}, u32[]{:S(2)}, u32[]{:S(2)}) %collective-permute-start.1) | collective-permute-done | bytes 98336 | tf_op jit(solution)/shard_map/ppermute | solution.py:460
  16.7 1.6 collective-permute-start.7
  18.3 1.5 collective-permute-start.6
  19.8 0.2 stack.339
  20.6 3.7 %collective-permute-done.6.refs_4_ = bf16[2,128,384]{2,1,0:T(8,128)(2,1)S(1)} collective-permute-done((bf16[2,128,384]{2,1,0:T(8,128)(2,1)S(1)}, bf16[2,128,384]{2,1,0:T(8,128)(2,1)S(1)}, u32[]{:S(2)}, u32[]{:S(2)}) %collective-permute-start.6) | collective-permute-done | bytes 196640 | tf_op jit(solution)/shard_map/ppermute | solution.py:460
  24.4 0.6 collective-permute-start.8
  25.0 1.6 collective-permute-start.9
  26.6 1.6 %collective-permute-start.5 = (bf16[112,384]{1,0:T(8,128)(2,1)S(1)}, bf16[112,384]{1,0:T(8,128)(2,1)S(1)}, u32[]{:S(2)}, u32[]{:S(2)}) collective-permute-start(bf16[112,384]{1,0:T(8,128)(2,1)S(1)} %reshape.53), channel_id=1, source_target_pairs={{0,24},{1,25},{2,26},{3,27},{4,28},{5,29},{6,30},{7,31},{8,0},{9,1... | collective-permute-start | bytes 258056 | tf_op jit(solution)/shard_map/ppermute | solution.py:460
  28.2 0.5 collective-permute-start.4
  28.7 1.9 %collective-permute-start.3 = (bf16[112,384]{1,0:T(8,128)(2,1)S(1)}, bf16[112,384]{1,0:T(8,128)(2,1)S(1)}, u32[]{:S(2)}, u32[]{:S(2)}) collective-permute-start(bf16[112,384]{1,0:T(8,128)(2,1)S(1)} %reshape.53), channel_id=1, source_target_pairs={{0,8},{1,9},{2,10},{3,11},{4,12},{5,13},{6,14},{7,15},{8,16},{9,17... | collective-permute-start | bytes 258056 | tf_op jit(solution)/shard_map/ppermute | solution.py:460
  30.7 0.7 pad_add_fusion
  31.3 0.7 collective-permute-done.5
  32.1 3.3 %collective-permute-done.4 = bf16[112,384]{1,0:T(8,128)(2,1)S(1)} collective-permute-done((bf16[112,384]{1,0:T(8,128)(2,1)S(1)}, bf16[112,384]{1,0:T(8,128)(2,1)S(1)}, u32[]{:S(2)}, u32[]{:S(2)}) %collective-permute-start.4) | collective-permute-done | bytes 86048 | tf_op jit(solution)/shard_map/ppermute | solution.py:460
  35.5 0.5 collective-permute-start.16
  36.1 0.4 collective-permute-start.14
  36.6 2.0 %collective-permute-done.14.refs_9_ = bf16[2,128,384]{2,1,0:T(8,128)(2,1)S(1)} collective-permute-done((bf16[2,128,384]{2,1,0:T(8,128)(2,1)S(1)}, bf16[2,128,384]{2,1,0:T(8,128)(2,1)S(1)}, u32[]{:S(2)}, u32[]{:S(2)}) %collective-permute-start.14) | collective-permute-done | bytes 196640 | tf_op jit(solution)/shard_map/ppermute | solution.py:460
  38.6 0.1 collective-permute-start.18
  38.8 0.1 collective-permute-done.15.refs_10_
  38.9 1.5 collective-permute-start.12
  40.4 0.5 collective-permute-start.11
  40.9 1.6 collective-permute-start.10
  42.6 0.8 copy-done.10
  43.3 16.6 %shard_map.101 = (f32[6,8,384]{2,1,0:T(8,128)}, bf16[6,384,384]{2,1,0:T(8,128)(2,1)}, bf16[384,1152]{1,0:T(8,128)(2,1)}, bf16[384,384]{1,0:T(8,128)(2,1)}, f32[8...) custom-call(s32[65]{0:T(128)} %get-tuple-element.65.refs_0_.scal_ref, ...), custom_call_target="tpu_custom_call" | custom-call | flops 15000000512 | bytes 20971520 | tf_op jit(solution)/shard_map/pallas_call | solution.py:563
  60.1 0.5 collective-permute-start.20
  60.6 1.3 collective-permute-done.19.refs_12_
  61.9 0.5 collective-permute-done.20.refs_13_
  62.4 0.3 collective-permute-done.21.refs_14_
  62.7 0.4 copy-done.14
  63.1 0.3 copy-done.15
  63.4 26.9 %shard_map.102 = (bf16[8,256,384]{2,1,0:T(8,128)(2,1)}, f32[8,256,384]{2,1,0:T(8,128)}, bf16[8,256,384]{2,1,0:T(8,128)(2,1)}, f32[4,8,384]{2,1,0:T(8,128)}, f32[...) custom-call(s32[65]{0:T(128)} %get-tuple-element.63.refs_0_, ...), custom_call_target="tpu_custom_call" | custom-call | flops 30000001024 | bytes 20971520 | tf_op jit(solution)/shard_map/pallas_call | solution.py:563
  90.5 10.6 %shard_map.103.refs_8_ = bf16[8,256,1152]{2,1,0:T(8,128)(2,1)} custom-call(s32[65]{0:T(128)} %get-tuple-element.65.refs_0_.scal_ref, bf16[8,256,1152]{2,1,0:T(8,128)(2,1)} %get-tuple-element.86.qkv_ref, bf16[8,6,256,256]{3,2,1,0:T(8,128)(2,1)} %get-tuple-element.87.probs_ref, bf16[8,256,384]{2,1,0:T(8,128)(2,1)} %get-tuple-element.88.dmixed_ref), custom_call_target="tpu_custom_call" | custom-call | flops 12999999488 | bytes 20971520 | tf_op jit(solution)/shard_map/pallas_call | solution.py:563
  101.0 0.4 fusion.12
  101.6 6.8 %collective-permute-start.23 = (bf16[4,112,384]{2,1,0:T(8,128)(2,1)S(1)}, bf16[4,112,384]{2,1,0:T(8,128)(2,1)S(1)}, u32[]{:S(2)}, u32[]{:S(2)}) collective-permute-start(bf16[4,112,384]{2,1,0:T(8,128)(2,1)S(1)} %get-tuple-element.97), channel_id=1, source_target_pairs={{0,2},{1,3},{2,0},{3,1},{4,6},{5,7},{6,4},{7,5},{8,10},{9,11},{10,... | collective-permute-start | bytes 1032200 | tf_op jit(solution)/shard_map/ppermute | solution.py:460
  108.4 1.7 %collective-permute-start.24 = (bf16[4,112,384]{2,1,0:T(8,128)(2,1)S(1)}, bf16[4,112,384]{2,1,0:T(8,128)(2,1)S(1)}, u32[]{:S(2)}, u32[]{:S(2)}) collective-permute-start(bf16[4,112,384]{2,1,0:T(8,128)(2,1)S(1)} %get-tuple-element.98), channel_id=1, source_target_pairs={{0,4},{1,5},{2,6},{3,7},{4,0},{5,1},{6,2},{7,3},{8,12},{9,13},{10,... | collective-permute-start | bytes 1032200 | tf_op jit(solution)/shard_map/ppermute | solution.py:460
  110.1 1.4 collective-permute-start.25
  111.5 12.9 %shard_map.104 = (f32[8,256,384]{2,1,0:T(8,128)}, f32[8,384]{1,0:T(8,128)}, bf16[8,128,384]{2,1,0:T(8,128)(2,1)}, bf16[8,128,384]{2,1,0:T(8,128)(2,1)}, bf16[8,1...) custom-call(s32[65]{0:T(128)} %get-tuple-element.65.refs_0_.scal_ref, f32[6,8,384]{2,1,0:T(8,128)} %get-tuple-element.72.refs_1_, ...), custom_call_target="tpu_custom_call" | custom-call | flops 15000000512 | bytes 20971520 | tf_op jit(solution)/shard_map/pallas_call | solution.py:563
  124.5 0.9 collective-permute-done.24
  125.4 1.8 %collective-permute-done.25 = bf16[4,112,384]{2,1,0:T(8,128)(2,1)S(1)} collective-permute-done((bf16[4,112,384]{2,1,0:T(8,128)(2,1)S(1)}, bf16[4,112,384]{2,1,0:T(8,128)(2,1)S(1)}, u32[]{:S(2)}, u32[]{:S(2)}) %collective-permute-start.25) | collective-permute-done | bytes 344096 | tf_op jit(solution)/shard_map/ppermute | solution.py:460
  127.2 0.4 collective-permute-start.26
  127.7 2.0 %collective-permute-done.26 = bf16[8,128,384]{2,1,0:T(8,128)(2,1)S(1)} collective-permute-done((bf16[8,128,384]{2,1,0:T(8,128)(2,1)}, bf16[8,128,384]{2,1,0:T(8,128)(2,1)S(1)}, u32[]{:S(2)}, u32[]{:S(2)}) %collective-permute-start.26) | collective-permute-done | bytes 786464 | tf_op jit(solution)/shard_map/ppermute | solution.py:460
  129.8 1.3 convert_add_fusion.2
  131.1 1.0 collective-permute-start.27
  132.1 0.2 convert_add_fusion.1
  132.4 2.0 %collective-permute-start.31 = (bf16[4,128,384]{2,1,0:T(8,128)(2,1)S(1)}, bf16[4,128,384]{2,1,0:T(8,128)(2,1)S(1)}, u32[]{:S(2)}, u32[]{:S(2)}) collective-permute-start(bf16[4,128,384]{2,1,0:T(8,128)(2,1)S(1)} %slice.165), channel_id=1, source_target_pairs={{0,4},{1,5},{2,6},{3,7},{4,0},{5,1},{6,2},{7,3},{8,12},{9,13},{10,... | collective-permute-start | bytes 1179656 | tf_op jit(solution)/shard_map/ppermute | solution.py:460
  134.3 0.2 fusion.13
  134.5 0.4 collective-permute-start.35
  134.9 3.5 %collective-permute-start.37 = (bf16[112,384]{1,0:T(8,128)(2,1)S(1)}, bf16[112,384]{1,0:T(8,128)(2,1)S(1)}, u32[]{:S(2)}, u32[]{:S(2)}) collective-permute-start(bf16[112,384]{1,0:T(8,128)(2,1)S(1)} %get-tuple-element.127), channel_id=1, source_target_pairs={{0,24},{1,25},{2,26},{3,27},{4,28},{5,29},{6,30},{7,31},{8,0},{9,1... | collective-permute-start | bytes 258056 | tf_op jit(solution)/shard_map/ppermute | solution.py:460
  138.4 4.2 %collective-permute-done.27 = bf16[4,128,384]{2,1,0:T(8,128)(2,1)S(1)} collective-permute-done((bf16[4,128,384]{2,1,0:T(8,128)(2,1)S(1)}, bf16[4,128,384]{2,1,0:T(8,128)(2,1)S(1)}, u32[]{:S(2)}, u32[]{:S(2)}) %collective-permute-start.27) | collective-permute-done | bytes 393248 | tf_op jit(solution)/shard_map/ppermute | solution.py:460
  142.7 1.6 %collective-permute-start.28 = (bf16[2,128,384]{2,1,0:T(8,128)(2,1)S(1)}, bf16[2,128,384]{2,1,0:T(8,128)(2,1)S(1)}, u32[]{:S(2)}, u32[]{:S(2)}) collective-permute-start(bf16[2,128,384]{2,1,0:T(8,128)(2,1)S(1)} %fusion.4), channel_id=1, source_target_pairs={{0,4},{1,5},{2,6},{3,7},{4,0},{5,1},{6,2},{7,3},{8,12},{9,13},{10,... | collective-permute-start | bytes 589832 | tf_op jit(solution)/shard_map/ppermute | solution.py:460
  144.4 1.1 collective-permute-start.32
  145.5 3.6 %collective-permute-done.28 = bf16[2,128,384]{2,1,0:T(8,128)(2,1)S(1)} collective-permute-done((bf16[2,128,384]{2,1,0:T(8,128)(2,1)S(1)}, bf16[2,128,384]{2,1,0:T(8,128)(2,1)S(1)}, u32[]{:S(2)}, u32[]{:S(2)}) %collective-permute-start.28) | collective-permute-done | bytes 196640 | tf_op jit(solution)/shard_map/ppermute | solution.py:460
  149.2 1.0 collective-permute-start.29
  150.2 0.4 collective-permute-done.32
  150.6 0.3 collective-permute-start.33
  150.9 3.3 %collective-permute-start.34 = (bf16[128,384]{1,0:T(8,128)(2,1)S(1)}, bf16[128,384]{1,0:T(8,128)(2,1)S(1)}, u32[]{:S(2)}, u32[]{:S(2)}) collective-permute-start(bf16[128,384]{1,0:T(8,128)(2,1)S(1)} %get-tuple-element.130), channel_id=1, source_target_pairs={{0,24},{1,25},{2,26},{3,27},{4,28},{5,29},{6,30},{7,31},{8,0},{9,1... | collective-permute-start | bytes 294920 | tf_op jit(solution)/shard_map/ppermute | solution.py:460
  154.3 0.8 dynamic_slice.7
  155.1 1.5 collective-permute-done.29
  156.6 2.6 %collective-permute-done.33 = bf16[128,384]{1,0:T(8,128)(2,1)S(1)} collective-permute-done((bf16[128,384]{1,0:T(8,128)(2,1)S(1)}, bf16[128,384]{1,0:T(8,128)(2,1)S(1)}, u32[]{:S(2)}, u32[]{:S(2)}) %collective-permute-start.33) | collective-permute-done | bytes 98336 | tf_op jit(solution)/shard_map/ppermute | solution.py:460
  159.3 0.8 dynamic_slice.6
  (92 shorter events, 1.8 us)
Async XLA Ops:
  2.7 8.3 %collective-permute-start.2 = (bf16[128,384]{1,0:T(8,128)(2,1)S(1)}, bf16[128,384]{1,0:T(8,128)(2,1)S(1)}, u32[]{:S(2)}, u32[]{:S(2)}) collective-permute-start(bf16[128,384]{1,0:T(8,128)(2,1)S(1)} %reshape.52), channel_id=1, source_target_pairs={{0,24},{1,25},{2,26},{3,27},{4,28},{5,29},{6,30},{7,31},{8,0},{9,1... | collective-permute-start | bytes 294920 | tf_op jit(solution)/shard_map/ppermute | solution.py:460
  7.8 8.8 %collective-permute-start.1 = (bf16[128,384]{1,0:T(8,128)(2,1)S(1)}, bf16[128,384]{1,0:T(8,128)(2,1)S(1)}, u32[]{:S(2)}, u32[]{:S(2)}) collective-permute-start(bf16[128,384]{1,0:T(8,128)(2,1)S(1)} %reshape.52), channel_id=1, source_target_pairs={{0,16},{1,17},{2,18},{3,19},{4,20},{5,21},{6,22},{7,23},{8,24},{9,... | collective-permute-start | bytes 294920 | tf_op jit(solution)/shard_map/ppermute | solution.py:460
  7.8 8.8 %collective-permute-start = (bf16[128,384]{1,0:T(8,128)(2,1)S(1)}, bf16[128,384]{1,0:T(8,128)(2,1)S(1)}, u32[]{:S(2)}, u32[]{:S(2)}) collective-permute-start(bf16[128,384]{1,0:T(8,128)(2,1)S(1)} %reshape.52), channel_id=1, source_target_pairs={{0,8},{1,9},{2,10},{3,11},{4,12},{5,13},{6,14},{7,15},{8,16},{9,17... | collective-permute-start | bytes 294920 | tf_op jit(solution)/shard_map/ppermute | solution.py:460
  16.6 25.9 %copy-start = (bf16[4,128,384]{2,1,0:T(8,128)(2,1)}, bf16[4,128,384]{2,1,0:T(8,128)(2,1)S(1)}, u32[]{:S(2)}) copy-start(bf16[4,128,384]{2,1,0:T(8,128)(2,1)S(1)} %pad_maximum_fusion.refs_3_) | copy-start | bytes 1179652
  16.7 8.3 %collective-permute-start.7 = (bf16[2,128,384]{2,1,0:T(8,128)(2,1)S(1)}, bf16[2,128,384]{2,1,0:T(8,128)(2,1)S(1)}, u32[]{:S(2)}, u32[]{:S(2)}) collective-permute-start(bf16[2,128,384]{2,1,0:T(8,128)(2,1)S(1)} %get-tuple-element.124), channel_id=1, source_target_pairs={{0,4},{1,5},{2,6},{3,7},{4,0},{5,1},{6,2},{7,3},{8,12},{9,13},{10,... | collective-permute-start | bytes 589832 | tf_op jit(solution)/shard_map/ppermute | solution.py:460
  18.3 6.1 %collective-permute-start.6 = (bf16[2,128,384]{2,1,0:T(8,128)(2,1)S(1)}, bf16[2,128,384]{2,1,0:T(8,128)(2,1)S(1)}, u32[]{:S(2)}, u32[]{:S(2)}) collective-permute-start(bf16[2,128,384]{2,1,0:T(8,128)(2,1)S(1)} %get-tuple-element.125), channel_id=1, source_target_pairs={{0,2},{1,3},{2,0},{3,1},{4,6},{5,7},{6,4},{7,5},{8,10},{9,11},{10,... | collective-permute-start | bytes 589832 | tf_op jit(solution)/shard_map/ppermute | solution.py:460
  24.3 18.2 %copy-start.5 = (bf16[2,128,384]{2,1,0:T(8,128)(2,1)}, bf16[2,128,384]{2,1,0:T(8,128)(2,1)S(1)}, u32[]{:S(2)}) copy-start(bf16[2,128,384]{2,1,0:T(8,128)(2,1)S(1)} %collective-permute-done.6.refs_4_) | copy-start | bytes 589828
  24.4 11.0 %collective-permute-start.8 = (bf16[4,128,384]{2,1,0:T(8,128)(2,1)S(1)}, bf16[4,128,384]{2,1,0:T(8,128)(2,1)S(1)}, u32[]{:S(2)}, u32[]{:S(2)}) collective-permute-start(bf16[4,128,384]{2,1,0:T(8,128)(2,1)S(1)} %pad_maximum_fusion.1), channel_id=1, source_target_pairs={{0,4},{1,5},{2,6},{3,7},{4,0},{5,1},{6,2},{7,3},{8,12},{9,13},{10,... | collective-permute-start | bytes 1179656 | tf_op jit(solution)/shard_map/ppermute | solution.py:460
  25.0 17.5 %copy-start.4 = (bf16[2,128,384]{2,1,0:T(8,128)(2,1)}, bf16[2,128,384]{2,1,0:T(8,128)(2,1)S(1)}, u32[]{:S(2)}) copy-start(bf16[2,128,384]{2,1,0:T(8,128)(2,1)S(1)} %collective-permute-done.7.refs_5_) | copy-start | bytes 589828
  25.0 10.4 %collective-permute-start.9 = (bf16[4,128,384]{2,1,0:T(8,128)(2,1)S(1)}, bf16[4,128,384]{2,1,0:T(8,128)(2,1)S(1)}, u32[]{:S(2)}, u32[]{:S(2)}) collective-permute-start(bf16[4,128,384]{2,1,0:T(8,128)(2,1)S(1)} %pad_maximum_fusion.2), channel_id=1, source_target_pairs={{0,2},{1,3},{2,0},{3,1},{4,6},{5,7},{6,4},{7,5},{8,10},{9,11},{10,... | collective-permute-start | bytes 1179656 | tf_op jit(solution)/shard_map/ppermute | solution.py:460
  26.6 5.5 %collective-permute-start.5 = (bf16[112,384]{1,0:T(8,128)(2,1)S(1)}, bf16[112,384]{1,0:T(8,128)(2,1)S(1)}, u32[]{:S(2)}, u32[]{:S(2)}) collective-permute-start(bf16[112,384]{1,0:T(8,128)(2,1)S(1)} %reshape.53), channel_id=1, source_target_pairs={{0,24},{1,25},{2,26},{3,27},{4,28},{5,29},{6,30},{7,31},{8,0},{9,1... | collective-permute-start | bytes 258056 | tf_op jit(solution)/shard_map/ppermute | solution.py:460
  28.2 7.1 %collective-permute-start.4 = (bf16[112,384]{1,0:T(8,128)(2,1)S(1)}, bf16[112,384]{1,0:T(8,128)(2,1)S(1)}, u32[]{:S(2)}, u32[]{:S(2)}) collective-permute-start(bf16[112,384]{1,0:T(8,128)(2,1)S(1)} %reshape.53), channel_id=1, source_target_pairs={{0,16},{1,17},{2,18},{3,19},{4,20},{5,21},{6,22},{7,23},{8,24},{9,... | collective-permute-start | bytes 258056 | tf_op jit(solution)/shard_map/ppermute | solution.py:460
  28.7 6.6 %collective-permute-start.3 = (bf16[112,384]{1,0:T(8,128)(2,1)S(1)}, bf16[112,384]{1,0:T(8,128)(2,1)S(1)}, u32[]{:S(2)}, u32[]{:S(2)}) collective-permute-start(bf16[112,384]{1,0:T(8,128)(2,1)S(1)} %reshape.53), channel_id=1, source_target_pairs={{0,8},{1,9},{2,10},{3,11},{4,12},{5,13},{6,14},{7,15},{8,16},{9,17... | collective-permute-start | bytes 258056 | tf_op jit(solution)/shard_map/ppermute | solution.py:460
  35.4 24.5 %copy-start.3 = (bf16[4,112,384]{2,1,0:T(8,128)(2,1)}, bf16[4,112,384]{2,1,0:T(8,128)(2,1)S(1)}, u32[]{:S(2)}) copy-start(bf16[4,112,384]{2,1,0:T(8,128)(2,1)S(1)} %pad_maximum_fusion.3.refs_7_) | copy-start | bytes 1032196
  35.4 7.1 %copy-start.6 = (bf16[4,128,384]{2,1,0:T(8,128)(2,1)}, bf16[4,128,384]{2,1,0:T(8,128)(2,1)S(1)}, u32[]{:S(2)}) copy-start(bf16[4,128,384]{2,1,0:T(8,128)(2,1)S(1)} %collective-permute-done.8.refs_6_) | copy-start | bytes 1179652
  35.4 7.1 %copy-start.7 = (bf16[4,128,384]{2,1,0:T(8,128)(2,1)}, bf16[4,128,384]{2,1,0:T(8,128)(2,1)S(1)}, u32[]{:S(2)}) copy-start(bf16[4,128,384]{2,1,0:T(8,128)(2,1)S(1)} %collective-permute-done.9.refs_7_) | copy-start | bytes 1179652
  35.5 5.0 %collective-permute-start.13 = (bf16[4,128,384]{2,1,0:T(8,128)(2,1)S(1)}, bf16[4,128,384]{2,1,0:T(8,128)(2,1)S(1)}, u32[]{:S(2)}, u32[]{:S(2)}) collective-permute-start(bf16[4,128,384]{2,1,0:T(8,128)(2,1)S(1)} %pad_maximum_fusion.refs_3_), channel_id=1, source_target_pairs={{0,1},{1,0},{2,3},{3,2},{4,5},{5,4},{6,7},{7,6},{8,9},{9,8},{10,11... | collective-permute-start | bytes 1179656 | tf_op jit(solution)/shard_map/ppermute | solution.py:460
  35.5 5.4 %collective-permute-start.16 = (bf16[4,128,384]{2,1,0:T(8,128)(2,1)S(1)}, bf16[4,128,384]{2,1,0:T(8,128)(2,1)S(1)}, u32[]{:S(2)}, u32[]{:S(2)}) collective-permute-start(bf16[4,128,384]{2,1,0:T(8,128)(2,1)S(1)} %collective-permute-done.8.refs_6_), channel_id=1, source_target_pairs={{0,1},{1,0},{2,3},{3,2},{4,5},{5,4},{6,7},{7,6},{8,9},{9,8},{10,11... | collective-permute-start | bytes 1179656 | tf_op jit(solution)/shard_map/ppermute | solution.py:460
  36.0 6.5 %collective-permute-start.17 = (bf16[4,128,384]{2,1,0:T(8,128)(2,1)S(1)}, bf16[4,128,384]{2,1,0:T(8,128)(2,1)S(1)}, u32[]{:S(2)}, u32[]{:S(2)}) collective-permute-start(bf16[4,128,384]{2,1,0:T(8,128)(2,1)S(1)} %collective-permute-done.9.refs_7_), channel_id=1, source_target_pairs={{0,1},{1,0},{2,3},{3,2},{4,5},{5,4},{6,7},{7,6},{8,9},{9,8},{10,11... | collective-permute-start | bytes 1179656 | tf_op jit(solution)/shard_map/ppermute | solution.py:460
  36.1 2.5 %collective-permute-start.14 = (bf16[2,128,384]{2,1,0:T(8,128)(2,1)S(1)}, bf16[2,128,384]{2,1,0:T(8,128)(2,1)S(1)}, u32[]{:S(2)}, u32[]{:S(2)}) collective-permute-start(bf16[2,128,384]{2,1,0:T(8,128)(2,1)S(1)} %collective-permute-done.6.refs_4_), channel_id=1, source_target_pairs={{0,1},{1,0},{2,3},{3,2},{4,5},{5,4},{6,7},{7,6},{8,9},{9,8},{10,11... | collective-permute-start | bytes 589832 | tf_op jit(solution)/shard_map/ppermute | solution.py:460
  36.5 2.4 %collective-permute-start.15 = (bf16[2,128,384]{2,1,0:T(8,128)(2,1)S(1)}, bf16[2,128,384]{2,1,0:T(8,128)(2,1)S(1)}, u32[]{:S(2)}, u32[]{:S(2)}) collective-permute-start(bf16[2,128,384]{2,1,0:T(8,128)(2,1)S(1)} %collective-permute-done.7.refs_5_), channel_id=1, source_target_pairs={{0,1},{1,0},{2,3},{3,2},{4,5},{5,4},{6,7},{7,6},{8,9},{9,8},{10,11... | collective-permute-start | bytes 589832 | tf_op jit(solution)/shard_map/ppermute | solution.py:460
  38.6 3.9 %copy-start.16 = (bf16[2,128,384]{2,1,0:T(8,128)(2,1)}, bf16[2,128,384]{2,1,0:T(8,128)(2,1)S(1)}, u32[]{:S(2)}) copy-start(bf16[2,128,384]{2,1,0:T(8,128)(2,1)S(1)} %collective-permute-done.14.refs_9_) | copy-start | bytes 589828
  38.6 22.0 %collective-permute-start.18 = (bf16[4,112,384]{2,1,0:T(8,128)(2,1)S(1)}, bf16[4,112,384]{2,1,0:T(8,128)(2,1)S(1)}, u32[]{:S(2)}, u32[]{:S(2)}) collective-permute-start(bf16[4,112,384]{2,1,0:T(8,128)(2,1)S(1)} %pad_maximum_fusion.3.refs_7_), channel_id=1, source_target_pairs={{0,1},{1,0},{2,3},{3,2},{4,5},{5,4},{6,7},{7,6},{8,9},{9,8},{10,11... | collective-permute-start | bytes 1032200 | tf_op jit(solution)/shard_map/ppermute | solution.py:460
  38.9 2.0 %copy-start.17 = (bf16[2,128,384]{2,1,0:T(8,128)(2,1)}, bf16[2,128,384]{2,1,0:T(8,128)(2,1)S(1)}, u32[]{:S(2)}) copy-start(bf16[2,128,384]{2,1,0:T(8,128)(2,1)S(1)} %collective-permute-done.15.refs_10_) | copy-start | bytes 589828
  38.9 21.0 %collective-permute-start.12 = (bf16[4,112,384]{2,1,0:T(8,128)(2,1)S(1)}, bf16[4,112,384]{2,1,0:T(8,128)(2,1)S(1)}, u32[]{:S(2)}, u32[]{:S(2)}) collective-permute-start(bf16[4,112,384]{2,1,0:T(8,128)(2,1)S(1)} %pad_maximum_fusion.3.refs_7_), channel_id=1, source_target_pairs={{0,6},{1,7},{2,4},{3,5},{4,2},{5,3},{6,0},{7,1},{8,14},{9,15},{10,... | collective-permute-start | bytes 1032200 | tf_op jit(solution)/shard_map/ppermute | solution.py:460
  40.4 2.1 %copy-start.8 = (bf16[4,128,384]{2,1,0:T(8,128)(2,1)}, bf16[4,128,384]{2,1,0:T(8,128)(2,1)S(1)}, u32[]{:S(2)}) copy-start(bf16[4,128,384]{2,1,0:T(8,128)(2,1)S(1)} %collective-permute-done.13.refs_8_) | copy-start | bytes 1179652
  40.4 19.5 %collective-permute-start.11 = (bf16[4,112,384]{2,1,0:T(8,128)(2,1)S(1)}, bf16[4,112,384]{2,1,0:T(8,128)(2,1)}, u32[]{:S(2)}, u32[]{:S(2)}) collective-permute-start(bf16[4,112,384]{2,1,0:T(8,128)(2,1)S(1)} %pad_maximum_fusion.3.refs_7_), channel_id=1, source_target_pairs={{0,4},{1,5},{2,6},{3,7},{4,0},{5,1},{6,2},{7,3},{8,12},{9,13},{10,... | collective-permute-start | bytes 1032200 | tf_op jit(solution)/shard_map/ppermute | solution.py:460
  40.9 1.6 %copy-start.9 = (bf16[4,128,384]{2,1,0:T(8,128)(2,1)}, bf16[4,128,384]{2,1,0:T(8,128)(2,1)S(1)}, u32[]{:S(2)}) copy-start(bf16[4,128,384]{2,1,0:T(8,128)(2,1)S(1)} %collective-permute-done.16.refs_11_) | copy-start | bytes 1179652
  40.9 19.0 %collective-permute-start.10 = (bf16[4,112,384]{2,1,0:T(8,128)(2,1)S(1)}, bf16[4,112,384]{2,1,0:T(8,128)(2,1)}, u32[]{:S(2)}, u32[]{:S(2)}) collective-permute-start(bf16[4,112,384]{2,1,0:T(8,128)(2,1)S(1)} %pad_maximum_fusion.3.refs_7_), channel_id=1, source_target_pairs={{0,2},{1,3},{2,0},{3,1},{4,6},{5,7},{6,4},{7,5},{8,10},{9,11},{10,... | collective-permute-start | bytes 1032200 | tf_op jit(solution)/shard_map/ppermute | solution.py:460
  42.6 0.8 copy-start.10
  60.0 2.7 %copy-start.12 = (bf16[4,112,384]{2,1,0:T(8,128)(2,1)}, bf16[4,112,384]{2,1,0:T(8,128)(2,1)S(1)}, u32[]{:S(2)}) copy-start(bf16[4,112,384]{2,1,0:T(8,128)(2,1)S(1)} %collective-permute-done.12.refs_10_) | copy-start | bytes 1032196
  60.0 1.9 %collective-permute-start.19 = (bf16[4,112,384]{2,1,0:T(8,128)(2,1)}, bf16[4,112,384]{2,1,0:T(8,128)(2,1)S(1)}, u32[]{:S(2)}, u32[]{:S(2)}) collective-permute-start(bf16[4,112,384]{2,1,0:T(8,128)(2,1)} %collective-permute-done.10.refs_8_), channel_id=1, source_target_pairs={{0,1},{1,0},{2,3},{3,2},{4,5},{5,4},{6,7},{7,6},{8,9},{9,8},{10,11... | collective-permute-start | bytes 1032200 | tf_op jit(solution)/shard_map/ppermute | solution.py:460
  60.1 2.3 %collective-permute-start.20 = (bf16[4,112,384]{2,1,0:T(8,128)(2,1)}, bf16[4,112,384]{2,1,0:T(8,128)(2,1)S(1)}, u32[]{:S(2)}, u32[]{:S(2)}) collective-permute-start(bf16[4,112,384]{2,1,0:T(8,128)(2,1)} %collective-permute-done.11.refs_9_), channel_id=1, source_target_pairs={{0,1},{1,0},{2,3},{3,2},{4,5},{5,4},{6,7},{7,6},{8,9},{9,8},{10,11... | collective-permute-start | bytes 1032200 | tf_op jit(solution)/shard_map/ppermute | solution.py:460
  60.6 2.1 %collective-permute-start.21 = (bf16[4,112,384]{2,1,0:T(8,128)(2,1)S(1)}, bf16[4,112,384]{2,1,0:T(8,128)(2,1)S(1)}, u32[]{:S(2)}, u32[]{:S(2)}) collective-permute-start(bf16[4,112,384]{2,1,0:T(8,128)(2,1)S(1)} %collective-permute-done.12.refs_10_), channel_id=1, source_target_pairs={{0,1},{1,0},{2,3},{3,2},{4,5},{5,4},{6,7},{7,6},{8,9},{9,8},{10,11... | collective-permute-start | bytes 1032200 | tf_op jit(solution)/shard_map/ppermute | solution.py:460
  60.6 2.1 %copy-start.11 = (bf16[4,112,384]{2,1,0:T(8,128)(2,1)}, bf16[4,112,384]{2,1,0:T(8,128)(2,1)S(1)}, u32[]{:S(2)}) copy-start(bf16[4,112,384]{2,1,0:T(8,128)(2,1)S(1)} %collective-permute-done.18.refs_11_) | copy-start | bytes 1032196
  61.9 0.8 copy-start.13
  62.4 0.7 copy-start.14
  62.7 0.7 copy-start.15
  90.4 10.7 %collective-permute-start.22 = (bf16[16,112,384]{2,1,0:T(8,128)(2,1)}, bf16[16,112,384]{2,1,0:T(8,128)(2,1)S(1)}, u32[]{:S(2)}, u32[]{:S(2)}) collective-permute-start(bf16[16,112,384]{2,1,0:T(8,128)(2,1)} %get-tuple-element.84), channel_id=1, source_target_pairs={{0,1},{1,0},{2,3},{3,2},{4,5},{5,4},{6,7},{7,6},{8,9},{9,8},{10,11... | collective-permute-start | bytes 4128776 | tf_op jit(solution)/shard_map/ppermute | solution.py:460
  90.4 10.6 %copy-start.1 = (bf16[16,112,384]{2,1,0:T(8,128)(2,1)S(1)}, bf16[16,112,384]{2,1,0:T(8,128)(2,1)}, u32[]{:S(2)}) copy-start(bf16[16,112,384]{2,1,0:T(8,128)(2,1)} %get-tuple-element.89) | copy-start | bytes 4128772
  101.6 22.9 %collective-permute-start.23 = (bf16[4,112,384]{2,1,0:T(8,128)(2,1)S(1)}, bf16[4,112,384]{2,1,0:T(8,128)(2,1)S(1)}, u32[]{:S(2)}, u32[]{:S(2)}) collective-permute-start(bf16[4,112,384]{2,1,0:T(8,128)(2,1)S(1)} %get-tuple-element.97), channel_id=1, source_target_pairs={{0,2},{1,3},{2,0},{3,1},{4,6},{5,7},{6,4},{7,5},{8,10},{9,11},{10,... | collective-permute-start | bytes 1032200 | tf_op jit(solution)/shard_map/ppermute | solution.py:460
  108.4 17.0 %collective-permute-start.24 = (bf16[4,112,384]{2,1,0:T(8,128)(2,1)S(1)}, bf16[4,112,384]{2,1,0:T(8,128)(2,1)S(1)}, u32[]{:S(2)}, u32[]{:S(2)}) collective-permute-start(bf16[4,112,384]{2,1,0:T(8,128)(2,1)S(1)} %get-tuple-element.98), channel_id=1, source_target_pairs={{0,4},{1,5},{2,6},{3,7},{4,0},{5,1},{6,2},{7,3},{8,12},{9,13},{10,... | collective-permute-start | bytes 1032200 | tf_op jit(solution)/shard_map/ppermute | solution.py:460
  110.1 17.1 %collective-permute-start.25 = (bf16[4,112,384]{2,1,0:T(8,128)(2,1)S(1)}, bf16[4,112,384]{2,1,0:T(8,128)(2,1)S(1)}, u32[]{:S(2)}, u32[]{:S(2)}) collective-permute-start(bf16[4,112,384]{2,1,0:T(8,128)(2,1)S(1)} %get-tuple-element.99), channel_id=1, source_target_pairs={{0,6},{1,7},{2,4},{3,5},{4,2},{5,3},{6,0},{7,1},{8,14},{9,15},{10,... | collective-permute-start | bytes 1032200 | tf_op jit(solution)/shard_map/ppermute | solution.py:460
  127.2 4.9 %copy-start.2 = (bf16[8,128,384]{2,1,0:T(8,128)(2,1)S(1)}, bf16[8,128,384]{2,1,0:T(8,128)(2,1)}, u32[]{:S(2)}) copy-start(bf16[8,128,384]{2,1,0:T(8,128)(2,1)} %get-tuple-element.106) | copy-start | bytes 2359300
  127.2 2.6 %collective-permute-start.26 = (bf16[8,128,384]{2,1,0:T(8,128)(2,1)}, bf16[8,128,384]{2,1,0:T(8,128)(2,1)S(1)}, u32[]{:S(2)}, u32[]{:S(2)}) collective-permute-start(bf16[8,128,384]{2,1,0:T(8,128)(2,1)} %get-tuple-element.105), channel_id=1, source_target_pairs={{0,1},{1,0},{2,3},{3,2},{4,5},{5,4},{6,7},{7,6},{8,9},{9,8},{10,11... | collective-permute-start | bytes 2359304 | tf_op jit(solution)/shard_map/ppermute | solution.py:460
  127.6 4.5 %collective-permute-start.30 = (bf16[8,128,384]{2,1,0:T(8,128)(2,1)}, bf16[8,128,384]{2,1,0:T(8,128)(2,1)S(1)}, u32[]{:S(2)}, u32[]{:S(2)}) collective-permute-start(bf16[8,128,384]{2,1,0:T(8,128)(2,1)} %get-tuple-element.107), channel_id=1, source_target_pairs={{0,1},{1,0},{2,3},{3,2},{4,5},{5,4},{6,7},{7,6},{8,9},{9,8},{10,11... | collective-permute-start | bytes 2359304 | tf_op jit(solution)/shard_map/ppermute | solution.py:460
  131.1 11.5 %collective-permute-start.27 = (bf16[4,128,384]{2,1,0:T(8,128)(2,1)S(1)}, bf16[4,128,384]{2,1,0:T(8,128)(2,1)S(1)}, u32[]{:S(2)}, u32[]{:S(2)}) collective-permute-start(bf16[4,128,384]{2,1,0:T(8,128)(2,1)S(1)} %slice.166), channel_id=1, source_target_pairs={{0,2},{1,3},{2,0},{3,1},{4,6},{5,7},{6,4},{7,5},{8,10},{9,11},{10,... | collective-permute-start | bytes 1179656 | tf_op jit(solution)/shard_map/ppermute | solution.py:460
  132.4 11.9 %collective-permute-start.31 = (bf16[4,128,384]{2,1,0:T(8,128)(2,1)S(1)}, bf16[4,128,384]{2,1,0:T(8,128)(2,1)S(1)}, u32[]{:S(2)}, u32[]{:S(2)}) collective-permute-start(bf16[4,128,384]{2,1,0:T(8,128)(2,1)S(1)} %slice.165), channel_id=1, source_target_pairs={{0,4},{1,5},{2,6},{3,7},{4,0},{5,1},{6,2},{7,3},{8,12},{9,13},{10,... | collective-permute-start | bytes 1179656 | tf_op jit(solution)/shard_map/ppermute | solution.py:460
  134.5 16.4 %collective-permute-start.35 = (bf16[112,384]{1,0:T(8,128)(2,1)S(1)}, bf16[112,384]{1,0:T(8,128)(2,1)S(1)}, u32[]{:S(2)}, u32[]{:S(2)}) collective-permute-start(bf16[112,384]{1,0:T(8,128)(2,1)S(1)} %get-tuple-element.126), channel_id=1, source_target_pairs={{0,8},{1,9},{2,10},{3,11},{4,12},{5,13},{6,14},{7,15},{8,16},{9,17... | collective-permute-start | bytes 258056 | tf_op jit(solution)/shard_map/ppermute | solution.py:460
  134.9 19.3 %collective-permute-start.37 = (bf16[112,384]{1,0:T(8,128)(2,1)S(1)}, bf16[112,384]{1,0:T(8,128)(2,1)S(1)}, u32[]{:S(2)}, u32[]{:S(2)}) collective-permute-start(bf16[112,384]{1,0:T(8,128)(2,1)S(1)} %get-tuple-element.127), channel_id=1, source_target_pairs={{0,24},{1,25},{2,26},{3,27},{4,28},{5,29},{6,30},{7,31},{8,0},{9,1... | collective-permute-start | bytes 258056 | tf_op jit(solution)/shard_map/ppermute | solution.py:460
  138.4 15.8 %collective-permute-start.36 = (bf16[112,384]{1,0:T(8,128)(2,1)S(1)}, bf16[112,384]{1,0:T(8,128)(2,1)S(1)}, u32[]{:S(2)}, u32[]{:S(2)}) collective-permute-start(bf16[112,384]{1,0:T(8,128)(2,1)S(1)} %get-tuple-element.128), channel_id=1, source_target_pairs={{0,16},{1,17},{2,18},{3,19},{4,20},{5,21},{6,22},{7,23},{8,24},{9,... | collective-permute-start | bytes 258056 | tf_op jit(solution)/shard_map/ppermute | solution.py:460
  142.7 6.4 %collective-permute-start.28 = (bf16[2,128,384]{2,1,0:T(8,128)(2,1)S(1)}, bf16[2,128,384]{2,1,0:T(8,128)(2,1)S(1)}, u32[]{:S(2)}, u32[]{:S(2)}) collective-permute-start(bf16[2,128,384]{2,1,0:T(8,128)(2,1)S(1)} %fusion.4), channel_id=1, source_target_pairs={{0,4},{1,5},{2,6},{3,7},{4,0},{5,1},{6,2},{7,3},{8,12},{9,13},{10,... | collective-permute-start | bytes 589832 | tf_op jit(solution)/shard_map/ppermute | solution.py:460
  144.4 6.1 %collective-permute-start.32 = (bf16[2,128,384]{2,1,0:T(8,128)(2,1)S(1)}, bf16[2,128,384]{2,1,0:T(8,128)(2,1)S(1)}, u32[]{:S(2)}, u32[]{:S(2)}) collective-permute-start(bf16[2,128,384]{2,1,0:T(8,128)(2,1)S(1)} %fusion.3), channel_id=1, source_target_pairs={{0,2},{1,3},{2,0},{3,1},{4,6},{5,7},{6,4},{7,5},{8,10},{9,11},{10,... | collective-permute-start | bytes 589832 | tf_op jit(solution)/shard_map/ppermute | solution.py:460
  149.2 7.4 %collective-permute-start.29 = (bf16[128,384]{1,0:T(8,128)(2,1)S(1)}, bf16[128,384]{1,0:T(8,128)(2,1)S(1)}, u32[]{:S(2)}, u32[]{:S(2)}) collective-permute-start(bf16[128,384]{1,0:T(8,128)(2,1)S(1)} %fusion.11), channel_id=1, source_target_pairs={{0,8},{1,9},{2,10},{3,11},{4,12},{5,13},{6,14},{7,15},{8,16},{9,17... | collective-permute-start | bytes 294920 | tf_op jit(solution)/shard_map/ppermute | solution.py:460
  150.6 8.5 %collective-permute-start.33 = (bf16[128,384]{1,0:T(8,128)(2,1)S(1)}, bf16[128,384]{1,0:T(8,128)(2,1)S(1)}, u32[]{:S(2)}, u32[]{:S(2)}) collective-permute-start(bf16[128,384]{1,0:T(8,128)(2,1)S(1)} %get-tuple-element.129), channel_id=1, source_target_pairs={{0,16},{1,17},{2,18},{3,19},{4,20},{5,21},{6,22},{7,23},{8,24},{9,... | collective-permute-start | bytes 294920 | tf_op jit(solution)/shard_map/ppermute | solution.py:460
  150.9 8.3 %collective-permute-start.34 = (bf16[128,384]{1,0:T(8,128)(2,1)S(1)}, bf16[128,384]{1,0:T(8,128)(2,1)S(1)}, u32[]{:S(2)}, u32[]{:S(2)}) collective-permute-start(bf16[128,384]{1,0:T(8,128)(2,1)S(1)} %get-tuple-element.130), channel_id=1, source_target_pairs={{0,24},{1,25},{2,26},{3,27},{4,28},{5,29},{6,30},{7,31},{8,0},{9,1... | collective-permute-start | bytes 294920 | tf_op jit(solution)/shard_map/ppermute | solution.py:460

commit v5 on v4

--- a/solution.py
+++ b/solution.py
@@ -115,20 +115,22 @@
         at += slots
 
 
-def emit(scal_ref, base, out_refs, rows_ref):
+def emit(scal_ref, base, out_refs, stage_refs, sem_refs, rows_ref):
     at = base
-    for ref in out_refs:
+    for out_ref, ref, sem in zip(out_refs, stage_refs, sem_refs):
         slots, height = ref.shape[0], ref.shape[1]
 
-        def one(slot, carry, ref=ref, at=at, height=height):
+        def one(slot, carry, out_ref=out_ref, ref=ref, sem=sem, at=at, height=height):
             start = pl.multiple_of(scal_ref[at + slot] * 8, 8)
             for tile in range(TILES):
-                lanes = slice(tile * LANES, (tile + 1) * LANES)
-                ref[slot, :, lanes] = rows_ref[tile, pl.ds(start, height), :].astype(ref.dtype)
+                ref[slot, :, lanes_of(tile)] = rows_ref[tile, pl.ds(start, height), :].astype(ref.dtype)
+            pltpu.make_async_copy(ref.at[slot], out_ref.at[slot], sem).start()
             return carry
 
         lax.fori_loop(0, slots, one, 0)
         at += slots
+    for out_ref, ref, sem in zip(out_refs, stage_refs, sem_refs):
+        pltpu.make_async_copy(ref, out_ref, sem).wait()
 
 
 def lanes_of(tile, offset=0):
@@ -206,9 +208,9 @@
     outs = refs[n_pieces : n_pieces + 5 + n_out]
     out_ref, dx_ref, dmixed_ref, dmod_ref, dproj_ref = outs[:5]
     send_refs = outs[5:]
-    rows_ref, fc1_ref, fc2_ref, bias_ref, act_ref, slope_ref, du_ref, dfc1_ref, dfc2_ref, dbias_ref = refs[
-        n_pieces + 5 + n_out :
-    ]
+    scratch = refs[n_pieces + 5 + n_out :]
+    rows_ref, fc1_ref, fc2_ref, bias_ref, act_ref, slope_ref, du_ref, dfc1_ref, dfc2_ref, dbias_ref = scratch[:10]
+    stage_refs, sem_refs = scratch[10 : 10 + n_out], scratch[10 + n_out :]
     step = pl.program_id(0)
     last = pl.num_programs(0) - 1
 
@@ -302,7 +304,7 @@
             rows_ref[tile, pl.ds(FC2_AT, FF), :] = dfc2_ref[lanes_of(tile), :].T
             rows_ref[tile, pl.ds(B_FC2_AT, 1), :] = dbias_ref[1:2, lanes_of(tile)]
             rows_ref[tile, pl.ds(B_PROJ_AT, 1), :] = dbias_ref[2:3, lanes_of(tile)]
-        emit(scal_ref, 1 + sum(ref.shape[0] for ref in pieces), send_refs, rows_ref)
+        emit(scal_ref, 1 + sum(ref.shape[0] for ref in pieces), send_refs, stage_refs, sem_refs, rows_ref)
 
 
 def attend_back_kernel(scal_ref, qkv_ref, probs_ref, dmixed_ref, dqkv_ref, dprobs_ref, low_ref, dq_t_ref):
@@ -341,7 +343,9 @@
 ):
     grad_x_ref, grad_cond_ref = refs[:2]
     send_refs = refs[2 : 2 + n_out]
-    rows_ref, dqkv_w_ref, dmod_ref, dbias_ref, ada_ref, ada_sem = refs[2 + n_out :]
+    scratch = refs[2 + n_out :]
+    rows_ref, dqkv_w_ref, dmod_ref, dbias_ref, ada_ref, ada_sem = scratch[:6]
+    stage_refs, sem_refs = scratch[6 : 6 + n_out], scratch[6 + n_out :]
     fetch = pltpu.make_async_copy(ada_hbm_ref, ada_ref, ada_sem)
     step = pl.program_id(0)
     last = pl.num_programs(0) - 1
@@ -395,7 +399,7 @@
             rows_ref[tile, pl.ds(PROJ_AT, D), :] = dproj_ref[:, lanes_of(tile)]
             rows_ref[tile, pl.ds(B_QV_AT, 1), :] = dbias_ref[0:1, lanes_of(tile)]
             rows_ref[tile, pl.ds(B_QV_AT + 1, 1), :] = dbias_ref[0:1, lanes_of(tile, 2 * D)]
-        emit(scal_ref, base, send_refs, rows_ref)
+        emit(scal_ref, base, send_refs, stage_refs, sem_refs, rows_ref)
 
 
 class Direct:
@@ -468,10 +472,12 @@
         by_y = self.shift(second, dy=1)
         by_xy = self.shift(jnp.concatenate([first, by_x]), dy=1)
         by_yx = self.shift(jnp.concatenate([second, by_y]), dx=1)
-        return [own, by_x, by_y, by_xy, by_yx]
+        return [own, by_x, by_y, by_xy, by_yx, jnp.concatenate([own, by_x, by_y])]
 
     def pass_on(self, held):
-        return held + [self.shift(array, dc=1) for array in held]
+        early = held[-1]
+        held = held[:-1]
+        return held + [self.shift(array, dc=1) for array in (early, *held[3:])]
 
     def begin(self, parts):
         send_a, send_b, keep_a, keep_b = parts
@@ -509,6 +515,9 @@
         self.gathered = [device(-k, dy, dx, dc) for dc in (0, 1) for dy, dx in sides for k in range(4)]
         self.sent = [device(k, dy, dx, dc) for dc in (1, 0) for dy, dx in sides for k in range(4)]
         self.slots = [(16, BF16)] * 2
+
+    def pass_on(self, held):
+        return held + [self.shift(array, dc=1) for array in held]
 
     def join(self, own, others):
         half = len(others) // 2
@@ -651,7 +660,7 @@
             [whole(), whole(), by_latent(MLP_STEP, seq, D), by_latent(MLP_STEP, seq, D), by_latent(MLP_STEP, D, seq), by_latent(MLP_STEP, seq, D)]
             + [whole()] * n_mlp_pieces,
             [by_latent(MLP_STEP, seq, D), by_latent(MLP_STEP, seq, D), by_latent(MLP_STEP, seq, D), whole(), whole()]
-            + [whole()] * n_mlp_out,
+            + [pl.BlockSpec(memory_space=pl.ANY)] * n_mlp_out,
             [
                 struct((count, seq, D), BF16),
                 struct((count, seq, D), F32),
@@ -671,7 +680,9 @@
                 pltpu.VMEM((D, FF), F32),
                 pltpu.VMEM((D, FF), F32),
                 pltpu.VMEM((8, FF), F32),
-            ],
+            ]
+            + [pltpu.VMEM((slots, mlp_height, D), kind) for slots, kind in mlp_plan.slots]
+            + [pltpu.SemaphoreType.DMA] * n_mlp_out,
             [mlp_scal, mod, proj, latents, branch, mixed, cotangent] + mlp_pieces,
             30 * 10**9,
         )
@@ -699,7 +710,7 @@
             lambda *refs: finish_kernel(n_out, 1 + devices, *refs),
             count // FINISH_STEP,
             [whole()] * 3 + [pl.BlockSpec(memory_space=pl.ANY)] + [whole()] * 2 + [by_latent(FINISH_STEP, seq, D), by_latent(FINISH_STEP, seq, 3 * D), by_latent(FINISH_STEP, seq, D)],
-            [by_latent(FINISH_STEP, seq, D), whole()] + [whole()] * n_out,
+            [by_latent(FINISH_STEP, seq, D), whole()] + [pl.BlockSpec(memory_space=pl.ANY)] * n_out,
             [struct((count, seq, D), F32), struct((count, D), F32)]
             + [struct((slots, attn_height, D), kind) for slots, kind in plan.slots],
             [
@@ -709,7 +720,9 @@
                 pltpu.VMEM((8, 3 * D), F32),
                 pltpu.VMEM((6, D, D), BF16),
                 pltpu.SemaphoreType.DMA,
-            ],
+            ]
+            + [pltpu.VMEM((slots, attn_height, D), kind) for slots, kind in plan.slots]
+            + [pltpu.SemaphoreType.DMA] * n_out,
             [attn_scal, mod, qkv_w, condition, ada, dmod, dproj, latents, grad_qkv, grad_middle],
             15 * 10**9,
         )

time: 161 us -> 160 us (level)
  starting transfers between devices: 45.6 us -> 56.8 us
  waiting for transfers between devices: 34.5 us -> 26.8 us
  Pallas kernels: 67 us -> 62.3 us
    ppermute x38 -> x36, starting transfers between devices: 45.6 us -> 56.8 us  [shift(): return lax.ppermute(values, AXIS, pairs)]
    ppermute x38 -> x36, waiting for transfers between devices: 34.5 us -> 26.8 us  [shift(): return lax.ppermute(values, AXIS, pairs)]
    pallas_call x4, Pallas kernels: 67 us -> 62.3 us  [call(): pl.pallas_call(kernel, grid_spec=pltpu.PrefetchScalarGridSpec(num_scalar_...]
  transfers between devices with their start and end apart: 38 -> 36, of which waited for: 17 -> 15; matrix products, arithmetic and copies ran while one was open for 4% -> 4% of each run, Pallas kernels for 25% -> 24%
where the time goes in v5:
time: 160 us; the launch traced here: 159 us
  Pallas kernels  62.3 us (39%)
  starting transfers between devices  56.8 us (36%)
  waiting for transfers between devices  26.8 us (17%)
  local copies, waits for them, and re-layouts  8.2 us (5%)
  other arithmetic  3.29 us (2%)
  between operations  1.78 us (1%)
    pallas_call x4, Pallas kernels, call(): pl.pallas_call(kernel, grid_spec=pltpu.PrefetchScalarGridSpec(num_scalar_...  62.3 us
    ppermute x36, starting transfers between devices, shift(): return lax.ppermute(values, AXIS, pairs)  56.8 us
    ppermute x36, waiting for transfers between devices, shift(): return lax.ppermute(values, AXIS, pairs)  26.8 us
    dynamic_update_slice x2, local copies, waits for them, and re-layouts, to_piece(): lax.dynamic_update_slice(flat, share, (size * me % GROUP,)).reshape(rows, D)  3.89 us
  transfers between devices with their start and end apart: 36, of which 15 were waited for; matrix products, arithmetic and copies ran while one was open for 4% of the time, Pallas kernels for 24%

profile of v5, /device:TPU:0, one launch (start us, length us, event | category | flops | bytes accessed | tf_op | source)
XLA Modules:
  0.0 159.2 jit_solution(4830574000321099100)
XLA Ops:
  0.7 2.0 %dynamic_update_slice.6 = bf16[49152]{0:T(1024)(128)(2,1)S(1)} dynamic-update-slice(bf16[49152]{0:T(1024)(128)(2,1)S(1)} %broadcast_in_dim.6, bf16[46176]{0:T(1024)(128)(2,1)} %param.8, s32[]{:T(128)S(6)} %select_n.1113) | dynamic-update-slice | bytes 184708 | tf_op jit(solution)/shard_map/dynamic_update_slice | solution.py:555
  2.7 5.1 %collective-permute-start.2 = (bf16[128,384]{1,0:T(8,128)(2,1)S(1)}, bf16[128,384]{1,0:T(8,128)(2,1)S(1)}, u32[]{:S(2)}, u32[]{:S(2)}) collective-permute-start(bf16[128,384]{1,0:T(8,128)(2,1)S(1)} %reshape.52), channel_id=1, source_target_pairs={{0,24},{1,25},{2,26},{3,27},{4,28},{5,29},{6,30},{7,31},{8,0},{9,1... | collective-permute-start | bytes 294920 | tf_op jit(solution)/shard_map/ppermute | solution.py:464
  7.8 1.0 collective-permute-start
  8.9 1.9 %dynamic_update_slice.7 = bf16[43008]{0:T(1024)(128)(2,1)S(1)} dynamic-update-slice(bf16[43008]{0:T(1024)(128)(2,1)S(1)} %broadcast_in_dim.7, bf16[36936]{0:T(1024)(128)(2,1)} %param.9, s32[]{:T(128)S(6)} %select_n.1115) | dynamic-update-slice | bytes 147748 | tf_op jit(solution)/shard_map/dynamic_update_slice | solution.py:555
  10.9 0.1 stack.338
  11.1 5.5 %collective-permute-done.1 = bf16[128,384]{1,0:T(8,128)(2,1)S(1)} collective-permute-done((bf16[128,384]{1,0:T(8,128)(2,1)S(1)}, bf16[128,384]{1,0:T(8,128)(2,1)S(1)}, u32[]{:S(2)}, u32[]{:S(2)}) %collective-permute-start.1) | collective-permute-done | bytes 98336 | tf_op jit(solution)/shard_map/ppermute | solution.py:464
  16.7 1.6 collective-permute-start.7
  18.3 1.5 collective-permute-start.6
  19.8 0.2 stack.339
  19.9 4.4 %collective-permute-done.6.refs_4_ = bf16[2,128,384]{2,1,0:T(8,128)(2,1)S(1)} collective-permute-done((bf16[2,128,384]{2,1,0:T(8,128)(2,1)S(1)}, bf16[2,128,384]{2,1,0:T(8,128)(2,1)S(1)}, u32[]{:S(2)}, u32[]{:S(2)}) %collective-permute-start.6) | collective-permute-done | bytes 196640 | tf_op jit(solution)/shard_map/ppermute | solution.py:464
  24.4 0.6 collective-permute-start.8
  25.0 1.6 collective-permute-start.9
  27.2 1.6 %collective-permute-start.5 = (bf16[112,384]{1,0:T(8,128)(2,1)S(1)}, bf16[112,384]{1,0:T(8,128)(2,1)S(1)}, u32[]{:S(2)}, u32[]{:S(2)}) collective-permute-start(bf16[112,384]{1,0:T(8,128)(2,1)S(1)} %reshape.53), channel_id=1, source_target_pairs={{0,24},{1,25},{2,26},{3,27},{4,28},{5,29},{6,30},{7,31},{8,0},{9,1... | collective-permute-start | bytes 258056 | tf_op jit(solution)/shard_map/ppermute | solution.py:464
  28.9 0.5 collective-permute-start.4
  29.4 1.9 %collective-permute-start.3 = (bf16[112,384]{1,0:T(8,128)(2,1)S(1)}, bf16[112,384]{1,0:T(8,128)(2,1)S(1)}, u32[]{:S(2)}, u32[]{:S(2)}) collective-permute-start(bf16[112,384]{1,0:T(8,128)(2,1)S(1)} %reshape.53), channel_id=1, source_target_pairs={{0,8},{1,9},{2,10},{3,11},{4,12},{5,13},{6,14},{7,15},{8,16},{9,17... | collective-permute-start | bytes 258056 | tf_op jit(solution)/shard_map/ppermute | solution.py:464
  31.3 0.7 pad_add_fusion
  32.0 0.7 collective-permute-done.5
  32.7 3.3 %collective-permute-done.4 = bf16[112,384]{1,0:T(8,128)(2,1)S(1)} collective-permute-done((bf16[112,384]{1,0:T(8,128)(2,1)S(1)}, bf16[112,384]{1,0:T(8,128)(2,1)S(1)}, u32[]{:S(2)}, u32[]{:S(2)}) %collective-permute-start.4) | collective-permute-done | bytes 86048 | tf_op jit(solution)/shard_map/ppermute | solution.py:464
  36.1 0.1 pad_maximum_fusion
  36.3 0.5 collective-permute-start.14
  36.8 0.1 collective-permute-start.15
  36.9 0.4 collective-permute-start.16
  37.3 1.5 collective-permute-start.12
  38.8 0.3 collective-permute-done.14.refs_9_
  39.2 1.5 collective-permute-start.11
  40.7 0.5 collective-permute-start.10
  41.2 0.2 copy-done.10
  41.4 0.9 copy-done.6
  42.3 14.9 %shard_map.101 = (f32[6,8,384]{2,1,0:T(8,128)}, bf16[6,384,384]{2,1,0:T(8,128)(2,1)}, bf16[384,1152]{1,0:T(8,128)(2,1)}, bf16[384,384]{1,0:T(8,128)(2,1)}, f32[8...) custom-call(s32[65]{0:T(128)} %get-tuple-element.66.refs_0_.scal_ref, ...), custom_call_target="tpu_custom_call" | custom-call | flops 15000000512 | bytes 20971520 | tf_op jit(solution)/shard_map/pallas_call | solution.py:572
  57.3 1.6 collective-permute-start.17
  58.9 0.1 collective-permute-start.18
  59.0 0.4 collective-permute-start.19
  59.4 1.0 collective-permute-done.17.refs_12_
  60.4 0.5 collective-permute-done.18.refs_13_
  60.9 0.3 collective-permute-done.19.refs_14_
  61.1 0.4 copy-done.14
  61.6 0.3 copy-done.15
  61.9 23.5 %shard_map.102 = (bf16[8,256,384]{2,1,0:T(8,128)(2,1)}, f32[8,256,384]{2,1,0:T(8,128)}, bf16[8,256,384]{2,1,0:T(8,128)(2,1)}, f32[4,8,384]{2,1,0:T(8,128)}, f32[...) custom-call(s32[65]{0:T(128)} %get-tuple-element.64.refs_0_, ...), custom_call_target="tpu_custom_call" | custom-call | flops 30000001024 | bytes 20971520 | tf_op jit(solution)/shard_map/pallas_call | solution.py:572
  85.4 3.9 %collective-permute-start.20 = (bf16[16,112,384]{2,1,0:T(8,128)(2,1)}, bf16[16,112,384]{2,1,0:T(8,128)(2,1)S(1)}, u32[]{:S(2)}, u32[]{:S(2)}) collective-permute-start(bf16[16,112,384]{2,1,0:T(8,128)(2,1)} %get-tuple-element.86), channel_id=1, source_target_pairs={{0,1},{1,0},{2,3},{3,2},{4,5},{5,4},{6,7},{7,6},{8,9},{9,8},{10,11... | collective-permute-start | bytes 4128776 | tf_op jit(solution)/shard_map/ppermute | solution.py:464
  89.3 10.7 %shard_map.103.refs_8_ = bf16[8,256,1152]{2,1,0:T(8,128)(2,1)} custom-call(s32[65]{0:T(128)} %get-tuple-element.66.refs_0_.scal_ref, bf16[8,256,1152]{2,1,0:T(8,128)(2,1)} %get-tuple-element.88.qkv_ref, bf16[8,6,256,256]{3,2,1,0:T(8,128)(2,1)} %get-tuple-element.89.probs_ref, bf16[8,256,384]{2,1,0:T(8,128)(2,1)} %get-tuple-element.90.dmixed_ref), custom_call_target="tpu_custom_call" | custom-call | flops 12999999488 | bytes 20971520 | tf_op jit(solution)/shard_map/pallas_call | solution.py:572
  100.0 0.4 fusion.12
  100.4 0.1 fusion.14
  100.6 11.0 %collective-permute-start.22 = (bf16[4,112,384]{2,1,0:T(8,128)(2,1)S(1)}, bf16[4,112,384]{2,1,0:T(8,128)(2,1)S(1)}, u32[]{:S(2)}, u32[]{:S(2)}) collective-permute-start(bf16[4,112,384]{2,1,0:T(8,128)(2,1)S(1)} %get-tuple-element.100), channel_id=1, source_target_pairs={{0,4},{1,5},{2,6},{3,7},{4,0},{5,1},{6,2},{7,3},{8,12},{9,13},{10,... | collective-permute-start | bytes 1032200 | tf_op jit(solution)/shard_map/ppermute | solution.py:464
  111.7 13.1 %shard_map.104 = (f32[8,256,384]{2,1,0:T(8,128)}, f32[8,384]{1,0:T(8,128)}, bf16[8,128,384]{2,1,0:T(8,128)(2,1)}, bf16[8,128,384]{2,1,0:T(8,128)(2,1)}, bf16[8,1...) custom-call(s32[65]{0:T(128)} %get-tuple-element.66.refs_0_.scal_ref, f32[6,8,384]{2,1,0:T(8,128)} %get-tuple-element.74.refs_1_, ...), custom_call_target="tpu_custom_call" | custom-call | flops 15000000512 | bytes 20971520 | tf_op jit(solution)/shard_map/pallas_call | solution.py:572
  124.9 0.5 collective-permute-start.28
  125.4 2.0 %collective-permute-done.24 = bf16[8,128,384]{2,1,0:T(8,128)(2,1)S(1)} collective-permute-done((bf16[8,128,384]{2,1,0:T(8,128)(2,1)}, bf16[8,128,384]{2,1,0:T(8,128)(2,1)S(1)}, u32[]{:S(2)}, u32[]{:S(2)}) %collective-permute-start.24) | collective-permute-done | bytes 786464 | tf_op jit(solution)/shard_map/ppermute | solution.py:464
  127.4 1.3 convert_add_fusion.2
  128.7 1.5 collective-permute-start.25
  130.3 0.2 convert_add_fusion.1
  130.5 3.7 %collective-permute-start.29 = (bf16[4,128,384]{2,1,0:T(8,128)(2,1)S(1)}, bf16[4,128,384]{2,1,0:T(8,128)(2,1)S(1)}, u32[]{:S(2)}, u32[]{:S(2)}) collective-permute-start(bf16[4,128,384]{2,1,0:T(8,128)(2,1)S(1)} %slice.165), channel_id=1, source_target_pairs={{0,4},{1,5},{2,6},{3,7},{4,0},{5,1},{6,2},{7,3},{8,12},{9,13},{10,... | collective-permute-start | bytes 1179656 | tf_op jit(solution)/shard_map/ppermute | solution.py:464
  134.2 0.2 fusion.13
  134.5 3.8 %collective-permute-start.35 = (bf16[112,384]{1,0:T(8,128)(2,1)S(1)}, bf16[112,384]{1,0:T(8,128)(2,1)S(1)}, u32[]{:S(2)}, u32[]{:S(2)}) collective-permute-start(bf16[112,384]{1,0:T(8,128)(2,1)S(1)} %get-tuple-element.129), channel_id=1, source_target_pairs={{0,24},{1,25},{2,26},{3,27},{4,28},{5,29},{6,30},{7,31},{8,0},{9,1... | collective-permute-start | bytes 258056 | tf_op jit(solution)/shard_map/ppermute | solution.py:464
  138.3 1.6 %collective-permute-done.25 = bf16[4,128,384]{2,1,0:T(8,128)(2,1)S(1)} collective-permute-done((bf16[4,128,384]{2,1,0:T(8,128)(2,1)S(1)}, bf16[4,128,384]{2,1,0:T(8,128)(2,1)S(1)}, u32[]{:S(2)}, u32[]{:S(2)}) %collective-permute-start.25) | collective-permute-done | bytes 393248 | tf_op jit(solution)/shard_map/ppermute | solution.py:464
  140.0 3.5 %collective-permute-start.26 = (bf16[2,128,384]{2,1,0:T(8,128)(2,1)S(1)}, bf16[2,128,384]{2,1,0:T(8,128)(2,1)S(1)}, u32[]{:S(2)}, u32[]{:S(2)}) collective-permute-start(bf16[2,128,384]{2,1,0:T(8,128)(2,1)S(1)} %fusion.4), channel_id=1, source_target_pairs={{0,4},{1,5},{2,6},{3,7},{4,0},{5,1},{6,2},{7,3},{8,12},{9,13},{10,... | collective-permute-start | bytes 589832 | tf_op jit(solution)/shard_map/ppermute | solution.py:464
  143.6 1.8 %collective-permute-start.30 = (bf16[2,128,384]{2,1,0:T(8,128)(2,1)S(1)}, bf16[2,128,384]{2,1,0:T(8,128)(2,1)S(1)}, u32[]{:S(2)}, u32[]{:S(2)}) collective-permute-start(bf16[2,128,384]{2,1,0:T(8,128)(2,1)S(1)} %fusion.3), channel_id=1, source_target_pairs={{0,2},{1,3},{2,0},{3,1},{4,6},{5,7},{6,4},{7,5},{8,10},{9,11},{10,... | collective-permute-start | bytes 589832 | tf_op jit(solution)/shard_map/ppermute | solution.py:464
  145.4 2.8 %collective-permute-done.26 = bf16[2,128,384]{2,1,0:T(8,128)(2,1)S(1)} collective-permute-done((bf16[2,128,384]{2,1,0:T(8,128)(2,1)S(1)}, bf16[2,128,384]{2,1,0:T(8,128)(2,1)S(1)}, u32[]{:S(2)}, u32[]{:S(2)}) %collective-permute-start.26) | collective-permute-done | bytes 196640 | tf_op jit(solution)/shard_map/ppermute | solution.py:464
  148.3 1.1 collective-permute-start.27
  149.4 0.5 collective-permute-done.30
  149.9 1.8 %collective-permute-start.31 = (bf16[128,384]{1,0:T(8,128)(2,1)S(1)}, bf16[128,384]{1,0:T(8,128)(2,1)S(1)}, u32[]{:S(2)}, u32[]{:S(2)}) collective-permute-start(bf16[128,384]{1,0:T(8,128)(2,1)S(1)} %get-tuple-element.131), channel_id=1, source_target_pairs={{0,16},{1,17},{2,18},{3,19},{4,20},{5,21},{6,22},{7,23},{8,24},{9,... | collective-permute-start | bytes 294920 | tf_op jit(solution)/shard_map/ppermute | solution.py:464
  151.7 1.9 %collective-permute-start.32 = (bf16[128,384]{1,0:T(8,128)(2,1)S(1)}, bf16[128,384]{1,0:T(8,128)(2,1)S(1)}, u32[]{:S(2)}, u32[]{:S(2)}) collective-permute-start(bf16[128,384]{1,0:T(8,128)(2,1)S(1)} %get-tuple-element.132), channel_id=1, source_target_pairs={{0,24},{1,25},{2,26},{3,27},{4,28},{5,29},{6,30},{7,31},{8,0},{9,1... | collective-permute-start | bytes 294920 | tf_op jit(solution)/shard_map/ppermute | solution.py:464
  153.7 0.8 dynamic_slice.7
  154.5 1.4 collective-permute-done.27
  155.9 2.4 %collective-permute-done.31 = bf16[128,384]{1,0:T(8,128)(2,1)S(1)} collective-permute-done((bf16[128,384]{1,0:T(8,128)(2,1)S(1)}, bf16[128,384]{1,0:T(8,128)(2,1)S(1)}, u32[]{:S(2)}, u32[]{:S(2)}) %collective-permute-start.31) | collective-permute-done | bytes 98336 | tf_op jit(solution)/shard_map/ppermute | solution.py:464
  158.4 0.8 dynamic_slice.6
  (85 shorter events, 1.5 us)
Async XLA Ops:
  2.7 8.3 %collective-permute-start.2 = (bf16[128,384]{1,0:T(8,128)(2,1)S(1)}, bf16[128,384]{1,0:T(8,128)(2,1)S(1)}, u32[]{:S(2)}, u32[]{:S(2)}) collective-permute-start(bf16[128,384]{1,0:T(8,128)(2,1)S(1)} %reshape.52), channel_id=1, source_target_pairs={{0,24},{1,25},{2,26},{3,27},{4,28},{5,29},{6,30},{7,31},{8,0},{9,1... | collective-permute-start | bytes 294920 | tf_op jit(solution)/shard_map/ppermute | solution.py:464
  7.8 8.8 %collective-permute-start.1 = (bf16[128,384]{1,0:T(8,128)(2,1)S(1)}, bf16[128,384]{1,0:T(8,128)(2,1)S(1)}, u32[]{:S(2)}, u32[]{:S(2)}) collective-permute-start(bf16[128,384]{1,0:T(8,128)(2,1)S(1)} %reshape.52), channel_id=1, source_target_pairs={{0,16},{1,17},{2,18},{3,19},{4,20},{5,21},{6,22},{7,23},{8,24},{9,... | collective-permute-start | bytes 294920 | tf_op jit(solution)/shard_map/ppermute | solution.py:464
  7.8 8.8 %collective-permute-start = (bf16[128,384]{1,0:T(8,128)(2,1)S(1)}, bf16[128,384]{1,0:T(8,128)(2,1)S(1)}, u32[]{:S(2)}, u32[]{:S(2)}) collective-permute-start(bf16[128,384]{1,0:T(8,128)(2,1)S(1)} %reshape.52), channel_id=1, source_target_pairs={{0,8},{1,9},{2,10},{3,11},{4,12},{5,13},{6,14},{7,15},{8,16},{9,17... | collective-permute-start | bytes 294920 | tf_op jit(solution)/shard_map/ppermute | solution.py:464
  16.6 19.5 %copy-start = (bf16[4,128,384]{2,1,0:T(8,128)(2,1)}, bf16[4,128,384]{2,1,0:T(8,128)(2,1)S(1)}, u32[]{:S(2)}) copy-start(bf16[4,128,384]{2,1,0:T(8,128)(2,1)S(1)} %pad_maximum_fusion.1.refs_3_) | copy-start | bytes 1179652
  16.7 8.3 %collective-permute-start.7 = (bf16[2,128,384]{2,1,0:T(8,128)(2,1)S(1)}, bf16[2,128,384]{2,1,0:T(8,128)(2,1)S(1)}, u32[]{:S(2)}, u32[]{:S(2)}) collective-permute-start(bf16[2,128,384]{2,1,0:T(8,128)(2,1)S(1)} %get-tuple-element.126), channel_id=1, source_target_pairs={{0,4},{1,5},{2,6},{3,7},{4,0},{5,1},{6,2},{7,3},{8,12},{9,13},{10,... | collective-permute-start | bytes 589832 | tf_op jit(solution)/shard_map/ppermute | solution.py:464
  18.3 6.1 %collective-permute-start.6 = (bf16[2,128,384]{2,1,0:T(8,128)(2,1)S(1)}, bf16[2,128,384]{2,1,0:T(8,128)(2,1)S(1)}, u32[]{:S(2)}, u32[]{:S(2)}) collective-permute-start(bf16[2,128,384]{2,1,0:T(8,128)(2,1)S(1)} %get-tuple-element.127), channel_id=1, source_target_pairs={{0,2},{1,3},{2,0},{3,1},{4,6},{5,7},{6,4},{7,5},{8,10},{9,11},{10,... | collective-permute-start | bytes 589832 | tf_op jit(solution)/shard_map/ppermute | solution.py:464
  24.3 11.9 %copy-start.3 = (bf16[2,128,384]{2,1,0:T(8,128)(2,1)}, bf16[2,128,384]{2,1,0:T(8,128)(2,1)S(1)}, u32[]{:S(2)}) copy-start(bf16[2,128,384]{2,1,0:T(8,128)(2,1)S(1)} %collective-permute-done.6.refs_4_) | copy-start | bytes 589828
  24.4 11.8 %collective-permute-start.8 = (bf16[4,128,384]{2,1,0:T(8,128)(2,1)S(1)}, bf16[4,128,384]{2,1,0:T(8,128)(2,1)S(1)}, u32[]{:S(2)}, u32[]{:S(2)}) collective-permute-start(bf16[4,128,384]{2,1,0:T(8,128)(2,1)S(1)} %pad_maximum_fusion.2), channel_id=1, source_target_pairs={{0,4},{1,5},{2,6},{3,7},{4,0},{5,1},{6,2},{7,3},{8,12},{9,13},{10,... | collective-permute-start | bytes 1179656 | tf_op jit(solution)/shard_map/ppermute | solution.py:464
  25.0 16.3 %copy-start.2 = (bf16[2,128,384]{2,1,0:T(8,128)(2,1)}, bf16[2,128,384]{2,1,0:T(8,128)(2,1)S(1)}, u32[]{:S(2)}) copy-start(bf16[2,128,384]{2,1,0:T(8,128)(2,1)S(1)} %collective-permute-done.7.refs_5_) | copy-start | bytes 589828
  25.0 11.2 %collective-permute-start.9 = (bf16[4,128,384]{2,1,0:T(8,128)(2,1)S(1)}, bf16[4,128,384]{2,1,0:T(8,128)(2,1)S(1)}, u32[]{:S(2)}, u32[]{:S(2)}) collective-permute-start(bf16[4,128,384]{2,1,0:T(8,128)(2,1)S(1)} %pad_maximum_fusion.3), channel_id=1, source_target_pairs={{0,2},{1,3},{2,0},{3,1},{4,6},{5,7},{6,4},{7,5},{8,10},{9,11},{10,... | collective-permute-start | bytes 1179656 | tf_op jit(solution)/shard_map/ppermute | solution.py:464
  27.2 5.5 %collective-permute-start.5 = (bf16[112,384]{1,0:T(8,128)(2,1)S(1)}, bf16[112,384]{1,0:T(8,128)(2,1)S(1)}, u32[]{:S(2)}, u32[]{:S(2)}) collective-permute-start(bf16[112,384]{1,0:T(8,128)(2,1)S(1)} %reshape.53), channel_id=1, source_target_pairs={{0,24},{1,25},{2,26},{3,27},{4,28},{5,29},{6,30},{7,31},{8,0},{9,1... | collective-permute-start | bytes 258056 | tf_op jit(solution)/shard_map/ppermute | solution.py:464
  28.9 7.1 %collective-permute-start.4 = (bf16[112,384]{1,0:T(8,128)(2,1)S(1)}, bf16[112,384]{1,0:T(8,128)(2,1)S(1)}, u32[]{:S(2)}, u32[]{:S(2)}) collective-permute-start(bf16[112,384]{1,0:T(8,128)(2,1)S(1)} %reshape.53), channel_id=1, source_target_pairs={{0,16},{1,17},{2,18},{3,19},{4,20},{5,21},{6,22},{7,23},{8,24},{9,... | collective-permute-start | bytes 258056 | tf_op jit(solution)/shard_map/ppermute | solution.py:464
  29.4 6.6 %collective-permute-start.3 = (bf16[112,384]{1,0:T(8,128)(2,1)S(1)}, bf16[112,384]{1,0:T(8,128)(2,1)S(1)}, u32[]{:S(2)}, u32[]{:S(2)}) collective-permute-start(bf16[112,384]{1,0:T(8,128)(2,1)S(1)} %reshape.53), channel_id=1, source_target_pairs={{0,8},{1,9},{2,10},{3,11},{4,12},{5,13},{6,14},{7,15},{8,16},{9,17... | collective-permute-start | bytes 258056 | tf_op jit(solution)/shard_map/ppermute | solution.py:464
  36.1 21.2 %copy-start.5 = (bf16[4,112,384]{2,1,0:T(8,128)(2,1)}, bf16[4,112,384]{2,1,0:T(8,128)(2,1)S(1)}, u32[]{:S(2)}) copy-start(bf16[4,112,384]{2,1,0:T(8,128)(2,1)S(1)} %pad_maximum_fusion.4.refs_7_) | copy-start | bytes 1032196
  36.2 5.0 %copy-start.7 = (bf16[4,128,384]{2,1,0:T(8,128)(2,1)}, bf16[4,128,384]{2,1,0:T(8,128)(2,1)S(1)}, u32[]{:S(2)}) copy-start(bf16[4,128,384]{2,1,0:T(8,128)(2,1)S(1)} %collective-permute-done.8.refs_6_) | copy-start | bytes 1179652
  36.2 5.0 %copy-start.8 = (bf16[4,128,384]{2,1,0:T(8,128)(2,1)}, bf16[4,128,384]{2,1,0:T(8,128)(2,1)S(1)}, u32[]{:S(2)}) copy-start(bf16[4,128,384]{2,1,0:T(8,128)(2,1)S(1)} %collective-permute-done.9.refs_7_) | copy-start | bytes 1179652
  36.2 5.0 %collective-permute-start.13 = (bf16[8,128,384]{2,1,0:T(8,128)(2,1)S(1)}, bf16[8,128,384]{2,1,0:T(8,128)(2,1)S(1)}, u32[]{:S(2)}, u32[]{:S(2)}) collective-permute-start(bf16[8,128,384]{2,1,0:T(8,128)(2,1)S(1)} %pad_maximum_fusion), channel_id=1, source_target_pairs={{0,1},{1,0},{2,3},{3,2},{4,5},{5,4},{6,7},{7,6},{8,9},{9,8},{10,11... | collective-permute-start | bytes 2359304 | tf_op jit(solution)/shard_map/ppermute | solution.py:464
  36.3 2.8 %collective-permute-start.14 = (bf16[4,128,384]{2,1,0:T(8,128)(2,1)S(1)}, bf16[4,128,384]{2,1,0:T(8,128)(2,1)S(1)}, u32[]{:S(2)}, u32[]{:S(2)}) collective-permute-start(bf16[4,128,384]{2,1,0:T(8,128)(2,1)S(1)} %collective-permute-done.8.refs_6_), channel_id=1, source_target_pairs={{0,1},{1,0},{2,3},{3,2},{4,5},{5,4},{6,7},{7,6},{8,9},{9,8},{10,11... | collective-permute-start | bytes 1179656 | tf_op jit(solution)/shard_map/ppermute | solution.py:464
  36.8 3.9 %collective-permute-start.15 = (bf16[4,128,384]{2,1,0:T(8,128)(2,1)S(1)}, bf16[4,128,384]{2,1,0:T(8,128)(2,1)S(1)}, u32[]{:S(2)}, u32[]{:S(2)}) collective-permute-start(bf16[4,128,384]{2,1,0:T(8,128)(2,1)S(1)} %collective-permute-done.9.refs_7_), channel_id=1, source_target_pairs={{0,1},{1,0},{2,3},{3,2},{4,5},{5,4},{6,7},{7,6},{8,9},{9,8},{10,11... | collective-permute-start | bytes 1179656 | tf_op jit(solution)/shard_map/ppermute | solution.py:464
  36.9 22.5 %collective-permute-start.16 = (bf16[4,112,384]{2,1,0:T(8,128)(2,1)S(1)}, bf16[4,112,384]{2,1,0:T(8,128)(2,1)S(1)}, u32[]{:S(2)}, u32[]{:S(2)}) collective-permute-start(bf16[4,112,384]{2,1,0:T(8,128)(2,1)S(1)} %pad_maximum_fusion.4.refs_7_), channel_id=1, source_target_pairs={{0,1},{1,0},{2,3},{3,2},{4,5},{5,4},{6,7},{7,6},{8,9},{9,8},{10,11... | collective-permute-start | bytes 1032200 | tf_op jit(solution)/shard_map/ppermute | solution.py:464
  37.3 19.9 %collective-permute-start.12 = (bf16[4,112,384]{2,1,0:T(8,128)(2,1)S(1)}, bf16[4,112,384]{2,1,0:T(8,128)(2,1)S(1)}, u32[]{:S(2)}, u32[]{:S(2)}) collective-permute-start(bf16[4,112,384]{2,1,0:T(8,128)(2,1)S(1)} %pad_maximum_fusion.4.refs_7_), channel_id=1, source_target_pairs={{0,6},{1,7},{2,4},{3,5},{4,2},{5,3},{6,0},{7,1},{8,14},{9,15},{10,... | collective-permute-start | bytes 1032200 | tf_op jit(solution)/shard_map/ppermute | solution.py:464
  39.2 2.1 %copy-start.9 = (bf16[4,128,384]{2,1,0:T(8,128)(2,1)}, bf16[4,128,384]{2,1,0:T(8,128)(2,1)S(1)}, u32[]{:S(2)}) copy-start(bf16[4,128,384]{2,1,0:T(8,128)(2,1)S(1)} %collective-permute-done.14.refs_9_) | copy-start | bytes 1179652
  39.2 18.1 %collective-permute-start.11 = (bf16[4,112,384]{2,1,0:T(8,128)(2,1)S(1)}, bf16[4,112,384]{2,1,0:T(8,128)(2,1)}, u32[]{:S(2)}, u32[]{:S(2)}) collective-permute-start(bf16[4,112,384]{2,1,0:T(8,128)(2,1)S(1)} %pad_maximum_fusion.4.refs_7_), channel_id=1, source_target_pairs={{0,4},{1,5},{2,6},{3,7},{4,0},{5,1},{6,2},{7,3},{8,12},{9,13},{10,... | collective-permute-start | bytes 1032200 | tf_op jit(solution)/shard_map/ppermute | solution.py:464
  40.7 0.8 copy-start.10
  40.7 16.6 %collective-permute-start.10 = (bf16[4,112,384]{2,1,0:T(8,128)(2,1)S(1)}, bf16[4,112,384]{2,1,0:T(8,128)(2,1)}, u32[]{:S(2)}, u32[]{:S(2)}) collective-permute-start(bf16[4,112,384]{2,1,0:T(8,128)(2,1)S(1)} %pad_maximum_fusion.4.refs_7_), channel_id=1, source_target_pairs={{0,2},{1,3},{2,0},{3,1},{4,6},{5,7},{6,4},{7,5},{8,10},{9,11},{10,... | collective-permute-start | bytes 1032200 | tf_op jit(solution)/shard_map/ppermute | solution.py:464
  41.4 0.9 copy-start.6
  57.3 3.9 %copy-start.12 = (bf16[4,112,384]{2,1,0:T(8,128)(2,1)}, bf16[4,112,384]{2,1,0:T(8,128)(2,1)S(1)}, u32[]{:S(2)}) copy-start(bf16[4,112,384]{2,1,0:T(8,128)(2,1)S(1)} %collective-permute-done.12.refs_10_) | copy-start | bytes 1032196
  57.3 3.1 %collective-permute-start.17 = (bf16[4,112,384]{2,1,0:T(8,128)(2,1)}, bf16[4,112,384]{2,1,0:T(8,128)(2,1)S(1)}, u32[]{:S(2)}, u32[]{:S(2)}) collective-permute-start(bf16[4,112,384]{2,1,0:T(8,128)(2,1)} %collective-permute-done.10.refs_8_), channel_id=1, source_target_pairs={{0,1},{1,0},{2,3},{3,2},{4,5},{5,4},{6,7},{7,6},{8,9},{9,8},{10,11... | collective-permute-start | bytes 1032200 | tf_op jit(solution)/shard_map/ppermute | solution.py:464
  58.9 2.0 %collective-permute-start.18 = (bf16[4,112,384]{2,1,0:T(8,128)(2,1)}, bf16[4,112,384]{2,1,0:T(8,128)(2,1)S(1)}, u32[]{:S(2)}, u32[]{:S(2)}) collective-permute-start(bf16[4,112,384]{2,1,0:T(8,128)(2,1)} %collective-permute-done.11.refs_9_), channel_id=1, source_target_pairs={{0,1},{1,0},{2,3},{3,2},{4,5},{5,4},{6,7},{7,6},{8,9},{9,8},{10,11... | collective-permute-start | bytes 1032200 | tf_op jit(solution)/shard_map/ppermute | solution.py:464
  59.0 2.2 %collective-permute-start.19 = (bf16[4,112,384]{2,1,0:T(8,128)(2,1)S(1)}, bf16[4,112,384]{2,1,0:T(8,128)(2,1)S(1)}, u32[]{:S(2)}, u32[]{:S(2)}) collective-permute-start(bf16[4,112,384]{2,1,0:T(8,128)(2,1)S(1)} %collective-permute-done.12.refs_10_), channel_id=1, source_target_pairs={{0,1},{1,0},{2,3},{3,2},{4,5},{5,4},{6,7},{7,6},{8,9},{9,8},{10,11... | collective-permute-start | bytes 1032200 | tf_op jit(solution)/shard_map/ppermute | solution.py:464
  59.4 1.8 %copy-start.11 = (bf16[4,112,384]{2,1,0:T(8,128)(2,1)}, bf16[4,112,384]{2,1,0:T(8,128)(2,1)S(1)}, u32[]{:S(2)}) copy-start(bf16[4,112,384]{2,1,0:T(8,128)(2,1)S(1)} %collective-permute-done.16.refs_11_) | copy-start | bytes 1032196
  60.4 0.8 copy-start.13
  60.9 0.7 copy-start.14
  61.1 0.7 copy-start.15
  85.4 14.6 %collective-permute-start.20 = (bf16[16,112,384]{2,1,0:T(8,128)(2,1)}, bf16[16,112,384]{2,1,0:T(8,128)(2,1)S(1)}, u32[]{:S(2)}, u32[]{:S(2)}) collective-permute-start(bf16[16,112,384]{2,1,0:T(8,128)(2,1)} %get-tuple-element.86), channel_id=1, source_target_pairs={{0,1},{1,0},{2,3},{3,2},{4,5},{5,4},{6,7},{7,6},{8,9},{9,8},{10,11... | collective-permute-start | bytes 4128776 | tf_op jit(solution)/shard_map/ppermute | solution.py:464
  89.3 10.7 %copy-start.1 = (bf16[16,112,384]{2,1,0:T(8,128)(2,1)S(1)}, bf16[16,112,384]{2,1,0:T(8,128)(2,1)}, u32[]{:S(2)}) copy-start(bf16[16,112,384]{2,1,0:T(8,128)(2,1)} %get-tuple-element.91) | copy-start | bytes 4128772
  100.6 24.2 %collective-permute-start.21 = (bf16[4,112,384]{2,1,0:T(8,128)(2,1)S(1)}, bf16[4,112,384]{2,1,0:T(8,128)(2,1)S(1)}, u32[]{:S(2)}, u32[]{:S(2)}) collective-permute-start(bf16[4,112,384]{2,1,0:T(8,128)(2,1)S(1)} %get-tuple-element.99), channel_id=1, source_target_pairs={{0,2},{1,3},{2,0},{3,1},{4,6},{5,7},{6,4},{7,5},{8,10},{9,11},{10,... | collective-permute-start | bytes 1032200 | tf_op jit(solution)/shard_map/ppermute | solution.py:464
  100.6 24.2 %collective-permute-start.22 = (bf16[4,112,384]{2,1,0:T(8,128)(2,1)S(1)}, bf16[4,112,384]{2,1,0:T(8,128)(2,1)S(1)}, u32[]{:S(2)}, u32[]{:S(2)}) collective-permute-start(bf16[4,112,384]{2,1,0:T(8,128)(2,1)S(1)} %get-tuple-element.100), channel_id=1, source_target_pairs={{0,4},{1,5},{2,6},{3,7},{4,0},{5,1},{6,2},{7,3},{8,12},{9,13},{10,... | collective-permute-start | bytes 1032200 | tf_op jit(solution)/shard_map/ppermute | solution.py:464
  111.7 13.2 %collective-permute-start.23 = (bf16[4,112,384]{2,1,0:T(8,128)(2,1)S(1)}, bf16[4,112,384]{2,1,0:T(8,128)(2,1)S(1)}, u32[]{:S(2)}, u32[]{:S(2)}) collective-permute-start(bf16[4,112,384]{2,1,0:T(8,128)(2,1)S(1)} %get-tuple-element.101), channel_id=1, source_target_pairs={{0,6},{1,7},{2,4},{3,5},{4,2},{5,3},{6,0},{7,1},{8,14},{9,15},{10,... | collective-permute-start | bytes 1032200 | tf_op jit(solution)/shard_map/ppermute | solution.py:464
  124.8 5.4 %copy-start.4 = (bf16[8,128,384]{2,1,0:T(8,128)(2,1)S(1)}, bf16[8,128,384]{2,1,0:T(8,128)(2,1)}, u32[]{:S(2)}) copy-start(bf16[8,128,384]{2,1,0:T(8,128)(2,1)} %get-tuple-element.108) | copy-start | bytes 2359300
  124.8 2.5 %collective-permute-start.24 = (bf16[8,128,384]{2,1,0:T(8,128)(2,1)}, bf16[8,128,384]{2,1,0:T(8,128)(2,1)S(1)}, u32[]{:S(2)}, u32[]{:S(2)}) collective-permute-start(bf16[8,128,384]{2,1,0:T(8,128)(2,1)} %get-tuple-element.107), channel_id=1, source_target_pairs={{0,1},{1,0},{2,3},{3,2},{4,5},{5,4},{6,7},{7,6},{8,9},{9,8},{10,11... | collective-permute-start | bytes 2359304 | tf_op jit(solution)/shard_map/ppermute | solution.py:464
  124.9 5.4 %collective-permute-start.28 = (bf16[8,128,384]{2,1,0:T(8,128)(2,1)}, bf16[8,128,384]{2,1,0:T(8,128)(2,1)S(1)}, u32[]{:S(2)}, u32[]{:S(2)}) collective-permute-start(bf16[8,128,384]{2,1,0:T(8,128)(2,1)} %get-tuple-element.109), channel_id=1, source_target_pairs={{0,1},{1,0},{2,3},{3,2},{4,5},{5,4},{6,7},{7,6},{8,9},{9,8},{10,11... | collective-permute-start | bytes 2359304 | tf_op jit(solution)/shard_map/ppermute | solution.py:464
  128.7 11.2 %collective-permute-start.25 = (bf16[4,128,384]{2,1,0:T(8,128)(2,1)S(1)}, bf16[4,128,384]{2,1,0:T(8,128)(2,1)S(1)}, u32[]{:S(2)}, u32[]{:S(2)}) collective-permute-start(bf16[4,128,384]{2,1,0:T(8,128)(2,1)S(1)} %slice.166), channel_id=1, source_target_pairs={{0,2},{1,3},{2,0},{3,1},{4,6},{5,7},{6,4},{7,5},{8,10},{9,11},{10,... | collective-permute-start | bytes 1179656 | tf_op jit(solution)/shard_map/ppermute | solution.py:464
  130.5 13.0 %collective-permute-start.29 = (bf16[4,128,384]{2,1,0:T(8,128)(2,1)S(1)}, bf16[4,128,384]{2,1,0:T(8,128)(2,1)S(1)}, u32[]{:S(2)}, u32[]{:S(2)}) collective-permute-start(bf16[4,128,384]{2,1,0:T(8,128)(2,1)S(1)} %slice.165), channel_id=1, source_target_pairs={{0,4},{1,5},{2,6},{3,7},{4,0},{5,1},{6,2},{7,3},{8,12},{9,13},{10,... | collective-permute-start | bytes 1179656 | tf_op jit(solution)/shard_map/ppermute | solution.py:464
  134.4 17.3 %collective-permute-start.33 = (bf16[112,384]{1,0:T(8,128)(2,1)S(1)}, bf16[112,384]{1,0:T(8,128)(2,1)S(1)}, u32[]{:S(2)}, u32[]{:S(2)}) collective-permute-start(bf16[112,384]{1,0:T(8,128)(2,1)S(1)} %get-tuple-element.128), channel_id=1, source_target_pairs={{0,8},{1,9},{2,10},{3,11},{4,12},{5,13},{6,14},{7,15},{8,16},{9,17... | collective-permute-start | bytes 258056 | tf_op jit(solution)/shard_map/ppermute | solution.py:464
  134.5 19.2 %collective-permute-start.35 = (bf16[112,384]{1,0:T(8,128)(2,1)S(1)}, bf16[112,384]{1,0:T(8,128)(2,1)S(1)}, u32[]{:S(2)}, u32[]{:S(2)}) collective-permute-start(bf16[112,384]{1,0:T(8,128)(2,1)S(1)} %get-tuple-element.129), channel_id=1, source_target_pairs={{0,24},{1,25},{2,26},{3,27},{4,28},{5,29},{6,30},{7,31},{8,0},{9,1... | collective-permute-start | bytes 258056 | tf_op jit(solution)/shard_map/ppermute | solution.py:464
  138.3 15.4 %collective-permute-start.34 = (bf16[112,384]{1,0:T(8,128)(2,1)S(1)}, bf16[112,384]{1,0:T(8,128)(2,1)S(1)}, u32[]{:S(2)}, u32[]{:S(2)}) collective-permute-start(bf16[112,384]{1,0:T(8,128)(2,1)S(1)} %get-tuple-element.130), channel_id=1, source_target_pairs={{0,16},{1,17},{2,18},{3,19},{4,20},{5,21},{6,22},{7,23},{8,24},{9,... | collective-permute-start | bytes 258056 | tf_op jit(solution)/shard_map/ppermute | solution.py:464
  140.0 8.2 %collective-permute-start.26 = (bf16[2,128,384]{2,1,0:T(8,128)(2,1)S(1)}, bf16[2,128,384]{2,1,0:T(8,128)(2,1)S(1)}, u32[]{:S(2)}, u32[]{:S(2)}) collective-permute-start(bf16[2,128,384]{2,1,0:T(8,128)(2,1)S(1)} %fusion.4), channel_id=1, source_target_pairs={{0,4},{1,5},{2,6},{3,7},{4,0},{5,1},{6,2},{7,3},{8,12},{9,13},{10,... | collective-permute-start | bytes 589832 | tf_op jit(solution)/shard_map/ppermute | solution.py:464
  143.6 6.2 %collective-permute-start.30 = (bf16[2,128,384]{2,1,0:T(8,128)(2,1)S(1)}, bf16[2,128,384]{2,1,0:T(8,128)(2,1)S(1)}, u32[]{:S(2)}, u32[]{:S(2)}) collective-permute-start(bf16[2,128,384]{2,1,0:T(8,128)(2,1)S(1)} %fusion.3), channel_id=1, source_target_pairs={{0,2},{1,3},{2,0},{3,1},{4,6},{5,7},{6,4},{7,5},{8,10},{9,11},{10,... | collective-permute-start | bytes 589832 | tf_op jit(solution)/shard_map/ppermute | solution.py:464
  148.3 7.7 %collective-permute-start.27 = (bf16[128,384]{1,0:T(8,128)(2,1)S(1)}, bf16[128,384]{1,0:T(8,128)(2,1)S(1)}, u32[]{:S(2)}, u32[]{:S(2)}) collective-permute-start(bf16[128,384]{1,0:T(8,128)(2,1)S(1)} %fusion.11), channel_id=1, source_target_pairs={{0,8},{1,9},{2,10},{3,11},{4,12},{5,13},{6,14},{7,15},{8,16},{9,17... | collective-permute-start | bytes 294920 | tf_op jit(solution)/shard_map/ppermute | solution.py:464
  149.9 8.4 %collective-permute-start.31 = (bf16[128,384]{1,0:T(8,128)(2,1)S(1)}, bf16[128,384]{1,0:T(8,128)(2,1)S(1)}, u32[]{:S(2)}, u32[]{:S(2)}) collective-permute-start(bf16[128,384]{1,0:T(8,128)(2,1)S(1)} %get-tuple-element.131), channel_id=1, source_target_pairs={{0,16},{1,17},{2,18},{3,19},{4,20},{5,21},{6,22},{7,23},{8,24},{9,... | collective-permute-start | bytes 294920 | tf_op jit(solution)/shard_map/ppermute | solution.py:464
  151.7 6.6 %collective-permute-start.32 = (bf16[128,384]{1,0:T(8,128)(2,1)S(1)}, bf16[128,384]{1,0:T(8,128)(2,1)S(1)}, u32[]{:S(2)}, u32[]{:S(2)}) collective-permute-start(bf16[128,384]{1,0:T(8,128)(2,1)S(1)} %get-tuple-element.132), channel_id=1, source_target_pairs={{0,24},{1,25},{2,26},{3,27},{4,28},{5,29},{6,30},{7,31},{8,0},{9,1... | collective-permute-start | bytes 294920 | tf_op jit(solution)/shard_map/ppermute | solution.py:464

commit v6 on v5

--- a/solution.py
+++ b/solution.py
@@ -551,8 +551,8 @@
 
 def to_piece(share, rows, me):
     size = share.shape[0]
-    flat = jnp.zeros((rows * D,), share.dtype)
-    return lax.dynamic_update_slice(flat, share, (size * me % GROUP,)).reshape(rows, D)
+    padded = jnp.pad(share, (GROUP, rows * D - size))
+    return lax.dynamic_slice(padded, (GROUP - size * me % GROUP,), (rows * D,)).reshape(rows, D)
 
 
 def from_piece(piece, size, me):

time: 160 us -> 160 us (level)
  starting transfers between devices: 56.8 us -> 35.6 us
  Pallas kernels: 62.3 us -> 78 us
  waiting for transfers between devices: 26.8 us -> 33.7 us
  local copies, waits for them, and re-layouts: 8.2 us -> 6.37 us
    ppermute x36, starting transfers between devices: 56.8 us -> 35.6 us  [shift(): return lax.ppermute(values, AXIS, pairs)]
    pallas_call x4, Pallas kernels: 62.3 us -> 78 us  [call(): pl.pallas_call(kernel, grid_spec=pltpu.PrefetchScalarGridSpec(num_scalar_...]
    ppermute x36, waiting for transfers between devices: 26.8 us -> 33.7 us  [shift(): return lax.ppermute(values, AXIS, pairs)]
    dynamic_update_slice x2 -> x0, local copies, waits for them, and re-layouts: 3.89 us -> none  [to_piece(): lax.dynamic_update_slice(flat, share, (size * me % GROUP,)).reshape(rows, D)]
    dynamic_slice x0 -> x2, local copies, waits for them, and re-layouts: none -> 2.06 us  [to_piece(): lax.dynamic_slice(padded, (GROUP - size * me % GROUP,), (rows * D,))]
  transfers between devices with their start and end apart: 36 -> 36, of which waited for: 15 -> 15; matrix products, arithmetic and copies ran while one was open for 4% -> 3% of each run, Pallas kernels for 24% -> 28%
where the time goes in v6:
time: 160 us; the launch traced here: 159 us
  Pallas kernels  78 us (49%)
  starting transfers between devices  35.6 us (22%)
  waiting for transfers between devices  33.7 us (21%)
  local copies, waits for them, and re-layouts  6.37 us (4%)
  other arithmetic  3.39 us (2%)
  between operations  2.15 us (1%)
    pallas_call x4, Pallas kernels, call(): pl.pallas_call(kernel, grid_spec=pltpu.PrefetchScalarGridSpec(num_scalar_...  78 us
    ppermute x36, starting transfers between devices, shift(): return lax.ppermute(values, AXIS, pairs)  35.6 us
    ppermute x36, waiting for transfers between devices, shift(): return lax.ppermute(values, AXIS, pairs)  33.7 us
  transfers between devices with their start and end apart: 36, of which 15 were waited for; matrix products, arithmetic and copies ran while one was open for 3% of the time, Pallas kernels for 28%

profile of v6, /device:TPU:0, one launch (start us, length us, event | category | flops | bytes accessed | tf_op | source)
XLA Modules:
  0.0 159.2 jit_solution(12392939998143326505)
XLA Ops:
  0.7 1.0 pad_dynamic-slice_fusion
  1.8 5.1 %collective-permute-start.2 = (bf16[128,384]{1,0:T(8,128)(2,1)S(1)}, bf16[128,384]{1,0:T(8,128)(2,1)S(1)}, u32[]{:S(2)}, u32[]{:S(2)}) collective-permute-start(bf16[128,384]{1,0:T(8,128)(2,1)S(1)} %reshape.52), channel_id=1, source_target_pairs={{0,24},{1,25},{2,26},{3,27},{4,28},{5,29},{6,30},{7,31},{8,0},{9,1... | collective-permute-start | bytes 294920 | tf_op jit(solution)/shard_map/ppermute | solution.py:464
  6.9 1.0 collective-permute-start
  7.9 1.0 pad_dynamic-slice_fusion.1
  9.3 0.1 stack.338
  9.5 0.6 collective-permute-done.2
  10.1 5.5 %collective-permute-done.1 = bf16[128,384]{1,0:T(8,128)(2,1)S(1)} collective-permute-done((bf16[128,384]{1,0:T(8,128)(2,1)S(1)}, bf16[128,384]{1,0:T(8,128)(2,1)S(1)}, u32[]{:S(2)}, u32[]{:S(2)}) %collective-permute-start.1) | collective-permute-done | bytes 98336 | tf_op jit(solution)/shard_map/ppermute | solution.py:464
  15.7 1.6 collective-permute-start.7
  17.3 1.5 collective-permute-start.6
  18.8 0.2 stack.339
  19.0 4.4 %collective-permute-done.6.refs_4_ = bf16[2,128,384]{2,1,0:T(8,128)(2,1)S(1)} collective-permute-done((bf16[2,128,384]{2,1,0:T(8,128)(2,1)S(1)}, bf16[2,128,384]{2,1,0:T(8,128)(2,1)S(1)}, u32[]{:S(2)}, u32[]{:S(2)}) %collective-permute-start.6) | collective-permute-done | bytes 196640 | tf_op jit(solution)/shard_map/ppermute | solution.py:464
  23.4 0.6 collective-permute-start.8
  24.1 1.6 collective-permute-start.9
  26.3 1.6 %collective-permute-start.5 = (bf16[112,384]{1,0:T(8,128)(2,1)S(1)}, bf16[112,384]{1,0:T(8,128)(2,1)S(1)}, u32[]{:S(2)}, u32[]{:S(2)}) collective-permute-start(bf16[112,384]{1,0:T(8,128)(2,1)S(1)} %reshape.53), channel_id=1, source_target_pairs={{0,24},{1,25},{2,26},{3,27},{4,28},{5,29},{6,30},{7,31},{8,0},{9,1... | collective-permute-start | bytes 258056 | tf_op jit(solution)/shard_map/ppermute | solution.py:464
  27.9 0.5 collective-permute-start.4
  28.4 1.9 %collective-permute-start.3 = (bf16[112,384]{1,0:T(8,128)(2,1)S(1)}, bf16[112,384]{1,0:T(8,128)(2,1)S(1)}, u32[]{:S(2)}, u32[]{:S(2)}) collective-permute-start(bf16[112,384]{1,0:T(8,128)(2,1)S(1)} %reshape.53), channel_id=1, source_target_pairs={{0,8},{1,9},{2,10},{3,11},{4,12},{5,13},{6,14},{7,15},{8,16},{9,17... | collective-permute-start | bytes 258056 | tf_op jit(solution)/shard_map/ppermute | solution.py:464
  30.3 0.7 pad_add_fusion
  31.0 0.7 collective-permute-done.5
  31.7 3.3 %collective-permute-done.4 = bf16[112,384]{1,0:T(8,128)(2,1)S(1)} collective-permute-done((bf16[112,384]{1,0:T(8,128)(2,1)S(1)}, bf16[112,384]{1,0:T(8,128)(2,1)S(1)}, u32[]{:S(2)}, u32[]{:S(2)}) %collective-permute-start.4) | collective-permute-done | bytes 86048 | tf_op jit(solution)/shard_map/ppermute | solution.py:464
  35.1 0.1 pad_maximum_fusion
  35.3 0.1 collective-permute-start.13
  35.4 0.5 collective-permute-start.14
  35.9 0.1 collective-permute-start.15
  35.9 0.4 collective-permute-start.16
  36.4 1.5 collective-permute-start.12
  37.9 0.3 collective-permute-done.14.refs_9_
  38.2 1.5 collective-permute-start.11
  39.7 0.5 collective-permute-start.10
  40.3 0.2 copy-done.10
  40.5 0.9 copy-done.6
  41.4 18.2 %shard_map.101 = (f32[6,8,384]{2,1,0:T(8,128)}, bf16[6,384,384]{2,1,0:T(8,128)(2,1)}, bf16[384,1152]{1,0:T(8,128)(2,1)}, bf16[384,384]{1,0:T(8,128)(2,1)}, f32[8...) custom-call(s32[65]{0:T(128)} %get-tuple-element.66.refs_0_.scal_ref, ...), custom_call_target="tpu_custom_call" | custom-call | flops 15000000512 | bytes 20971520 | tf_op jit(solution)/shard_map/pallas_call | solution.py:572
  59.7 0.5 collective-permute-start.18
  60.2 0.1 collective-permute-start.19
  60.3 1.3 collective-permute-done.17.refs_12_
  61.6 0.3 collective-permute-done.18.refs_13_
  61.9 0.5 collective-permute-done.19.refs_14_
  62.4 0.2 copy-done.15
  62.6 0.5 copy-done.16
  63.1 32.7 %shard_map.102 = (bf16[8,256,384]{2,1,0:T(8,128)(2,1)}, f32[8,256,384]{2,1,0:T(8,128)}, bf16[8,256,384]{2,1,0:T(8,128)(2,1)}, f32[4,8,384]{2,1,0:T(8,128)}, f32[...) custom-call(s32[65]{0:T(128)} %get-tuple-element.64.refs_0_, ...), custom_call_target="tpu_custom_call" | custom-call | flops 30000001024 | bytes 20971520 | tf_op jit(solution)/shard_map/pallas_call | solution.py:572
  95.9 12.3 %shard_map.103.refs_8_ = bf16[8,256,1152]{2,1,0:T(8,128)(2,1)} custom-call(s32[65]{0:T(128)} %get-tuple-element.66.refs_0_.scal_ref, bf16[8,256,1152]{2,1,0:T(8,128)(2,1)} %get-tuple-element.88.qkv_ref, bf16[8,6,256,256]{3,2,1,0:T(8,128)(2,1)} %get-tuple-element.89.probs_ref, bf16[8,256,384]{2,1,0:T(8,128)(2,1)} %get-tuple-element.90.dmixed_ref), custom_call_target="tpu_custom_call" | custom-call | flops 12999999488 | bytes 20971520 | tf_op jit(solution)/shard_map/pallas_call | solution.py:572
  108.2 0.4 fusion.12
  108.6 0.1 fusion.14
  108.8 0.1 collective-permute-start.21
  108.9 1.0 collective-permute-start.22
  109.9 2.5 %collective-permute-start.23 = (bf16[4,112,384]{2,1,0:T(8,128)(2,1)S(1)}, bf16[4,112,384]{2,1,0:T(8,128)(2,1)S(1)}, u32[]{:S(2)}, u32[]{:S(2)}) collective-permute-start(bf16[4,112,384]{2,1,0:T(8,128)(2,1)S(1)} %get-tuple-element.101), channel_id=1, source_target_pairs={{0,6},{1,7},{2,4},{3,5},{4,2},{5,3},{6,0},{7,1},{8,14},{9,15},{10,... | collective-permute-start | bytes 1032200 | tf_op jit(solution)/shard_map/ppermute | solution.py:464
  112.3 14.7 %shard_map.104 = (f32[8,256,384]{2,1,0:T(8,128)}, f32[8,384]{1,0:T(8,128)}, bf16[8,128,384]{2,1,0:T(8,128)(2,1)}, bf16[8,128,384]{2,1,0:T(8,128)(2,1)}, bf16[8,1...) custom-call(s32[65]{0:T(128)} %get-tuple-element.66.refs_0_.scal_ref, f32[6,8,384]{2,1,0:T(8,128)} %get-tuple-element.74.refs_1_, ...), custom_call_target="tpu_custom_call" | custom-call | flops 15000000512 | bytes 20971520 | tf_op jit(solution)/shard_map/pallas_call | solution.py:572
  127.2 0.5 collective-permute-start.28
  127.7 2.0 %collective-permute-done.24 = bf16[8,128,384]{2,1,0:T(8,128)(2,1)S(1)} collective-permute-done((bf16[8,128,384]{2,1,0:T(8,128)(2,1)}, bf16[8,128,384]{2,1,0:T(8,128)(2,1)S(1)}, u32[]{:S(2)}, u32[]{:S(2)}) %collective-permute-start.24) | collective-permute-done | bytes 786464 | tf_op jit(solution)/shard_map/ppermute | solution.py:464
  129.7 1.4 convert_add_fusion.2
  131.2 0.2 convert_add_fusion.1
  131.4 1.4 collective-permute-start.29
  132.8 0.2 fusion.13
  133.1 3.8 %collective-permute-start.35 = (bf16[112,384]{1,0:T(8,128)(2,1)S(1)}, bf16[112,384]{1,0:T(8,128)(2,1)S(1)}, u32[]{:S(2)}, u32[]{:S(2)}) collective-permute-start(bf16[112,384]{1,0:T(8,128)(2,1)S(1)} %get-tuple-element.129), channel_id=1, source_target_pairs={{0,24},{1,25},{2,26},{3,27},{4,28},{5,29},{6,30},{7,31},{8,0},{9,1... | collective-permute-start | bytes 258056 | tf_op jit(solution)/shard_map/ppermute | solution.py:464
  136.9 5.4 %collective-permute-done.25 = bf16[4,128,384]{2,1,0:T(8,128)(2,1)S(1)} collective-permute-done((bf16[4,128,384]{2,1,0:T(8,128)(2,1)S(1)}, bf16[4,128,384]{2,1,0:T(8,128)(2,1)S(1)}, u32[]{:S(2)}, u32[]{:S(2)}) %collective-permute-start.25) | collective-permute-done | bytes 393248 | tf_op jit(solution)/shard_map/ppermute | solution.py:464
  142.4 1.0 collective-permute-start.26
  143.6 1.0 collective-permute-start.30
  144.6 4.1 %collective-permute-done.26 = bf16[2,128,384]{2,1,0:T(8,128)(2,1)S(1)} collective-permute-done((bf16[2,128,384]{2,1,0:T(8,128)(2,1)S(1)}, bf16[2,128,384]{2,1,0:T(8,128)(2,1)S(1)}, u32[]{:S(2)}, u32[]{:S(2)}) %collective-permute-start.26) | collective-permute-done | bytes 196640 | tf_op jit(solution)/shard_map/ppermute | solution.py:464
  148.8 0.7 collective-permute-done.30
  149.6 1.2 collective-permute-start.31
  150.8 2.2 %collective-permute-start.32 = (bf16[128,384]{1,0:T(8,128)(2,1)S(1)}, bf16[128,384]{1,0:T(8,128)(2,1)S(1)}, u32[]{:S(2)}, u32[]{:S(2)}) collective-permute-start(bf16[128,384]{1,0:T(8,128)(2,1)S(1)} %get-tuple-element.132), channel_id=1, source_target_pairs={{0,24},{1,25},{2,26},{3,27},{4,28},{5,29},{6,30},{7,31},{8,0},{9,1... | collective-permute-start | bytes 294920 | tf_op jit(solution)/shard_map/ppermute | solution.py:464
  153.1 0.8 dynamic_slice.15
  153.8 2.0 %collective-permute-done.27 = bf16[128,384]{1,0:T(8,128)(2,1)S(1)} collective-permute-done((bf16[128,384]{1,0:T(8,128)(2,1)S(1)}, bf16[128,384]{1,0:T(8,128)(2,1)S(1)}, u32[]{:S(2)}, u32[]{:S(2)}) %collective-permute-start.27) | collective-permute-done | bytes 98336 | tf_op jit(solution)/shard_map/ppermute | solution.py:464
  155.8 2.5 %collective-permute-done.31 = bf16[128,384]{1,0:T(8,128)(2,1)S(1)} collective-permute-done((bf16[128,384]{1,0:T(8,128)(2,1)S(1)}, bf16[128,384]{1,0:T(8,128)(2,1)S(1)}, u32[]{:S(2)}, u32[]{:S(2)}) %collective-permute-start.31) | collective-permute-done | bytes 98336 | tf_op jit(solution)/shard_map/ppermute | solution.py:464
  158.4 0.8 dynamic_slice.14
  (85 shorter events, 1.5 us)
Async XLA Ops:
  1.8 8.3 %collective-permute-start.2 = (bf16[128,384]{1,0:T(8,128)(2,1)S(1)}, bf16[128,384]{1,0:T(8,128)(2,1)S(1)}, u32[]{:S(2)}, u32[]{:S(2)}) collective-permute-start(bf16[128,384]{1,0:T(8,128)(2,1)S(1)} %reshape.52), channel_id=1, source_target_pairs={{0,24},{1,25},{2,26},{3,27},{4,28},{5,29},{6,30},{7,31},{8,0},{9,1... | collective-permute-start | bytes 294920 | tf_op jit(solution)/shard_map/ppermute | solution.py:464
  6.9 8.7 %collective-permute-start.1 = (bf16[128,384]{1,0:T(8,128)(2,1)S(1)}, bf16[128,384]{1,0:T(8,128)(2,1)S(1)}, u32[]{:S(2)}, u32[]{:S(2)}) collective-permute-start(bf16[128,384]{1,0:T(8,128)(2,1)S(1)} %reshape.52), channel_id=1, source_target_pairs={{0,16},{1,17},{2,18},{3,19},{4,20},{5,21},{6,22},{7,23},{8,24},{9,... | collective-permute-start | bytes 294920 | tf_op jit(solution)/shard_map/ppermute | solution.py:464
  6.9 8.7 %collective-permute-start = (bf16[128,384]{1,0:T(8,128)(2,1)S(1)}, bf16[128,384]{1,0:T(8,128)(2,1)S(1)}, u32[]{:S(2)}, u32[]{:S(2)}) collective-permute-start(bf16[128,384]{1,0:T(8,128)(2,1)S(1)} %reshape.52), channel_id=1, source_target_pairs={{0,8},{1,9},{2,10},{3,11},{4,12},{5,13},{6,14},{7,15},{8,16},{9,17... | collective-permute-start | bytes 294920 | tf_op jit(solution)/shard_map/ppermute | solution.py:464
  15.7 19.5 %copy-start = (bf16[4,128,384]{2,1,0:T(8,128)(2,1)}, bf16[4,128,384]{2,1,0:T(8,128)(2,1)S(1)}, u32[]{:S(2)}) copy-start(bf16[4,128,384]{2,1,0:T(8,128)(2,1)S(1)} %pad_maximum_fusion.1.refs_3_) | copy-start | bytes 1179652
  15.7 8.3 %collective-permute-start.7 = (bf16[2,128,384]{2,1,0:T(8,128)(2,1)S(1)}, bf16[2,128,384]{2,1,0:T(8,128)(2,1)S(1)}, u32[]{:S(2)}, u32[]{:S(2)}) collective-permute-start(bf16[2,128,384]{2,1,0:T(8,128)(2,1)S(1)} %get-tuple-element.126), channel_id=1, source_target_pairs={{0,4},{1,5},{2,6},{3,7},{4,0},{5,1},{6,2},{7,3},{8,12},{9,13},{10,... | collective-permute-start | bytes 589832 | tf_op jit(solution)/shard_map/ppermute | solution.py:464
  17.3 6.1 %collective-permute-start.6 = (bf16[2,128,384]{2,1,0:T(8,128)(2,1)S(1)}, bf16[2,128,384]{2,1,0:T(8,128)(2,1)S(1)}, u32[]{:S(2)}, u32[]{:S(2)}) collective-permute-start(bf16[2,128,384]{2,1,0:T(8,128)(2,1)S(1)} %get-tuple-element.127), channel_id=1, source_target_pairs={{0,2},{1,3},{2,0},{3,1},{4,6},{5,7},{6,4},{7,5},{8,10},{9,11},{10,... | collective-permute-start | bytes 589832 | tf_op jit(solution)/shard_map/ppermute | solution.py:464
  23.4 11.9 %copy-start.3 = (bf16[2,128,384]{2,1,0:T(8,128)(2,1)}, bf16[2,128,384]{2,1,0:T(8,128)(2,1)S(1)}, u32[]{:S(2)}) copy-start(bf16[2,128,384]{2,1,0:T(8,128)(2,1)S(1)} %collective-permute-done.6.refs_4_) | copy-start | bytes 589828
  23.4 11.8 %collective-permute-start.8 = (bf16[4,128,384]{2,1,0:T(8,128)(2,1)S(1)}, bf16[4,128,384]{2,1,0:T(8,128)(2,1)S(1)}, u32[]{:S(2)}, u32[]{:S(2)}) collective-permute-start(bf16[4,128,384]{2,1,0:T(8,128)(2,1)S(1)} %pad_maximum_fusion.2), channel_id=1, source_target_pairs={{0,4},{1,5},{2,6},{3,7},{4,0},{5,1},{6,2},{7,3},{8,12},{9,13},{10,... | collective-permute-start | bytes 1179656 | tf_op jit(solution)/shard_map/ppermute | solution.py:464
  24.0 16.3 %copy-start.2 = (bf16[2,128,384]{2,1,0:T(8,128)(2,1)}, bf16[2,128,384]{2,1,0:T(8,128)(2,1)S(1)}, u32[]{:S(2)}) copy-start(bf16[2,128,384]{2,1,0:T(8,128)(2,1)S(1)} %collective-permute-done.7.refs_5_) | copy-start | bytes 589828
  24.1 11.2 %collective-permute-start.9 = (bf16[4,128,384]{2,1,0:T(8,128)(2,1)S(1)}, bf16[4,128,384]{2,1,0:T(8,128)(2,1)S(1)}, u32[]{:S(2)}, u32[]{:S(2)}) collective-permute-start(bf16[4,128,384]{2,1,0:T(8,128)(2,1)S(1)} %pad_maximum_fusion.3), channel_id=1, source_target_pairs={{0,2},{1,3},{2,0},{3,1},{4,6},{5,7},{6,4},{7,5},{8,10},{9,11},{10,... | collective-permute-start | bytes 1179656 | tf_op jit(solution)/shard_map/ppermute | solution.py:464
  26.3 5.5 %collective-permute-start.5 = (bf16[112,384]{1,0:T(8,128)(2,1)S(1)}, bf16[112,384]{1,0:T(8,128)(2,1)S(1)}, u32[]{:S(2)}, u32[]{:S(2)}) collective-permute-start(bf16[112,384]{1,0:T(8,128)(2,1)S(1)} %reshape.53), channel_id=1, source_target_pairs={{0,24},{1,25},{2,26},{3,27},{4,28},{5,29},{6,30},{7,31},{8,0},{9,1... | collective-permute-start | bytes 258056 | tf_op jit(solution)/shard_map/ppermute | solution.py:464
  27.9 7.1 %collective-permute-start.4 = (bf16[112,384]{1,0:T(8,128)(2,1)S(1)}, bf16[112,384]{1,0:T(8,128)(2,1)S(1)}, u32[]{:S(2)}, u32[]{:S(2)}) collective-permute-start(bf16[112,384]{1,0:T(8,128)(2,1)S(1)} %reshape.53), channel_id=1, source_target_pairs={{0,16},{1,17},{2,18},{3,19},{4,20},{5,21},{6,22},{7,23},{8,24},{9,... | collective-permute-start | bytes 258056 | tf_op jit(solution)/shard_map/ppermute | solution.py:464
  28.4 6.6 %collective-permute-start.3 = (bf16[112,384]{1,0:T(8,128)(2,1)S(1)}, bf16[112,384]{1,0:T(8,128)(2,1)S(1)}, u32[]{:S(2)}, u32[]{:S(2)}) collective-permute-start(bf16[112,384]{1,0:T(8,128)(2,1)S(1)} %reshape.53), channel_id=1, source_target_pairs={{0,8},{1,9},{2,10},{3,11},{4,12},{5,13},{6,14},{7,15},{8,16},{9,17... | collective-permute-start | bytes 258056 | tf_op jit(solution)/shard_map/ppermute | solution.py:464
  35.1 24.5 %copy-start.5 = (bf16[4,112,384]{2,1,0:T(8,128)(2,1)}, bf16[4,112,384]{2,1,0:T(8,128)(2,1)S(1)}, u32[]{:S(2)}) copy-start(bf16[4,112,384]{2,1,0:T(8,128)(2,1)S(1)} %pad_maximum_fusion.4.refs_7_) | copy-start | bytes 1032196
  35.3 5.0 %copy-start.7 = (bf16[4,128,384]{2,1,0:T(8,128)(2,1)}, bf16[4,128,384]{2,1,0:T(8,128)(2,1)S(1)}, u32[]{:S(2)}) copy-start(bf16[4,128,384]{2,1,0:T(8,128)(2,1)S(1)} %collective-permute-done.8.refs_6_) | copy-start | bytes 1179652
  35.3 5.0 %copy-start.8 = (bf16[4,128,384]{2,1,0:T(8,128)(2,1)}, bf16[4,128,384]{2,1,0:T(8,128)(2,1)S(1)}, u32[]{:S(2)}) copy-start(bf16[4,128,384]{2,1,0:T(8,128)(2,1)S(1)} %collective-permute-done.9.refs_7_) | copy-start | bytes 1179652
  35.3 5.0 %collective-permute-start.13 = (bf16[8,128,384]{2,1,0:T(8,128)(2,1)S(1)}, bf16[8,128,384]{2,1,0:T(8,128)(2,1)S(1)}, u32[]{:S(2)}, u32[]{:S(2)}) collective-permute-start(bf16[8,128,384]{2,1,0:T(8,128)(2,1)S(1)} %pad_maximum_fusion), channel_id=1, source_target_pairs={{0,1},{1,0},{2,3},{3,2},{4,5},{5,4},{6,7},{7,6},{8,9},{9,8},{10,11... | collective-permute-start | bytes 2359304 | tf_op jit(solution)/shard_map/ppermute | solution.py:464
  35.4 2.8 %collective-permute-start.14 = (bf16[4,128,384]{2,1,0:T(8,128)(2,1)S(1)}, bf16[4,128,384]{2,1,0:T(8,128)(2,1)S(1)}, u32[]{:S(2)}, u32[]{:S(2)}) collective-permute-start(bf16[4,128,384]{2,1,0:T(8,128)(2,1)S(1)} %collective-permute-done.8.refs_6_), channel_id=1, source_target_pairs={{0,1},{1,0},{2,3},{3,2},{4,5},{5,4},{6,7},{7,6},{8,9},{9,8},{10,11... | collective-permute-start | bytes 1179656 | tf_op jit(solution)/shard_map/ppermute | solution.py:464
  35.9 3.9 %collective-permute-start.15 = (bf16[4,128,384]{2,1,0:T(8,128)(2,1)S(1)}, bf16[4,128,384]{2,1,0:T(8,128)(2,1)S(1)}, u32[]{:S(2)}, u32[]{:S(2)}) collective-permute-start(bf16[4,128,384]{2,1,0:T(8,128)(2,1)S(1)} %collective-permute-done.9.refs_7_), channel_id=1, source_target_pairs={{0,1},{1,0},{2,3},{3,2},{4,5},{5,4},{6,7},{7,6},{8,9},{9,8},{10,11... | collective-permute-start | bytes 1179656 | tf_op jit(solution)/shard_map/ppermute | solution.py:464
  35.9 24.4 %collective-permute-start.16 = (bf16[4,112,384]{2,1,0:T(8,128)(2,1)S(1)}, bf16[4,112,384]{2,1,0:T(8,128)(2,1)S(1)}, u32[]{:S(2)}, u32[]{:S(2)}) collective-permute-start(bf16[4,112,384]{2,1,0:T(8,128)(2,1)S(1)} %pad_maximum_fusion.4.refs_7_), channel_id=1, source_target_pairs={{0,1},{1,0},{2,3},{3,2},{4,5},{5,4},{6,7},{7,6},{8,9},{9,8},{10,11... | collective-permute-start | bytes 1032200 | tf_op jit(solution)/shard_map/ppermute | solution.py:464
  36.4 23.2 %collective-permute-start.12 = (bf16[4,112,384]{2,1,0:T(8,128)(2,1)S(1)}, bf16[4,112,384]{2,1,0:T(8,128)(2,1)S(1)}, u32[]{:S(2)}, u32[]{:S(2)}) collective-permute-start(bf16[4,112,384]{2,1,0:T(8,128)(2,1)S(1)} %pad_maximum_fusion.4.refs_7_), channel_id=1, source_target_pairs={{0,6},{1,7},{2,4},{3,5},{4,2},{5,3},{6,0},{7,1},{8,14},{9,15},{10,... | collective-permute-start | bytes 1032200 | tf_op jit(solution)/shard_map/ppermute | solution.py:464
  38.2 2.1 %copy-start.9 = (bf16[4,128,384]{2,1,0:T(8,128)(2,1)}, bf16[4,128,384]{2,1,0:T(8,128)(2,1)S(1)}, u32[]{:S(2)}) copy-start(bf16[4,128,384]{2,1,0:T(8,128)(2,1)S(1)} %collective-permute-done.14.refs_9_) | copy-start | bytes 1179652
  38.2 21.4 %collective-permute-start.11 = (bf16[4,112,384]{2,1,0:T(8,128)(2,1)S(1)}, bf16[4,112,384]{2,1,0:T(8,128)(2,1)S(1)}, u32[]{:S(2)}, u32[]{:S(2)}) collective-permute-start(bf16[4,112,384]{2,1,0:T(8,128)(2,1)S(1)} %pad_maximum_fusion.4.refs_7_), channel_id=1, source_target_pairs={{0,4},{1,5},{2,6},{3,7},{4,0},{5,1},{6,2},{7,3},{8,12},{9,13},{10,... | collective-permute-start | bytes 1032200 | tf_op jit(solution)/shard_map/ppermute | solution.py:464
  39.7 0.8 copy-start.10
  39.7 19.9 %collective-permute-start.10 = (bf16[4,112,384]{2,1,0:T(8,128)(2,1)S(1)}, bf16[4,112,384]{2,1,0:T(8,128)(2,1)}, u32[]{:S(2)}, u32[]{:S(2)}) collective-permute-start(bf16[4,112,384]{2,1,0:T(8,128)(2,1)S(1)} %pad_maximum_fusion.4.refs_7_), channel_id=1, source_target_pairs={{0,2},{1,3},{2,0},{3,1},{4,6},{5,7},{6,4},{7,5},{8,10},{9,11},{10,... | collective-permute-start | bytes 1032200 | tf_op jit(solution)/shard_map/ppermute | solution.py:464
  40.5 0.9 copy-start.6
  59.6 2.7 %copy-start.12 = (bf16[4,112,384]{2,1,0:T(8,128)(2,1)}, bf16[4,112,384]{2,1,0:T(8,128)(2,1)S(1)}, u32[]{:S(2)}) copy-start(bf16[4,112,384]{2,1,0:T(8,128)(2,1)S(1)} %collective-permute-done.12.refs_10_) | copy-start | bytes 1032196
  59.6 2.7 %copy-start.13 = (bf16[4,112,384]{2,1,0:T(8,128)(2,1)}, bf16[4,112,384]{2,1,0:T(8,128)(2,1)S(1)}, u32[]{:S(2)}) copy-start(bf16[4,112,384]{2,1,0:T(8,128)(2,1)S(1)} %collective-permute-done.11.refs_9_) | copy-start | bytes 1032196
  59.7 1.9 %collective-permute-start.17 = (bf16[4,112,384]{2,1,0:T(8,128)(2,1)}, bf16[4,112,384]{2,1,0:T(8,128)(2,1)S(1)}, u32[]{:S(2)}, u32[]{:S(2)}) collective-permute-start(bf16[4,112,384]{2,1,0:T(8,128)(2,1)} %collective-permute-done.10.refs_8_), channel_id=1, source_target_pairs={{0,1},{1,0},{2,3},{3,2},{4,5},{5,4},{6,7},{7,6},{8,9},{9,8},{10,11... | collective-permute-start | bytes 1032200 | tf_op jit(solution)/shard_map/ppermute | solution.py:464
  59.7 2.1 %collective-permute-start.18 = (bf16[4,112,384]{2,1,0:T(8,128)(2,1)S(1)}, bf16[4,112,384]{2,1,0:T(8,128)(2,1)S(1)}, u32[]{:S(2)}, u32[]{:S(2)}) collective-permute-start(bf16[4,112,384]{2,1,0:T(8,128)(2,1)S(1)} %collective-permute-done.11.refs_9_), channel_id=1, source_target_pairs={{0,1},{1,0},{2,3},{3,2},{4,5},{5,4},{6,7},{7,6},{8,9},{9,8},{10,11... | collective-permute-start | bytes 1032200 | tf_op jit(solution)/shard_map/ppermute | solution.py:464
  60.2 2.1 %collective-permute-start.19 = (bf16[4,112,384]{2,1,0:T(8,128)(2,1)S(1)}, bf16[4,112,384]{2,1,0:T(8,128)(2,1)S(1)}, u32[]{:S(2)}, u32[]{:S(2)}) collective-permute-start(bf16[4,112,384]{2,1,0:T(8,128)(2,1)S(1)} %collective-permute-done.12.refs_10_), channel_id=1, source_target_pairs={{0,1},{1,0},{2,3},{3,2},{4,5},{5,4},{6,7},{7,6},{8,9},{9,8},{10,11... | collective-permute-start | bytes 1032200 | tf_op jit(solution)/shard_map/ppermute | solution.py:464
  60.3 2.1 %copy-start.11 = (bf16[4,112,384]{2,1,0:T(8,128)(2,1)}, bf16[4,112,384]{2,1,0:T(8,128)(2,1)S(1)}, u32[]{:S(2)}) copy-start(bf16[4,112,384]{2,1,0:T(8,128)(2,1)S(1)} %collective-permute-done.16.refs_11_) | copy-start | bytes 1032196
  61.6 0.8 copy-start.14
  61.9 0.8 copy-start.15
  62.4 0.7 copy-start.16
  95.8 12.4 %collective-permute-start.20 = (bf16[16,112,384]{2,1,0:T(8,128)(2,1)}, bf16[16,112,384]{2,1,0:T(8,128)(2,1)S(1)}, u32[]{:S(2)}, u32[]{:S(2)}) collective-permute-start(bf16[16,112,384]{2,1,0:T(8,128)(2,1)} %get-tuple-element.86), channel_id=1, source_target_pairs={{0,1},{1,0},{2,3},{3,2},{4,5},{5,4},{6,7},{7,6},{8,9},{9,8},{10,11... | collective-permute-start | bytes 4128776 | tf_op jit(solution)/shard_map/ppermute | solution.py:464
  95.9 12.4 %copy-start.1 = (bf16[16,112,384]{2,1,0:T(8,128)(2,1)S(1)}, bf16[16,112,384]{2,1,0:T(8,128)(2,1)}, u32[]{:S(2)}) copy-start(bf16[16,112,384]{2,1,0:T(8,128)(2,1)} %get-tuple-element.91) | copy-start | bytes 4128772
  108.8 18.3 %collective-permute-start.21 = (bf16[4,112,384]{2,1,0:T(8,128)(2,1)S(1)}, bf16[4,112,384]{2,1,0:T(8,128)(2,1)S(1)}, u32[]{:S(2)}, u32[]{:S(2)}) collective-permute-start(bf16[4,112,384]{2,1,0:T(8,128)(2,1)S(1)} %get-tuple-element.99), channel_id=1, source_target_pairs={{0,2},{1,3},{2,0},{3,1},{4,6},{5,7},{6,4},{7,5},{8,10},{9,11},{10,... | collective-permute-start | bytes 1032200 | tf_op jit(solution)/shard_map/ppermute | solution.py:464
  108.9 18.2 %collective-permute-start.22 = (bf16[4,112,384]{2,1,0:T(8,128)(2,1)S(1)}, bf16[4,112,384]{2,1,0:T(8,128)(2,1)S(1)}, u32[]{:S(2)}, u32[]{:S(2)}) collective-permute-start(bf16[4,112,384]{2,1,0:T(8,128)(2,1)S(1)} %get-tuple-element.100), channel_id=1, source_target_pairs={{0,4},{1,5},{2,6},{3,7},{4,0},{5,1},{6,2},{7,3},{8,12},{9,13},{10,... | collective-permute-start | bytes 1032200 | tf_op jit(solution)/shard_map/ppermute | solution.py:464
  109.9 17.2 %collective-permute-start.23 = (bf16[4,112,384]{2,1,0:T(8,128)(2,1)S(1)}, bf16[4,112,384]{2,1,0:T(8,128)(2,1)S(1)}, u32[]{:S(2)}, u32[]{:S(2)}) collective-permute-start(bf16[4,112,384]{2,1,0:T(8,128)(2,1)S(1)} %get-tuple-element.101), channel_id=1, source_target_pairs={{0,6},{1,7},{2,4},{3,5},{4,2},{5,3},{6,0},{7,1},{8,14},{9,15},{10,... | collective-permute-start | bytes 1032200 | tf_op jit(solution)/shard_map/ppermute | solution.py:464
  127.1 2.6 %collective-permute-start.24 = (bf16[8,128,384]{2,1,0:T(8,128)(2,1)}, bf16[8,128,384]{2,1,0:T(8,128)(2,1)S(1)}, u32[]{:S(2)}, u32[]{:S(2)}) collective-permute-start(bf16[8,128,384]{2,1,0:T(8,128)(2,1)} %get-tuple-element.107), channel_id=1, source_target_pairs={{0,1},{1,0},{2,3},{3,2},{4,5},{5,4},{6,7},{7,6},{8,9},{9,8},{10,11... | collective-permute-start | bytes 2359304 | tf_op jit(solution)/shard_map/ppermute | solution.py:464
  127.2 4.0 %collective-permute-start.28 = (bf16[8,128,384]{2,1,0:T(8,128)(2,1)}, bf16[8,128,384]{2,1,0:T(8,128)(2,1)S(1)}, u32[]{:S(2)}, u32[]{:S(2)}) collective-permute-start(bf16[8,128,384]{2,1,0:T(8,128)(2,1)} %get-tuple-element.109), channel_id=1, source_target_pairs={{0,1},{1,0},{2,3},{3,2},{4,5},{5,4},{6,7},{7,6},{8,9},{9,8},{10,11... | collective-permute-start | bytes 2359304 | tf_op jit(solution)/shard_map/ppermute | solution.py:464
  127.7 3.5 %copy-start.4 = (bf16[8,128,384]{2,1,0:T(8,128)(2,1)S(1)}, bf16[8,128,384]{2,1,0:T(8,128)(2,1)}, u32[]{:S(2)}) copy-start(bf16[8,128,384]{2,1,0:T(8,128)(2,1)} %get-tuple-element.108) | copy-start | bytes 2359300
  131.1 11.2 %collective-permute-start.25 = (bf16[4,128,384]{2,1,0:T(8,128)(2,1)S(1)}, bf16[4,128,384]{2,1,0:T(8,128)(2,1)S(1)}, u32[]{:S(2)}, u32[]{:S(2)}) collective-permute-start(bf16[4,128,384]{2,1,0:T(8,128)(2,1)S(1)} %slice.166), channel_id=1, source_target_pairs={{0,2},{1,3},{2,0},{3,1},{4,6},{5,7},{6,4},{7,5},{8,10},{9,11},{10,... | collective-permute-start | bytes 1179656 | tf_op jit(solution)/shard_map/ppermute | solution.py:464
  131.4 12.0 %collective-permute-start.29 = (bf16[4,128,384]{2,1,0:T(8,128)(2,1)S(1)}, bf16[4,128,384]{2,1,0:T(8,128)(2,1)S(1)}, u32[]{:S(2)}, u32[]{:S(2)}) collective-permute-start(bf16[4,128,384]{2,1,0:T(8,128)(2,1)S(1)} %slice.165), channel_id=1, source_target_pairs={{0,4},{1,5},{2,6},{3,7},{4,0},{5,1},{6,2},{7,3},{8,12},{9,13},{10,... | collective-permute-start | bytes 1179656 | tf_op jit(solution)/shard_map/ppermute | solution.py:464
  133.0 17.7 %collective-permute-start.33 = (bf16[112,384]{1,0:T(8,128)(2,1)S(1)}, bf16[112,384]{1,0:T(8,128)(2,1)S(1)}, u32[]{:S(2)}, u32[]{:S(2)}) collective-permute-start(bf16[112,384]{1,0:T(8,128)(2,1)S(1)} %get-tuple-element.128), channel_id=1, source_target_pairs={{0,8},{1,9},{2,10},{3,11},{4,12},{5,13},{6,14},{7,15},{8,16},{9,17... | collective-permute-start | bytes 258056 | tf_op jit(solution)/shard_map/ppermute | solution.py:464
  133.1 19.9 %collective-permute-start.35 = (bf16[112,384]{1,0:T(8,128)(2,1)S(1)}, bf16[112,384]{1,0:T(8,128)(2,1)S(1)}, u32[]{:S(2)}, u32[]{:S(2)}) collective-permute-start(bf16[112,384]{1,0:T(8,128)(2,1)S(1)} %get-tuple-element.129), channel_id=1, source_target_pairs={{0,24},{1,25},{2,26},{3,27},{4,28},{5,29},{6,30},{7,31},{8,0},{9,1... | collective-permute-start | bytes 258056 | tf_op jit(solution)/shard_map/ppermute | solution.py:464
  136.9 16.1 %collective-permute-start.34 = (bf16[112,384]{1,0:T(8,128)(2,1)S(1)}, bf16[112,384]{1,0:T(8,128)(2,1)S(1)}, u32[]{:S(2)}, u32[]{:S(2)}) collective-permute-start(bf16[112,384]{1,0:T(8,128)(2,1)S(1)} %get-tuple-element.130), channel_id=1, source_target_pairs={{0,16},{1,17},{2,18},{3,19},{4,20},{5,21},{6,22},{7,23},{8,24},{9,... | collective-permute-start | bytes 258056 | tf_op jit(solution)/shard_map/ppermute | solution.py:464
  142.4 6.2 %collective-permute-start.26 = (bf16[2,128,384]{2,1,0:T(8,128)(2,1)S(1)}, bf16[2,128,384]{2,1,0:T(8,128)(2,1)S(1)}, u32[]{:S(2)}, u32[]{:S(2)}) collective-permute-start(bf16[2,128,384]{2,1,0:T(8,128)(2,1)S(1)} %fusion.4), channel_id=1, source_target_pairs={{0,4},{1,5},{2,6},{3,7},{4,0},{5,1},{6,2},{7,3},{8,12},{9,13},{10,... | collective-permute-start | bytes 589832 | tf_op jit(solution)/shard_map/ppermute | solution.py:464
  143.6 5.9 %collective-permute-start.30 = (bf16[2,128,384]{2,1,0:T(8,128)(2,1)S(1)}, bf16[2,128,384]{2,1,0:T(8,128)(2,1)S(1)}, u32[]{:S(2)}, u32[]{:S(2)}) collective-permute-start(bf16[2,128,384]{2,1,0:T(8,128)(2,1)S(1)} %fusion.3), channel_id=1, source_target_pairs={{0,2},{1,3},{2,0},{3,1},{4,6},{5,7},{6,4},{7,5},{8,10},{9,11},{10,... | collective-permute-start | bytes 589832 | tf_op jit(solution)/shard_map/ppermute | solution.py:464
  148.7 7.1 %collective-permute-start.27 = (bf16[128,384]{1,0:T(8,128)(2,1)S(1)}, bf16[128,384]{1,0:T(8,128)(2,1)S(1)}, u32[]{:S(2)}, u32[]{:S(2)}) collective-permute-start(bf16[128,384]{1,0:T(8,128)(2,1)S(1)} %fusion.11), channel_id=1, source_target_pairs={{0,8},{1,9},{2,10},{3,11},{4,12},{5,13},{6,14},{7,15},{8,16},{9,17... | collective-permute-start | bytes 294920 | tf_op jit(solution)/shard_map/ppermute | solution.py:464
  149.6 8.8 %collective-permute-start.31 = (bf16[128,384]{1,0:T(8,128)(2,1)S(1)}, bf16[128,384]{1,0:T(8,128)(2,1)S(1)}, u32[]{:S(2)}, u32[]{:S(2)}) collective-permute-start(bf16[128,384]{1,0:T(8,128)(2,1)S(1)} %get-tuple-element.131), channel_id=1, source_target_pairs={{0,16},{1,17},{2,18},{3,19},{4,20},{5,21},{6,22},{7,23},{8,24},{9,... | collective-permute-start | bytes 294920 | tf_op jit(solution)/shard_map/ppermute | solution.py:464
  150.8 7.6 %collective-permute-start.32 = (bf16[128,384]{1,0:T(8,128)(2,1)S(1)}, bf16[128,384]{1,0:T(8,128)(2,1)S(1)}, u32[]{:S(2)}, u32[]{:S(2)}) collective-permute-start(bf16[128,384]{1,0:T(8,128)(2,1)S(1)} %get-tuple-element.132), channel_id=1, source_target_pairs={{0,24},{1,25},{2,26},{3,27},{4,28},{5,29},{6,30},{7,31},{8,0},{9,1... | collective-permute-start | bytes 294920 | tf_op jit(solution)/shard_map/ppermute | solution.py:464
